TPU v7x, 256 devices: a whole 4x4x8 slice. The times are simulated.
256 devices in a mesh: slab: 16 (over y, x), tile: 16 (over z, core).
Axes of the slice: x: 4, y: 4, z: 8, core: 2. Of those that a mesh axis runs over, the one named last changes fastest.
Arguments:
- sensitivity: float32 [64, 256, 1024], P('slab', 'tile'), may hold values from -32 to 32, as said below
- filtered_density: float32 [64, 256, 1024], P('slab', 'tile'), may hold values from 0 to 1
- passive_blocks: int32 [32, 128, 512], P('slab', 'tile'), may hold values 0 or 1
- history_steps: float32 [4, 64, 256, 1024], P(None, 'slab', 'tile'), may hold values from -40 to 40
- history_changes: float32 [4, 64, 256, 1024], P(None, 'slab', 'tile'), may hold values from -200 to 200
Outputs:
- direction: float32 [64, 256, 1024], P('slab', 'tile')
Inputs may be any that keep to these rules, and one draw needn't show every extreme that they name: `sensitivity`: adjoint sensitivities.
All inputs are finite; a program needn't handle non-finite values. No bound on the sum of `passive_blocks` on one device may be relied on, other than what follows from the above.
Results may differ from a plain program's by a relative error of at most 0.0001.
Values sent between devices are 32-bit elements; how exact they have to be, the bound alone decides.
No kernel may reach another device: no remote copies, remote signals or barrier semaphores. Data moves between devices by JAX's collectives and lax.ppermute only.
A program may use at most 64 MiB of HBM per device.

v0:
```python
import jax
import jax.numpy as jnp
from jax import lax
from jax.sharding import PartitionSpec as P

SWEEPS = 3
MEM = 4


radius_square = 4.0
sharpness = 8.0
threshold = 0.5


def padded_2(block, sides, width):
    for axis, dim in sides:
        count = lax.axis_size(axis)
        forward = [(i, i + 1) for i in range(count - 1)]
        backward = [(target, source) for source, target in forward]
        low = lax.ppermute(
            lax.slice_in_dim(block, block.shape[dim] - width, None, axis=dim), axis, forward
        )
        high = lax.ppermute(lax.slice_in_dim(block, 0, width, axis=dim), axis, backward)
        block = jnp.concatenate([low, block, high], axis=dim)
    return block


def expand_blocks(blocks):
    depth_n, rows_n, cols_n = blocks.shape
    spread = jnp.broadcast_to(blocks[:, None, :, None, :, None], (depth_n, 2, rows_n, 2, cols_n, 2))
    return spread.reshape(2 * depth_n, 2 * rows_n, 2 * cols_n)


def per_device(sensitivity, filtered_density, passive_blocks, history_steps, history_changes):
    depth_n, rows_n, cols_n = sensitivity.shape
    denominator = jnp.tanh(sharpness * threshold) + jnp.tanh(sharpness * (1.0 - threshold))
    slope = (
        sharpness * (1.0 - jnp.tanh(sharpness * (filtered_density - threshold)) ** 2) / denominator
    )
    weighted = sensitivity * slope
    diagonal_value = 1.0 + 6.0 * radius_square
    iterate = weighted / diagonal_value
    for sweep_index in range(SWEEPS):
        padded = padded_2(iterate, (("slab", 0), ("tile", 1)), 1)
        middle = padded[1:-1, 1:-1]
        along_x = jnp.pad(middle, ((0, 0), (0, 0), (1, 1)))
        beside_all = padded[2:, 1:-1] + padded[:-2, 1:-1]
        beside_all = beside_all + padded[1:-1, 2:] + padded[1:-1, :-2]
        beside_all = beside_all + along_x[:, :, 2:] + along_x[:, :, :-2]
        iterate = (weighted + radius_square * beside_all) / diagonal_value
    passive = expand_blocks(passive_blocks).astype(jnp.float32)
    gradient = iterate * (1.0 - passive)
    flat_steps = history_steps.reshape(MEM, -1)
    flat_changes = history_changes.reshape(MEM, -1)
    flat_grad = gradient.reshape(-1)
    curv, newest_yy = lax.psum(
        (
            jnp.sum(flat_steps * flat_changes, axis=1),
            jnp.sum(flat_changes[MEM - 1] * flat_changes[MEM - 1]),
        ),
        ("slab", "tile"),
    )
    reduced = flat_grad
    alphas = [None] * MEM
    for member in reversed(range(MEM)):
        product = lax.psum(jnp.sum(flat_steps[member] * reduced), ("slab", "tile"))
        alphas[member] = product / curv[member]
        reduced = reduced - alphas[member] * flat_changes[member]
    scaled = curv[MEM - 1] / newest_yy * reduced
    for member in range(MEM):
        product = lax.psum(jnp.sum(flat_changes[member] * scaled), ("slab", "tile"))
        betas = product / curv[member]
        scaled = scaled + (alphas[member] - betas) * flat_steps[member]
    return (-scaled).reshape(depth_n, rows_n, cols_n)


def solution(mesh):
    in_specs = (
        P("slab", "tile", None),
        P("slab", "tile", None),
        P("slab", "tile", None),
        P(None, "slab", "tile", None),
        P(None, "slab", "tile", None),
    )
    out_specs = P("slab", "tile", None)
    return jax.shard_map(
        per_device, mesh=mesh, in_specs=in_specs, out_specs=out_specs, check_vma=False
    )
```

profile of v0, /device:TPU:1, one launch (start us, length us, event | category | flops | bytes accessed | tf_op | source)
XLA Modules:
  0.0 692.5 jit_solution(12508966024024961055)
XLA Ops:
  2.4 4.6 collective-permute-start.1
  7.0 1.3 collective-permute-done.1
  8.4 5.5 collective-permute-start.3
  13.9 1.9 collective-permute-start.2
  15.8 3.2 collective-permute-done.2
  20.6 4.6 collective-permute-start.5
  25.2 1.3 collective-permute-done.5
  26.5 2.8 collective-permute-start.7
  29.3 1.9 collective-permute-start.6
  31.2 3.2 collective-permute-done.6
  36.0 4.6 collective-permute-start.9
  42.0 2.8 collective-permute-start.11
  44.8 1.9 collective-permute-start.10
  46.7 1.8 multiply_reduce_fusion
  48.5 6.2 broadcast_in_dim.2
  54.7 12.7 %sub.75 = f32[4,16,1024]{2,1,0:T(8,128)S(1)} reshape(f32[2,2,8,2,512,2]{5,4,3,2,1,0:T(8,128)} %broadcast_in_dim.2) | data formatting | bytes 524288 | tf_op jit(solution)/shard_map/sub | solution.py:52
  68.3 89.4 %all-reduce.4 = (f32[]{:T(128)}, f32[4]{0:T(128)S(1)}) all-reduce(f32[]{:T(128)} %get-tuple-element.19, f32[4]{0:T(128)S(1)} %multiply_reduce_fusion), channel_id=1, replica_groups=mesh['slab'=16,'tile'=16] {'slab','tile'}, use_global_device_ids=true, to_apply=%region_5.6 | all-reduce | flops 5 | bytes 40 | tf_op jit(solution)/shard_map/psum | solution.py:66
  160.4 74.3 %psum.73 = f32[]{:T(128)} all-reduce(f32[]{:T(128)} %get-tuple-element.17), channel_id=1, replica_groups=mesh['slab'=16,'tile'=16] {'slab','tile'}, use_global_device_ids=true, to_apply=%region_7.8 | all-reduce | flops 1 | bytes 8 | tf_op jit(solution)/shard_map/psum | solution.py:66
  236.7 73.7 %psum.74 = f32[]{:T(128)} all-reduce(f32[]{:T(128)} %get-tuple-element.6), channel_id=1, replica_groups=mesh['slab'=16,'tile'=16] {'slab','tile'}, use_global_device_ids=true, to_apply=%region_9.10 | all-reduce | flops 1 | bytes 8 | tf_op jit(solution)/shard_map/psum | solution.py:66
  312.3 73.5 %all-reduce.3 = (f32[]{:T(128)}, f32[]{:T(128)}) all-reduce(f32[]{:T(128)} %get-tuple-element.5, f32[]{:T(128)} %get-tuple-element.15), channel_id=1, replica_groups=mesh['slab'=16,'tile'=16] {'slab','tile'}, use_global_device_ids=true, to_apply=%region_3.4 | all-reduce | flops 2 | bytes 16 | tf_op jit(solution)/shard_map/psum | solution.py:56
  389.2 74.2 %psum.76 = f32[]{:T(128)} all-reduce(f32[]{:T(128)} %get-tuple-element.13), channel_id=1, replica_groups=mesh['slab'=16,'tile'=16] {'slab','tile'}, use_global_device_ids=true, to_apply=%region_13.14 | all-reduce | flops 1 | bytes 8 | tf_op jit(solution)/shard_map/psum | solution.py:71
  465.4 73.4 %psum.77 = f32[]{:T(128)} all-reduce(f32[]{:T(128)} %multiply_reduce_fusion.3), channel_id=1, replica_groups=mesh['slab'=16,'tile'=16] {'slab','tile'}, use_global_device_ids=true, to_apply=%region_15.16 | all-reduce | flops 1 | bytes 8 | tf_op jit(solution)/shard_map/psum | solution.py:71
  540.7 74.0 %psum.78 = f32[]{:T(128)} all-reduce(f32[]{:T(128)} %get-tuple-element.11), channel_id=1, replica_groups=mesh['slab'=16,'tile'=16] {'slab','tile'}, use_global_device_ids=true, to_apply=%region_17.18 | all-reduce | flops 1 | bytes 8 | tf_op jit(solution)/shard_map/psum | solution.py:71
  616.7 73.5 %psum.79 = f32[]{:T(128)} all-reduce(f32[]{:T(128)} %multiply_reduce_fusion.1), channel_id=1, replica_groups=mesh['slab'=16,'tile'=16] {'slab','tile'}, use_global_device_ids=true, to_apply=%region_19.20 | all-reduce | flops 1 | bytes 8 | tf_op jit(solution)/shard_map/psum | solution.py:71
  (35 shorter events, 14.1 us)
Async XLA Ops:
  1.1 5.9 collective-permute-start
  2.4 5.9 collective-permute-start.1
  8.4 7.4 %collective-permute-start.3 = (f32[6,1,1024]{2,1,0:T(1,128)S(1)}, f32[6,1,1024]{2,1,0:T(1,128)S(1)}, u32[]{:S(2)}, u32[]{:S(2)}) collective-permute-start(f32[6,1,1024]{2,1,0:T(1,128)S(1)} %get-tuple-element.28), channel_id=1, source_target_pairs={{0,1},{1,2},{2,3},{3,4},{4,5},{5,6},{6,7},{7,8},{8,9},{9,10},{10,1... | collective-permute-start | bytes 73736 | tf_op jit(solution)/shard_map/ppermute | solution.py:20
  13.9 5.1 collective-permute-start.2
  19.3 5.9 collective-permute-start.4
  20.6 5.9 collective-permute-start.5
  26.5 4.7 collective-permute-start.7
  29.3 5.1 collective-permute-start.6
  34.7 6.7 collective-permute-start.8
  36.0 5.9 collective-permute-start.9
  42.0 25.4 %collective-permute-start.11 = (f32[6,1,1024]{2,1,0:T(1,128)S(1)}, f32[6,1,1024]{2,1,0:T(1,128)S(1)}, u32[]{:S(2)}, u32[]{:S(2)}) collective-permute-start(f32[6,1,1024]{2,1,0:T(1,128)S(1)} %get-tuple-element.24), channel_id=1, source_target_pairs={{0,1},{1,2},{2,3},{3,4},{4,5},{5,6},{6,7},{7,8},{8,9},{9,10},{10,1... | collective-permute-start | bytes 73736 | tf_op jit(solution)/shard_map/ppermute | solution.py:20
  44.8 22.7 %collective-permute-start.10 = (f32[6,1,1024]{2,1,0:T(1,128)S(1)}, f32[6,1,1024]{2,1,0:T(1,128)S(1)}, u32[]{:S(2)}, u32[]{:S(2)}) collective-permute-start(f32[6,1,1024]{2,1,0:T(1,128)S(1)} %get-tuple-element.23), channel_id=1, source_target_pairs={{1,0},{2,1},{3,2},{4,3},{5,4},{6,5},{7,6},{8,7},{9,8},{10,9},{11,1... | collective-permute-start | bytes 73736 | tf_op jit(solution)/shard_map/ppermute | solution.py:23
  48.4 19.0 %copy-start.1 = (f32[4,4,16,1024]{3,2,1,0:T(8,128)S(1)}, f32[4,4,16,1024]{3,2,1,0:T(8,128)}, u32[]{:S(2)}) copy-start(f32[4,4,16,1024]{3,2,1,0:T(8,128)} %param.8) | copy-start | bytes 3145732
  48.4 111.2 %copy-start = (f32[4,4,16,1024]{3,2,1,0:T(8,128)S(1)}, f32[4,4,16,1024]{3,2,1,0:T(8,128)}, u32[]{:S(2)}) copy-start(f32[4,4,16,1024]{3,2,1,0:T(8,128)} %param.9) | copy-start | bytes 3145732
where the time goes:
time: 695 us; the launch traced here: 692 us
  blocking collectives  606 us (87%)
  starting transfers between devices  34.5 us (5%)
  local copies, waits for them, and re-layouts  19.6 us (3%)
  between operations  12.1 us (2%)
  other arithmetic  10.7 us (2%)
  waiting for transfers between devices  9.58 us (1%)
    psum x4, blocking collectives, per_device(): product = lax.psum(jnp.sum(flat_changes[member] * scaled), ('slab', 'tile'))  295 us
    psum x3, blocking collectives, per_device(): product = lax.psum(jnp.sum(flat_steps[member] * reduced), ('slab', 'tile'))  237 us
    psum x1, blocking collectives, per_device(): lax.psum((jnp.sum(flat_steps * flat_changes, axis=1), jnp.sum(flat_change...  73.5 us
    ppermute x6, starting transfers between devices, padded_2(): lax.ppermute(lax.slice_in_dim(block, block.shape[dim] - width, None, axis...  24.8 us
  transfers between devices with their start and end apart: 12, of which 5 were waited for; matrix products, arithmetic and copies ran while one was open for 3% of the time, Pallas kernels for 0%

commit v1 on v0

v1 whole, which is shorter than its diff:
```python
import jax
import jax.numpy as jnp
from jax import lax
from jax.experimental import pallas as pl
from jax.experimental.pallas import tpu as pltpu
from jax.sharding import PartitionSpec as P

SWEEPS = 3
MEM = 4

radius_square = 4.0
sharpness = 8.0
threshold = 0.5
diagonal_value = 1.0 + 6.0 * radius_square
coupling = radius_square / diagonal_value

F32 = jnp.float32
LANES = 128
PAIRS = [(i, j) for i in range(MEM) for j in range(i, MEM)]
SY = {pair: n for n, pair in enumerate(PAIRS)}
YY = {pair: len(PAIRS) + n for n, pair in enumerate(PAIRS)}
SG = [2 * len(PAIRS) + n for n in range(MEM)]
YG = [2 * len(PAIRS) + MEM + n for n in range(MEM)]
SUMS = 32
ROWS_SENT = 24

VMEM = pl.BlockSpec(memory_space=pltpu.VMEM)


def kernel_params(mib):
    return pltpu.CompilerParams(vmem_limit_bytes=mib * 1024 * 1024)


def weight_kernel(sens_ref, dens_ref, u_ref, odd_ref, even_ref):
    slab_odd = lax.rem(lax.axis_index("slab"), 2)
    denominator = jnp.tanh(F32(sharpness * threshold)) + jnp.tanh(
        F32(sharpness * (1.0 - threshold))
    )
    for z in range(sens_ref.shape[0]):
        bend = jnp.tanh(sharpness * (dens_ref[z] - threshold))
        slope = sharpness * (1.0 - bend * bend) / denominator
        u_ref[z] = sens_ref[z] * slope / diagonal_value
    odd_ref[...] = u_ref[pl.ds(slab_odd, SWEEPS)]
    even_ref[...] = u_ref[pl.ds(1 - slab_odd, SWEEPS)]


def gram_kernel(steps_ref, changes_ref, passive_ref, sums_ref, keep_ref):
    depth, rows, cols = steps_ref.shape[1:]
    blocks = rows // 8

    def step(index, sums):
        z, block = index // blocks, lax.rem(index, blocks)
        row = pl.ds(pl.multiple_of(block * 8, 8), 8)
        sums = list(sums)
        for col in range(0, cols, LANES):
            lane = pl.ds(col, LANES)
            s = [steps_ref[i, z, row, lane] for i in range(MEM)]
            y = [changes_ref[i, z, row, lane] for i in range(MEM)]
            for i, j in PAIRS:
                sums[SY[i, j]] += s[i] * y[j]
                sums[YY[i, j]] += y[i] * y[j]
        return tuple(sums)

    zero = jnp.zeros((8, LANES), F32)
    sums = lax.fori_loop(0, depth * blocks, step, (zero,) * (2 * len(PAIRS)))
    for n, value in enumerate(sums):
        sums_ref[n : n + 1, :] = jnp.sum(value, axis=0, keepdims=True)

    def doubling(shape, dim):
        place = lax.broadcasted_iota(jnp.int32, shape, dim) // 2
        matches = place == lax.broadcasted_iota(jnp.int32, shape, 1 - dim)
        return matches.astype(F32).astype(jnp.bfloat16)

    half_rows = passive_ref.shape[1]
    twice_rows = doubling((2 * half_rows, half_rows), 0)
    twice_cols = doubling((LANES, 2 * LANES), 1)
    for z in range(passive_ref.shape[0]):
        blocks = passive_ref[z].astype(F32).astype(jnp.bfloat16)
        blocks = jnp.dot(twice_rows, blocks, preferred_element_type=F32).astype(jnp.bfloat16)
        for col in range(0, passive_ref.shape[2], LANES):
            wide = jnp.dot(
                blocks[:, col : col + LANES], twice_cols, preferred_element_type=F32
            )
            keep_ref[z, :, 2 * col : 2 * col + 2 * LANES] = 1.0 - wide


def pack_kernel(u_ref, odd_ref, even_ref, row_odd_ref, row_even_ref):
    depth, rows = u_ref.shape[:2]
    slab_odd = lax.rem(lax.axis_index("slab"), 2)
    tile_odd = lax.rem(lax.axis_index("tile"), 2)

    def pack(low_ref, high_ref, out_ref, top):
        for z in range(depth):
            start = rows - 3 if top else 0
            out_ref[3 * z : 3 * z + 3, :] = u_ref[z, start : start + 3, :]
        start = rows - 2 if top else 0
        out_ref[12:14, :] = low_ref[2, start : start + 2, :]
        out_ref[14:16, :] = high_ref[0, start : start + 2, :]
        start = rows - 1 if top else 0
        out_ref[16:17, :] = low_ref[1, start : start + 1, :]
        out_ref[17:18, :] = high_ref[1, start : start + 1, :]
        out_ref[18:24, :] = jnp.zeros((6, out_ref.shape[1]), F32)

    for parity in range(2):
        for top in range(2):

            @pl.when((slab_odd == parity) & (tile_odd == top))
            def _():
                low_ref, high_ref = (even_ref, odd_ref) if parity else (odd_ref, even_ref)
                pack(low_ref, high_ref, row_odd_ref, top == 1)
                pack(low_ref, high_ref, row_even_ref, top == 0)


def sweep_kernel(
    u_ref,
    odd_ref,
    even_ref,
    row_odd_ref,
    row_even_ref,
    keep_ref,
    steps_ref,
    changes_ref,
    sums_ref,
    grad_ref,
    send_ref,
    start_ref,
    one_ref,
    two_ref,
    total_ref,
):
    depth, rows, cols = u_ref.shape
    slab, tile = lax.axis_index("slab"), lax.axis_index("tile")
    slab_odd, tile_odd = lax.rem(slab, 2), lax.rem(tile, 2)
    inside = {
        "low_z": (slab > 0).astype(F32),
        "high_z": (slab < lax.axis_size("slab") - 1).astype(F32),
        "low_y": (tile > 0).astype(F32),
        "high_y": (tile < lax.axis_size("tile") - 1).astype(F32),
    }

    for z in range(depth):
        start_ref[3 + z, 8 : 8 + rows, :] = u_ref[z]

    def layers(low_ref, high_ref):
        for z in range(3):
            start_ref[z, 8 : 8 + rows, :] = low_ref[z] * inside["low_z"]
            start_ref[7 + z, 8 : 8 + rows, :] = high_ref[z] * inside["high_z"]

    def edge(from_ref, first, count, z, factor, high):
        to = 8 + rows if high else 8 - count
        start_ref[z, to : to + count, :] = from_ref[first : first + count, :] * factor

    def beside(from_ref, high):
        factor = inside["high_y" if high else "low_y"]
        for z in range(depth):
            edge(from_ref, 3 * z, 3, 3 + z, factor, high)
        low_factor, high_factor = factor * inside["low_z"], factor * inside["high_z"]
        edge(from_ref, 12, 2, 2, low_factor, high)
        edge(from_ref, 14, 2, 7, high_factor, high)
        edge(from_ref, 16, 1, 1, low_factor, high)
        edge(from_ref, 17, 1, 8, high_factor, high)

    for parity in range(2):

        @pl.when(slab_odd == parity)
        def _():
            layers(*((even_ref, odd_ref) if parity else (odd_ref, even_ref)))

        @pl.when(tile_odd == parity)
        def _():
            beside(row_odd_ref, parity == 1)
            beside(row_even_ref, parity == 0)

    column = lax.broadcasted_iota(jnp.int32, (8, cols), 1)
    first, last = column == 0, column == cols - 1

    def relax(from_ref, z, row):
        here = from_ref[z, row : row + 8, :]
        around = from_ref[z - 1, row : row + 8, :] + from_ref[z + 1, row : row + 8, :]
        if row == 0:
            below = pltpu.roll(here, 1, 0)
        else:
            below = from_ref[z, row - 1 : row + 7, :]
        if row == rows + 8:
            above = pltpu.roll(here, 7, 0)
        else:
            above = from_ref[z, row + 1 : row + 9, :]
        around += below + above
        around += jnp.where(first, 0.0, pltpu.roll(here, 1, 1))
        around += jnp.where(last, 0.0, pltpu.roll(here, cols - 1, 1))
        return start_ref[z, row : row + 8, :] + coupling * around

    def outside(z, row):
        factor = None
        if z < 3:
            factor = inside["low_z"]
        if z > 6:
            factor = inside["high_z"]
        edge_factor = inside["low_y"] if row < 8 else inside["high_y"] if row >= 8 + rows else None
        if factor is None or edge_factor is None:
            return edge_factor if factor is None else factor
        return factor * edge_factor

    def sweep(from_ref, to_ref, reach):
        for z in range(3 - reach, 7 + reach):
            beyond = max(3 - z, z - 6, 0)
            wide = reach - beyond > 0
            for row in range(0 if wide else 8, 8 + rows + (8 if wide else 0), 8):
                value = relax(from_ref, z, row)
                factor = outside(z, row)
                to_ref[z, row : row + 8, :] = value if factor is None else value * factor

    sweep(start_ref, one_ref, 2)
    sweep(one_ref, two_ref, 1)

    sums = [jnp.zeros((8, LANES), F32) for _ in range(2 * MEM)]
    for z in range(depth):
        for row in range(0, rows, 8):
            value = relax(two_ref, 3 + z, 8 + row) * keep_ref[z // 2, row : row + 8, :]
            grad_ref[z, row : row + 8, :] = value
            for col in range(0, cols, LANES):
                piece = value[:, col : col + LANES]
                for i in range(MEM):
                    sums[i] += steps_ref[i, z, row : row + 8, col : col + LANES] * piece
                    sums[MEM + i] += changes_ref[i, z, row : row + 8, col : col + LANES] * piece
    done = 2 * len(PAIRS)
    total_ref[0:done, :] = sums_ref[0:done, :]
    for n, value in enumerate(sums):
        total_ref[done + n : done + n + 1, :] = jnp.sum(value, axis=0, keepdims=True)
    total_ref[done + 2 * MEM :, :] = jnp.zeros((SUMS - done - 2 * MEM, LANES), F32)
    totals = jnp.sum(total_ref[...], axis=1, keepdims=True)
    diagonal = lax.broadcasted_iota(jnp.int32, (SUMS, LANES), 0) == lax.broadcasted_iota(
        jnp.int32, (SUMS, LANES), 1
    )
    line = jnp.sum(jnp.where(diagonal, totals, 0.0), axis=0, keepdims=True)
    send_ref[...] = jnp.broadcast_to(line, send_ref.shape)


def combine_kernel(all_ref, grad_ref, steps_ref, changes_ref, out_ref):
    depth, rows, cols = grad_ref.shape
    line = jnp.sum(all_ref[...], axis=0, keepdims=True)

    def entry(n):
        return jnp.broadcast_to(line[:, n : n + 1], (8, LANES))

    sy = {pair: entry(n) for pair, n in SY.items()}
    yy = {pair: entry(n) for pair, n in YY.items()}
    inverse = [1.0 / sy[i, i] for i in range(MEM)]
    alphas = [None] * MEM
    for i in reversed(range(MEM)):
        product = entry(SG[i])
        for j in range(i + 1, MEM):
            product -= alphas[j] * sy[i, j]
        alphas[i] = product * inverse[i]
    scale = sy[MEM - 1, MEM - 1] / yy[MEM - 1, MEM - 1]
    weights = [None] * MEM
    for i in range(MEM):
        product = entry(YG[i])
        for j in range(MEM):
            product -= alphas[j] * yy[min(i, j), max(i, j)]
        product *= scale
        for j in range(i):
            product += weights[j] * sy[j, i]
        weights[i] = alphas[i] - product * inverse[i]
    on_changes = [scale * alphas[i] for i in range(MEM)]
    for z in range(depth):
        for row in range(0, rows, 8):
            for col in range(0, cols, LANES):
                lane = slice(col, col + LANES)
                value = -scale * grad_ref[z, row : row + 8, lane]
                for i in range(MEM):
                    value += on_changes[i] * changes_ref[i, z, row : row + 8, lane]
                    value -= weights[i] * steps_ref[i, z, row : row + 8, lane]
                out_ref[z, row : row + 8, lane] = value


def swaps(count):
    even = [(i, i ^ 1) for i in range(count)]
    odd = [(i, (i + 1) % count if i % 2 else (i - 1) % count) for i in range(count)]
    return odd, even


def per_device(sensitivity, filtered_density, passive_blocks, history_steps, history_changes):
    shape = sensitivity.shape
    depth, rows, cols = shape
    like = jax.ShapeDtypeStruct
    layers = like((SWEEPS, rows, cols), F32)
    devices = lax.axis_size("slab") * lax.axis_size("tile")

    u, send_odd, send_even = pl.pallas_call(
        weight_kernel,
        out_shape=(like(shape, F32), layers, layers),
        in_specs=[VMEM] * 2,
        out_specs=[VMEM] * 3,
        compiler_params=kernel_params(8),
        name="weights",
    )(sensitivity, filtered_density)

    odd, even = swaps(lax.axis_size("slab"))
    got_odd = lax.ppermute(send_odd, "slab", odd)
    got_even = lax.ppermute(send_even, "slab", even)

    sums, keep = pl.pallas_call(
        gram_kernel,
        out_shape=(like((SUMS, LANES), F32), like((depth // 2, rows, cols), F32)),
        in_specs=[VMEM] * 3,
        out_specs=[VMEM] * 2,
        compiler_params=kernel_params(8),
        cost_estimate=pl.CostEstimate(flops=8_000_000, bytes_accessed=2_300_000, transcendentals=0),
        name="gram",
    )(history_steps, history_changes, passive_blocks)

    edges = like((ROWS_SENT, cols), F32)
    row_odd, row_even = pl.pallas_call(
        pack_kernel,
        out_shape=(edges, edges),
        in_specs=[VMEM] * 3,
        out_specs=[VMEM] * 2,
        compiler_params=kernel_params(8),
        name="edges",
    )(u, got_odd, got_even)
    odd, even = swaps(lax.axis_size("tile"))
    row_odd = lax.ppermute(row_odd, "tile", odd)
    row_even = lax.ppermute(row_even, "tile", even)

    padded = pltpu.VMEM((depth + 6, rows + 16, cols), F32)
    gradient, line = pl.pallas_call(
        sweep_kernel,
        out_shape=(like(shape, F32), like((devices, LANES), F32)),
        in_specs=[VMEM] * 9,
        out_specs=[VMEM] * 2,
        scratch_shapes=[padded, padded, padded, pltpu.VMEM((SUMS, LANES), F32)],
        compiler_params=kernel_params(16),
        name="sweeps",
    )(u, got_odd, got_even, row_odd, row_even, keep, history_steps, history_changes, sums)

    lines = lax.all_to_all(line, ("slab", "tile"), 0, 0, tiled=True)

    return pl.pallas_call(
        combine_kernel,
        out_shape=like(shape, F32),
        in_specs=[VMEM] * 4,
        out_specs=VMEM,
        compiler_params=kernel_params(8),
        name="combine",
    )(lines, gradient, history_steps, history_changes)


def solution(mesh):
    in_specs = (
        P("slab", "tile", None),
        P("slab", "tile", None),
        P("slab", "tile", None),
        P(None, "slab", "tile", None),
        P(None, "slab", "tile", None),
    )
    out_specs = P("slab", "tile", None)
    return jax.shard_map(
        per_device, mesh=mesh, in_specs=in_specs, out_specs=out_specs, check_vma=False
    )
```

time: 695 us -> 48.1 us (0.07)
  blocking collectives: 606 us -> 23.5 us
  starting transfers between devices: 34.5 us -> 11.9 us
  local copies, waits for them, and re-layouts: 19.6 us -> 3.59 us
  between operations: 12.1 us -> 0.04 us
  other arithmetic: 10.7 us -> 0 us
    psum x8 -> x0, blocking collectives: 606 us -> none  [the longest x4 295 us: per_device(): product = lax.psum(jnp.sum(flat_changes[member] * scaled), ('slab', 'tile'))]
    all_to_all x0 -> x1, blocking collectives: none -> 23.5 us  [per_device(): lines = lax.all_to_all(line, ('slab', 'tile'), 0, 0, tiled=True)]
    ppermute x12 -> x4, starting transfers between devices: 34.5 us -> 11.9 us  [the longest x1 5.85 us: per_device(): got_odd = lax.ppermute(send_odd, 'slab', odd)]
    sub x1 -> x0, local copies, waits for them, and re-layouts: 12.7 us -> none  [per_device(): gradient = iterate * (1.0 - passive)]
    reduce_sum x9 -> x0, other arithmetic: 7.38 us -> none  [the longest x4 2.7 us: per_device(): product = lax.psum(jnp.sum(flat_changes[member] * scaled), ('slab', 'tile'))]
  transfers between devices with their start and end apart: 12 -> 4, of which waited for: 5 -> 2; matrix products, arithmetic and copies ran while one was open for 3% -> 0% of each run, Pallas kernels for 0% -> 2%
where the time goes in v1:
time: 48.1 us; the launch traced here: 47.8 us
  blocking collectives  23.5 us (49%)
  starting transfers between devices  11.9 us (25%)
  waiting for transfers between devices  5.46 us (11%)
  local copies, waits for them, and re-layouts  3.59 us (7%)
  Pallas kernels  3.36 us (7%)
    all_to_all x1, blocking collectives, per_device(): lines = lax.all_to_all(line, ('slab', 'tile'), 0, 0, tiled=True)  23.5 us
    ppermute x1, starting transfers between devices, per_device(): got_odd = lax.ppermute(send_odd, 'slab', odd)  5.85 us
    unnamed x12, local copies, waits for them, and re-layouts  3.59 us
    ppermute x1, waiting for transfers between devices, per_device(): got_odd = lax.ppermute(send_odd, 'slab', odd)  3.57 us
    ppermute x1, starting transfers between devices, per_device(): row_odd = lax.ppermute(row_odd, 'tile', odd)  3.48 us
    ppermute x1, starting transfers between devices, per_device(): row_even = lax.ppermute(row_even, 'tile', even)  2.58 us
    ppermute x1, waiting for transfers between devices, per_device(): got_even = lax.ppermute(send_even, 'slab', even)  1.88 us
    pallas_call x1, Pallas kernels, per_device(): pl.pallas_call(sweep_kernel, out_shape=(like(shape, F32), like((devices,...  1.37 us
  transfers between devices with their start and end apart: 4, of which 2 were waited for; matrix products, arithmetic and copies ran while one was open for 0% of the time, Pallas kernels for 2%

profile of v1, /device:TPU:1, one launch (start us, length us, event | category | flops | bytes accessed | tf_op | source)
XLA Modules:
  0.0 47.8 jit_solution(14735807035061888505)
XLA Ops:
  0.0 0.0 copy-start
  0.0 0.0 copy-start.3
  0.0 1.0 %copy-done.3 = f32[4,16,1024]{2,1,0:T(8,128)S(1)} copy-done((f32[4,16,1024]{2,1,0:T(8,128)S(1)}, f32[4,16,1024]{2,1,0:T(8,128)}, u32[]{:S(2)}) %copy-start.3) | copy-done | bytes 262168
  1.0 0.0 copy-start.4
  1.0 0.9 %copy-done.4 = f32[4,16,1024]{2,1,0:T(8,128)S(1)} copy-done((f32[4,16,1024]{2,1,0:T(8,128)S(1)}, f32[4,16,1024]{2,1,0:T(8,128)}, u32[]{:S(2)}) %copy-start.4) | copy-done | bytes 262168
  2.0 0.1 weights.1
  2.1 5.8 %collective-permute-start = (f32[3,16,1024]{2,1,0:T(8,128)S(1)}, f32[3,16,1024]{2,1,0:T(8,128)S(1)}, u32[]{:S(2)}, u32[]{:S(2)}) collective-permute-start(f32[3,16,1024]{2,1,0:T(8,128)S(1)} %get-tuple-element.15), channel_id=1, source_target_pairs={{0,240},{16,32},{32,16},{48,64},{64,48},{80,96},{96,80},{112,128},... | collective-permute-start | bytes 589832 | tf_op jit(solution)/shard_map/ppermute | solution.py:300
  7.9 0.0 collective-permute-start.1
  7.9 3.6 %collective-permute-done.odd_ref = f32[3,16,1024]{2,1,0:T(8,128)S(1)} collective-permute-done((f32[3,16,1024]{2,1,0:T(8,128)S(1)}, f32[3,16,1024]{2,1,0:T(8,128)S(1)}, u32[]{:S(2)}, u32[]{:S(2)}) %collective-permute-start) | collective-permute-done | bytes 196640 | tf_op jit(solution)/shard_map/ppermute | solution.py:300
  11.5 1.9 %collective-permute-done.1.even_ref = f32[3,16,1024]{2,1,0:T(8,128)S(1)} collective-permute-done((f32[3,16,1024]{2,1,0:T(8,128)S(1)}, f32[3,16,1024]{2,1,0:T(8,128)S(1)}, u32[]{:S(2)}, u32[]{:S(2)}) %collective-permute-start.1) | collective-permute-done | bytes 196640 | tf_op jit(solution)/shard_map/ppermute | solution.py:301
  13.4 0.0 copy-start.5
  13.4 0.1 edges.1
  13.5 3.5 %collective-permute-start.2 = (f32[24,1024]{1,0:T(8,128)S(1)}, f32[24,1024]{1,0:T(8,128)S(1)}, u32[]{:S(2)}, u32[]{:S(2)}) collective-permute-start(f32[24,1024]{1,0:T(8,128)S(1)} %get-tuple-element.17), channel_id=1, source_target_pairs={{0,15},{1,2},{2,1},{3,4},{4,3},{5,6},{6,5},{7,8},{8,7},{9,10},{10,... | collective-permute-start | bytes 294920 | tf_op jit(solution)/shard_map/ppermute | solution.py:323
  16.9 2.6 %collective-permute-start.3 = (f32[24,1024]{1,0:T(8,128)S(1)}, f32[24,1024]{1,0:T(8,128)S(1)}, u32[]{:S(2)}, u32[]{:S(2)}) collective-permute-start(f32[24,1024]{1,0:T(8,128)S(1)} %get-tuple-element.18), channel_id=1, source_target_pairs={{0,1},{1,0},{2,3},{3,2},{4,5},{5,4},{6,7},{7,6},{8,9},{9,8},{10,11... | collective-permute-start | bytes 294920 | tf_op jit(solution)/shard_map/ppermute | solution.py:324
  19.5 0.0 copy-done
  19.5 0.0 copy-done.5
  19.5 1.2 %copy-done.1 = f32[4,4,16,1024]{3,2,1,0:T(8,128)S(1)} copy-done((f32[4,4,16,1024]{3,2,1,0:T(8,128)S(1)}, f32[4,4,16,1024]{3,2,1,0:T(8,128)}, u32[]{:S(2)}) %copy-start.1) | copy-done | bytes 1048600
  20.8 0.8 %gram.1 = (f32[32,128]{1,0:T(8,128)S(1)}, f32[2,16,1024]{2,1,0:T(8,128)S(1)}) custom-call(f32[4,4,16,1024]{3,2,1,0:T(8,128)S(1)} %copy-done, f32[4,4,16,1024]{3,2,1,0:T(8,128)S(1)} %copy-done.1, s32[2,8,512]{2,1,0:T(8,128)S(1)} %copy-done.5), custom_call_target="tpu_custom_call" | custom-call | flops 8000000 | bytes 2300000 | tf_op jit(solution)/shard_map/gram/pallas_call | solution.py:303
  21.6 0.0 collective-permute-done.2.row_odd_ref
  21.6 0.0 collective-permute-done.3.row_even_ref
  21.6 0.4 copy-done.2
  22.0 1.4 %sweeps.1 = (f32[4,16,1024]{2,1,0:T(8,128)S(1)}, f32[256,128]{1,0:T(8,128)S(1)}) custom-call(f32[4,16,1024]{2,1,0:T(8,128)S(1)} %get-tuple-element.14.u_ref, f32[3,16,1024]{2,1,0:T(8,128)S(1)} %collective-permute-done.odd_ref, f32[3,16,1024]{2,1,0:T(8,128)S(1)} %collective-permute-done.1.even_ref, f32[24,1024]{1,0:T(8,128)S(1)} %collective-permute-done.2.row_odd_ref, ...), custom_call_target="tpu_custom_call" | custom-call | tf_op jit(solution)/shard_map/sweeps/pallas_call | solution.py:327
  23.4 23.5 %all_to_all.11 = f32[256,1,128]{2,1,0:T(1,128)S(1)} all-to-all(f32[256,1,128]{2,1,0:T(1,128)S(1)} %bitcast.5), channel_id=1, replica_groups=mesh['slab'=16,'tile'=16] {'slab','tile'}, dimensions={0} | all-to-all | bytes 262144 | tf_op jit(solution)/shard_map/all_to_all | solution.py:337
  46.8 1.0 %combine.1 = f32[4,16,1024]{2,1,0:T(8,128)} custom-call(f32[256,128]{1,0:T(8,128)S(1)} %bitcast.4, f32[4,16,1024]{2,1,0:T(8,128)S(1)} %get-tuple-element.22.grad_ref, f32[4,4,16,1024]{3,2,1,0:T(8,128)S(1)} %copy-done, f32[4,4,16,1024]{3,2,1,0:T(8,128)S(1)} %copy-done.2), custom_call_target="tpu_custom_call" | custom-call | tf_op jit(solution)/shard_map/combine/pallas_call | solution.py:339
  (2 shorter events, 0.0 us)
Async XLA Ops:
  0.0 19.5 %copy-start = (f32[4,4,16,1024]{3,2,1,0:T(8,128)S(1)}, f32[4,4,16,1024]{3,2,1,0:T(8,128)}, u32[]{:S(2)}) copy-start(f32[4,4,16,1024]{3,2,1,0:T(8,128)} %steps_ref.5) | copy-start | bytes 3145732
  0.0 1.0 %copy-start.3 = (f32[4,16,1024]{2,1,0:T(8,128)S(1)}, f32[4,16,1024]{2,1,0:T(8,128)}, u32[]{:S(2)}) copy-start(f32[4,16,1024]{2,1,0:T(8,128)} %sens_ref.1) | copy-start | bytes 786436
  1.0 0.9 %copy-start.4 = (f32[4,16,1024]{2,1,0:T(8,128)S(1)}, f32[4,16,1024]{2,1,0:T(8,128)}, u32[]{:S(2)}) copy-start(f32[4,16,1024]{2,1,0:T(8,128)} %dens_ref.1) | copy-start | bytes 786436
  2.1 9.4 %collective-permute-start = (f32[3,16,1024]{2,1,0:T(8,128)S(1)}, f32[3,16,1024]{2,1,0:T(8,128)S(1)}, u32[]{:S(2)}, u32[]{:S(2)}) collective-permute-start(f32[3,16,1024]{2,1,0:T(8,128)S(1)} %get-tuple-element.15), channel_id=1, source_target_pairs={{0,240},{16,32},{32,16},{48,64},{64,48},{80,96},{96,80},{112,128},... | collective-permute-start | bytes 589832 | tf_op jit(solution)/shard_map/ppermute | solution.py:300
  7.9 5.5 %collective-permute-start.1 = (f32[3,16,1024]{2,1,0:T(8,128)S(1)}, f32[3,16,1024]{2,1,0:T(8,128)S(1)}, u32[]{:S(2)}, u32[]{:S(2)}) collective-permute-start(f32[3,16,1024]{2,1,0:T(8,128)S(1)} %get-tuple-element.16), channel_id=1, source_target_pairs={{0,16},{16,0},{32,48},{48,32},{64,80},{80,64},{96,112},{112,96},{1... | collective-permute-start | bytes 589832 | tf_op jit(solution)/shard_map/ppermute | solution.py:301
  13.4 6.1 %copy-start.5 = (s32[2,8,512]{2,1,0:T(8,128)S(1)}, s32[2,8,512]{2,1,0:T(8,128)}, u32[]{:S(2)}) copy-start(s32[2,8,512]{2,1,0:T(8,128)} %passive_ref.1) | copy-start | bytes 98308
  13.5 8.1 %collective-permute-start.2 = (f32[24,1024]{1,0:T(8,128)S(1)}, f32[24,1024]{1,0:T(8,128)S(1)}, u32[]{:S(2)}, u32[]{:S(2)}) collective-permute-start(f32[24,1024]{1,0:T(8,128)S(1)} %get-tuple-element.17), channel_id=1, source_target_pairs={{0,15},{1,2},{2,1},{3,4},{4,3},{5,6},{6,5},{7,8},{8,7},{9,10},{10,... | collective-permute-start | bytes 294920 | tf_op jit(solution)/shard_map/ppermute | solution.py:323
  16.9 4.7 %collective-permute-start.3 = (f32[24,1024]{1,0:T(8,128)S(1)}, f32[24,1024]{1,0:T(8,128)S(1)}, u32[]{:S(2)}, u32[]{:S(2)}) collective-permute-start(f32[24,1024]{1,0:T(8,128)S(1)} %get-tuple-element.18), channel_id=1, source_target_pairs={{0,1},{1,0},{2,3},{3,2},{4,5},{5,4},{6,7},{7,6},{8,9},{9,8},{10,11... | collective-permute-start | bytes 294920 | tf_op jit(solution)/shard_map/ppermute | solution.py:324
  19.5 1.2 %copy-start.1 = (f32[4,4,16,1024]{3,2,1,0:T(8,128)S(1)}, f32[4,4,16,1024]{3,2,1,0:T(8,128)}, u32[]{:S(2)}) copy-start(f32[4,4,16,1024]{3,2,1,0:T(8,128)} %changes_ref.5) | copy-start | bytes 3145732
  20.8 1.2 %copy-start.2 = (f32[4,4,16,1024]{3,2,1,0:T(8,128)S(1)}, f32[4,4,16,1024]{3,2,1,0:T(8,128)}, u32[]{:S(2)}) copy-start(f32[4,4,16,1024]{3,2,1,0:T(8,128)} %changes_ref.5) | copy-start | bytes 3145732

commit v2 on v1

--- a/solution.py
+++ b/solution.py
@@ -22,55 +22,101 @@
 SG = [2 * len(PAIRS) + n for n in range(MEM)]
 YG = [2 * len(PAIRS) + MEM + n for n in range(MEM)]
 SUMS = 32
-ROWS_SENT = 24
+ROWS_SENT = 16
 
 VMEM = pl.BlockSpec(memory_space=pltpu.VMEM)
+HBM = pl.BlockSpec(memory_space=pltpu.HBM)
 
 
 def kernel_params(mib):
     return pltpu.CompilerParams(vmem_limit_bytes=mib * 1024 * 1024)
 
 
-def weight_kernel(sens_ref, dens_ref, u_ref, odd_ref, even_ref):
+def weight_kernel(
+    sens_hbm,
+    dens_hbm,
+    u_ref,
+    row_odd_ref,
+    row_even_ref,
+    odd_ref,
+    even_ref,
+    sens_ref,
+    dens_ref,
+    arrived,
+):
+    depth, rows, cols = u_ref.shape
     slab_odd = lax.rem(lax.axis_index("slab"), 2)
+    tile_odd = lax.rem(lax.axis_index("tile"), 2)
+    copies = [
+        [
+            pltpu.make_async_copy(from_ref.at[z], to_ref.at[z], arrived.at[n, z])
+            for n, (from_ref, to_ref) in enumerate(((sens_hbm, sens_ref), (dens_hbm, dens_ref)))
+        ]
+        for z in range(depth)
+    ]
+    for pair in copies:
+        for copy in pair:
+            copy.start()
     denominator = jnp.tanh(F32(sharpness * threshold)) + jnp.tanh(
         F32(sharpness * (1.0 - threshold))
     )
-    for z in range(sens_ref.shape[0]):
+    for z in range(depth):
+        for copy in copies[z]:
+            copy.wait()
         bend = jnp.tanh(sharpness * (dens_ref[z] - threshold))
         slope = sharpness * (1.0 - bend * bend) / denominator
         u_ref[z] = sens_ref[z] * slope / diagonal_value
+
     odd_ref[...] = u_ref[pl.ds(slab_odd, SWEEPS)]
     even_ref[...] = u_ref[pl.ds(1 - slab_odd, SWEEPS)]
 
-
-def gram_kernel(steps_ref, changes_ref, passive_ref, sums_ref, keep_ref):
+    def edge_rows(to_ref, start):
+        for z in range(depth):
+            to_ref[3 * z : 3 * z + 3, :] = u_ref[z, start : start + 3, :]
+        to_ref[3 * depth :, :] = jnp.zeros((to_ref.shape[0] - 3 * depth, cols), F32)
+
+    for parity in range(2):
+
+        @pl.when(tile_odd == parity)
+        def _():
+            edge_rows(row_odd_ref, rows - 3 if parity else 0)
+            edge_rows(row_even_ref, 0 if parity else rows - 3)
+
+
+def gram_kernel(
+    steps_hbm,
+    changes_hbm,
+    passive_hbm,
+    sums_ref,
+    keep_ref,
+    steps_ref,
+    changes_ref,
+    passive_ref,
+    arrived,
+    passive_arrived,
+):
     depth, rows, cols = steps_ref.shape[1:]
-    blocks = rows // 8
-
-    def step(index, sums):
-        z, block = index // blocks, lax.rem(index, blocks)
-        row = pl.ds(pl.multiple_of(block * 8, 8), 8)
-        sums = list(sums)
-        for col in range(0, cols, LANES):
-            lane = pl.ds(col, LANES)
-            s = [steps_ref[i, z, row, lane] for i in range(MEM)]
-            y = [changes_ref[i, z, row, lane] for i in range(MEM)]
-            for i, j in PAIRS:
-                sums[SY[i, j]] += s[i] * y[j]
-                sums[YY[i, j]] += y[i] * y[j]
-        return tuple(sums)
-
-    zero = jnp.zeros((8, LANES), F32)
-    sums = lax.fori_loop(0, depth * blocks, step, (zero,) * (2 * len(PAIRS)))
-    for n, value in enumerate(sums):
-        sums_ref[n : n + 1, :] = jnp.sum(value, axis=0, keepdims=True)
+    passive_copy = pltpu.make_async_copy(passive_hbm, passive_ref, passive_arrived)
+    copies = [
+        [
+            pltpu.make_async_copy(from_ref.at[:, z], to_ref.at[:, z], arrived.at[n, z])
+            for n, (from_ref, to_ref) in enumerate(
+                ((steps_hbm, steps_ref), (changes_hbm, changes_ref))
+            )
+        ]
+        for z in range(depth)
+    ]
+    passive_copy.start()
+    for pair in copies:
+        for copy in pair:
+            copy.start()
 
     def doubling(shape, dim):
         place = lax.broadcasted_iota(jnp.int32, shape, dim) // 2
         matches = place == lax.broadcasted_iota(jnp.int32, shape, 1 - dim)
         return matches.astype(F32).astype(jnp.bfloat16)
 
+    passive_copy.wait()
     half_rows = passive_ref.shape[1]
     twice_rows = doubling((2 * half_rows, half_rows), 0)
     twice_cols = doubling((LANES, 2 * LANES), 1)
@@ -83,32 +129,50 @@
             )
             keep_ref[z, :, 2 * col : 2 * col + 2 * LANES] = 1.0 - wide
 
-
-def pack_kernel(u_ref, odd_ref, even_ref, row_odd_ref, row_even_ref):
-    depth, rows = u_ref.shape[:2]
+    sums = (jnp.zeros((8, LANES), F32),) * (2 * len(PAIRS))
+    for z in range(depth):
+        for copy in copies[z]:
+            copy.wait()
+
+        def step(block, sums):
+            row = pl.ds(pl.multiple_of(block * 8, 8), 8)
+            sums = list(sums)
+            for col in range(0, cols, LANES):
+                lane = pl.ds(col, LANES)
+                s = [steps_ref[i, z, row, lane] for i in range(MEM)]
+                y = [changes_ref[i, z, row, lane] for i in range(MEM)]
+                for i, j in PAIRS:
+                    sums[SY[i, j]] += s[i] * y[j]
+                    sums[YY[i, j]] += y[i] * y[j]
+            return tuple(sums)
+
+        sums = lax.fori_loop(0, rows // 8, step, sums)
+    for n, value in enumerate(sums):
+        sums_ref[n : n + 1, :] = jnp.sum(value, axis=0, keepdims=True)
+
+
+def corner_kernel(row_odd_ref, row_even_ref, rim_odd_ref, rim_even_ref):
+    cols = rim_odd_ref.shape[1]
+    depth = 4
     slab_odd = lax.rem(lax.axis_index("slab"), 2)
     tile_odd = lax.rem(lax.axis_index("tile"), 2)
 
     def pack(low_ref, high_ref, out_ref, top):
-        for z in range(depth):
-            start = rows - 3 if top else 0
-            out_ref[3 * z : 3 * z + 3, :] = u_ref[z, start : start + 3, :]
-        start = rows - 2 if top else 0
-        out_ref[12:14, :] = low_ref[2, start : start + 2, :]
-        out_ref[14:16, :] = high_ref[0, start : start + 2, :]
-        start = rows - 1 if top else 0
-        out_ref[16:17, :] = low_ref[1, start : start + 1, :]
-        out_ref[17:18, :] = high_ref[1, start : start + 1, :]
-        out_ref[18:24, :] = jnp.zeros((6, out_ref.shape[1]), F32)
+        near, second = (3 * (depth - 1), 3 * (depth - 2)) if top else (0, 3)
+        out_ref[0:2, :] = low_ref[near + 1 : near + 3, :]
+        out_ref[2:4, :] = high_ref[near : near + 2, :]
+        out_ref[4:5, :] = low_ref[second + 2 : second + 3, :]
+        out_ref[5:6, :] = high_ref[second : second + 1, :]
+        out_ref[6:8, :] = jnp.zeros((2, cols), F32)
 
     for parity in range(2):
         for top in range(2):
 
-            @pl.when((slab_odd == parity) & (tile_odd == top))
+            @pl.when((tile_odd == parity) & (slab_odd == top))
             def _():
-                low_ref, high_ref = (even_ref, odd_ref) if parity else (odd_ref, even_ref)
-                pack(low_ref, high_ref, row_odd_ref, top == 1)
-                pack(low_ref, high_ref, row_even_ref, top == 0)
+                beside = (row_even_ref, row_odd_ref) if parity else (row_odd_ref, row_even_ref)
+                pack(*beside, rim_odd_ref, top == 1)
+                pack(*beside, rim_even_ref, top == 0)
 
 
 def sweep_kernel(
@@ -117,6 +181,8 @@
     even_ref,
     row_odd_ref,
     row_even_ref,
+    rim_odd_ref,
+    rim_even_ref,
     keep_ref,
     steps_ref,
     changes_ref,
@@ -141,30 +207,31 @@
     for z in range(depth):
         start_ref[3 + z, 8 : 8 + rows, :] = u_ref[z]
 
-    def layers(low_ref, high_ref):
-        for z in range(3):
-            start_ref[z, 8 : 8 + rows, :] = low_ref[z] * inside["low_z"]
-            start_ref[7 + z, 8 : 8 + rows, :] = high_ref[z] * inside["high_z"]
-
     def edge(from_ref, first, count, z, factor, high):
         to = 8 + rows if high else 8 - count
         start_ref[z, to : to + count, :] = from_ref[first : first + count, :] * factor
 
+    def below_and_above(from_ref, rim_ref, high):
+        factor = inside["high_z" if high else "low_z"]
+        for z in range(3):
+            start_ref[7 * high + z, 8 : 8 + rows, :] = from_ref[z] * factor
+        near, second = (7, 8) if high else (2, 1)
+        low_factor, high_factor = factor * inside["low_y"], factor * inside["high_y"]
+        edge(rim_ref, 0, 2, near, low_factor, False)
+        edge(rim_ref, 2, 2, near, high_factor, True)
+        edge(rim_ref, 4, 1, second, low_factor, False)
+        edge(rim_ref, 5, 1, second, high_factor, True)
+
     def beside(from_ref, high):
-        factor = inside["high_y" if high else "low_y"]
         for z in range(depth):
-            edge(from_ref, 3 * z, 3, 3 + z, factor, high)
-        low_factor, high_factor = factor * inside["low_z"], factor * inside["high_z"]
-        edge(from_ref, 12, 2, 2, low_factor, high)
-        edge(from_ref, 14, 2, 7, high_factor, high)
-        edge(from_ref, 16, 1, 1, low_factor, high)
-        edge(from_ref, 17, 1, 8, high_factor, high)
+            edge(from_ref, 3 * z, 3, 3 + z, inside["high_y" if high else "low_y"], high)
 
     for parity in range(2):
 
         @pl.when(slab_odd == parity)
         def _():
-            layers(*((even_ref, odd_ref) if parity else (odd_ref, even_ref)))
+            below_and_above(odd_ref, rim_odd_ref, parity == 1)
+            below_and_above(even_ref, rim_even_ref, parity == 0)
 
         @pl.when(tile_odd == parity)
         def _():
@@ -236,7 +303,7 @@
     send_ref[...] = jnp.broadcast_to(line, send_ref.shape)
 
 
-def combine_kernel(all_ref, grad_ref, steps_ref, changes_ref, out_ref):
+def combine_kernel(all_ref, grad_ref, steps_ref, changes_ref, out_hbm, out_ref, left):
     depth, rows, cols = grad_ref.shape
     line = jnp.sum(all_ref[...], axis=0, keepdims=True)
 
@@ -263,6 +330,9 @@
             product += weights[j] * sy[j, i]
         weights[i] = alphas[i] - product * inverse[i]
     on_changes = [scale * alphas[i] for i in range(MEM)]
+    copies = [
+        pltpu.make_async_copy(out_ref.at[z], out_hbm.at[z], left.at[z]) for z in range(depth)
+    ]
     for z in range(depth):
         for row in range(0, rows, 8):
             for col in range(0, cols, LANES):
@@ -272,6 +342,13 @@
                     value += on_changes[i] * changes_ref[i, z, row : row + 8, lane]
                     value -= weights[i] * steps_ref[i, z, row : row + 8, lane]
                 out_ref[z, row : row + 8, lane] = value
+        copies[z].start()
+    for copy in copies:
+        copy.wait()
+
+
+def in_hbm(array):
+    return pltpu.with_memory_space_constraint(array, pltpu.HBM)
 
 
 def swaps(count):
@@ -284,55 +361,74 @@
     shape = sensitivity.shape
     depth, rows, cols = shape
     like = jax.ShapeDtypeStruct
-    layers = like((SWEEPS, rows, cols), F32)
+    layers, rim, edges = (
+        like(size, F32) for size in ((SWEEPS, rows, cols), (8, cols), (ROWS_SENT, cols))
+    )
     devices = lax.axis_size("slab") * lax.axis_size("tile")
 
-    u, send_odd, send_even = pl.pallas_call(
+    u, row_odd, row_even, odd, even = pl.pallas_call(
         weight_kernel,
-        out_shape=(like(shape, F32), layers, layers),
-        in_specs=[VMEM] * 2,
-        out_specs=[VMEM] * 3,
+        out_shape=(like(shape, F32), edges, edges, layers, layers),
+        in_specs=[HBM] * 2,
+        out_specs=[VMEM] * 5,
+        scratch_shapes=[
+            pltpu.VMEM(shape, F32),
+            pltpu.VMEM(shape, F32),
+            pltpu.SemaphoreType.DMA((2, depth)),
+        ],
         compiler_params=kernel_params(8),
         name="weights",
-    )(sensitivity, filtered_density)
-
-    odd, even = swaps(lax.axis_size("slab"))
-    got_odd = lax.ppermute(send_odd, "slab", odd)
-    got_even = lax.ppermute(send_even, "slab", even)
-
-    sums, keep = pl.pallas_call(
-        gram_kernel,
-        out_shape=(like((SUMS, LANES), F32), like((depth // 2, rows, cols), F32)),
-        in_specs=[VMEM] * 3,
+    )(in_hbm(sensitivity), in_hbm(filtered_density))
+
+    slab_odd, slab_even = swaps(lax.axis_size("slab"))
+    tile_odd, tile_even = swaps(lax.axis_size("tile"))
+    odd = lax.ppermute(odd, "slab", slab_odd)
+    even = lax.ppermute(even, "slab", slab_even)
+    row_odd = lax.ppermute(row_odd, "tile", tile_odd)
+    row_even = lax.ppermute(row_even, "tile", tile_even)
+
+    rim_odd, rim_even = pl.pallas_call(
+        corner_kernel,
+        out_shape=(rim, rim),
+        in_specs=[VMEM] * 2,
         out_specs=[VMEM] * 2,
         compiler_params=kernel_params(8),
-        cost_estimate=pl.CostEstimate(flops=8_000_000, bytes_accessed=2_300_000, transcendentals=0),
+        name="corners",
+    )(row_odd, row_even)
+    rim_odd = lax.ppermute(rim_odd, "slab", slab_odd)
+    rim_even = lax.ppermute(rim_even, "slab", slab_even)
+
+    history = like(history_steps.shape, F32)
+    sums, keep, steps, changes = pl.pallas_call(
+        gram_kernel,
+        out_shape=(
+            like((SUMS, LANES), F32),
+            like((depth // 2, rows, cols), F32),
+            history,
+            history,
+        ),
+        in_specs=[HBM] * 3,
+        out_specs=[VMEM] * 4,
+        scratch_shapes=[
+            pltpu.VMEM(passive_blocks.shape, jnp.int32),
+            pltpu.SemaphoreType.DMA((2, depth)),
+            pltpu.SemaphoreType.DMA,
+        ],
+        compiler_params=kernel_params(8),
+        cost_estimate=pl.CostEstimate(flops=8_000_000, bytes_accessed=4_300_000, transcendentals=0),
         name="gram",
-    )(history_steps, history_changes, passive_blocks)
-
-    edges = like((ROWS_SENT, cols), F32)
-    row_odd, row_even = pl.pallas_call(
-        pack_kernel,
-        out_shape=(edges, edges),
-        in_specs=[VMEM] * 3,
-        out_specs=[VMEM] * 2,
-        compiler_params=kernel_params(8),
-        name="edges",
-    )(u, got_odd, got_even)
-    odd, even = swaps(lax.axis_size("tile"))
-    row_odd = lax.ppermute(row_odd, "tile", odd)
-    row_even = lax.ppermute(row_even, "tile", even)
+    )(in_hbm(history_steps), in_hbm(history_changes), in_hbm(passive_blocks))
 
     padded = pltpu.VMEM((depth + 6, rows + 16, cols), F32)
     gradient, line = pl.pallas_call(
         sweep_kernel,
         out_shape=(like(shape, F32), like((devices, LANES), F32)),
-        in_specs=[VMEM] * 9,
+        in_specs=[VMEM] * 11,
         out_specs=[VMEM] * 2,
         scratch_shapes=[padded, padded, padded, pltpu.VMEM((SUMS, LANES), F32)],
         compiler_params=kernel_params(16),
         name="sweeps",
-    )(u, got_odd, got_even, row_odd, row_even, keep, history_steps, history_changes, sums)
+    )(u, odd, even, row_odd, row_even, rim_odd, rim_even, keep, steps, changes, sums)
 
     lines = lax.all_to_all(line, ("slab", "tile"), 0, 0, tiled=True)
 
@@ -340,10 +436,11 @@
         combine_kernel,
         out_shape=like(shape, F32),
         in_specs=[VMEM] * 4,
-        out_specs=VMEM,
+        out_specs=HBM,
+        scratch_shapes=[pltpu.VMEM(shape, F32), pltpu.SemaphoreType.DMA((depth,))],
         compiler_params=kernel_params(8),
         name="combine",
-    )(lines, gradient, history_steps, history_changes)
+    )(lines, gradient, steps, changes)
 
 
 def solution(mesh):

time: 48.1 us -> 46 us (0.956)
  local copies, waits for them, and re-layouts: 3.59 us -> 0 us
  Pallas kernels: 3.36 us -> 5.75 us
  waiting for transfers between devices: 5.46 us -> 3.23 us
  starting transfers between devices: 11.9 us -> 13.5 us
    unnamed x12 -> x0, local copies, waits for them, and re-layouts: 3.59 us -> none
    ppermute x4 -> x6, waiting for transfers between devices: 5.46 us -> 3.23 us  [the longest x1 2.32 us: per_device(): rim_odd = lax.ppermute(rim_odd, 'slab', slab_odd)]
    ppermute x4 -> x6, starting transfers between devices: 11.9 us -> 13.5 us  [the longest x1 5.85 us: per_device(): odd = lax.ppermute(odd, 'slab', slab_odd)]
    pallas_call x1, Pallas kernels: 0.84 us -> 2.2 us  [per_device(): pl.pallas_call(gram_kernel, out_shape=(like((SUMS, LANES), F32), like((de...]
    pallas_call x2, Pallas kernels: 0.16 us -> 1.22 us  [the longest x1 1.2 us: per_device(): pl.pallas_call(weight_kernel, out_shape=(like(shape, F32), edges, edges,...]
  transfers between devices with their start and end apart: 4 -> 6, of which waited for: 2 -> 2; matrix products, arithmetic and copies ran while one was open for 0% -> 0% of each run, Pallas kernels for 2% -> 5%
where the time goes in v2:
time: 46 us; the launch traced here: 45.8 us
  blocking collectives  23.4 us (51%)
  starting transfers between devices  13.5 us (29%)
  Pallas kernels  5.75 us (12%)
  waiting for transfers between devices  3.23 us (7%)
    all_to_all x1, blocking collectives, per_device(): lines = lax.all_to_all(line, ('slab', 'tile'), 0, 0, tiled=True)  23.4 us
    ppermute x1, starting transfers between devices, per_device(): odd = lax.ppermute(odd, 'slab', slab_odd)  5.85 us
    ppermute x1, starting transfers between devices, per_device(): row_even = lax.ppermute(row_even, 'tile', tile_even)  3.5 us
    ppermute x1, starting transfers between devices, per_device(): row_odd = lax.ppermute(row_odd, 'tile', tile_odd)  2.47 us
    ppermute x1, waiting for transfers between devices, per_device(): rim_odd = lax.ppermute(rim_odd, 'slab', slab_odd)  2.32 us
    pallas_call x1, Pallas kernels, per_device(): pl.pallas_call(gram_kernel, out_shape=(like((SUMS, LANES), F32), like((de...  2.2 us
    pallas_call x1, Pallas kernels, per_device(): pl.pallas_call(sweep_kernel, out_shape=(like(shape, F32), like((devices,...  1.38 us
    pallas_call x1, Pallas kernels, per_device(): pl.pallas_call(weight_kernel, out_shape=(like(shape, F32), edges, edges,...  1.2 us
  transfers between devices with their start and end apart: 6, of which 2 were waited for; matrix products, arithmetic and copies ran while one was open for 0% of the time, Pallas kernels for 5%

profile of v2, /device:TPU:1, one launch (start us, length us, event | category | flops | bytes accessed | tf_op | source)
XLA Modules:
  0.0 45.8 jit_solution(4248525666210601526)
XLA Ops:
  0.0 1.2 %weights.1 = (f32[4,16,1024]{2,1,0:T(8,128)S(1)}, f32[16,1024]{1,0:T(8,128)S(1)}, f32[16,1024]{1,0:T(8,128)S(1)}, f32[3,16,1024]{2,1,0:T(8,128)S(1)}, f32[3,16,1024]{2,1,0:T(8,128)S(1)}) custom-call(f32[4,16,1024]{2,1,0:T(8,128)} %sens_hbm.1, f32[4,16,1024]{2,1,0:T(8,128)} %dens_hbm.1), custom_call_target="tpu_custom_call" | custom-call | tf_op jit(solution)/shard_map/weights/pallas_call | solution.py:369
  1.2 5.8 %collective-permute-start = (f32[3,16,1024]{2,1,0:T(8,128)S(1)}, f32[3,16,1024]{2,1,0:T(8,128)S(1)}, u32[]{:S(2)}, u32[]{:S(2)}) collective-permute-start(f32[3,16,1024]{2,1,0:T(8,128)S(1)} %get-tuple-element.19), channel_id=1, source_target_pairs={{0,240},{16,32},{32,16},{48,64},{64,48},{80,96},{96,80},{112,128},... | collective-permute-start | bytes 589832 | tf_op jit(solution)/shard_map/ppermute | solution.py:385
  7.1 0.0 collective-permute-start.1
  7.1 2.5 %collective-permute-start.2 = (f32[16,1024]{1,0:T(8,128)S(1)}, f32[16,1024]{1,0:T(8,128)S(1)}, u32[]{:S(2)}, u32[]{:S(2)}) collective-permute-start(f32[16,1024]{1,0:T(8,128)S(1)} %get-tuple-element.21), channel_id=1, source_target_pairs={{0,15},{1,2},{2,1},{3,4},{4,3},{5,6},{6,5},{7,8},{8,7},{9,10},{10,... | collective-permute-start | bytes 196616 | tf_op jit(solution)/shard_map/ppermute | solution.py:387
  9.5 3.5 %collective-permute-start.3 = (f32[16,1024]{1,0:T(8,128)S(1)}, f32[16,1024]{1,0:T(8,128)S(1)}, u32[]{:S(2)}, u32[]{:S(2)}) collective-permute-start(f32[16,1024]{1,0:T(8,128)S(1)} %get-tuple-element.22), channel_id=1, source_target_pairs={{0,1},{1,0},{2,3},{3,2},{4,5},{5,4},{6,7},{7,6},{8,9},{9,8},{10,11... | collective-permute-start | bytes 196616 | tf_op jit(solution)/shard_map/ppermute | solution.py:388
  13.0 0.0 collective-permute-done.2.row_odd_ref
  13.0 0.9 %collective-permute-done.3.row_even_ref = f32[16,1024]{1,0:T(8,128)S(1)} collective-permute-done((f32[16,1024]{1,0:T(8,128)S(1)}, f32[16,1024]{1,0:T(8,128)S(1)}, u32[]{:S(2)}, u32[]{:S(2)}) %collective-permute-start.3) | collective-permute-done | bytes 65568 | tf_op jit(solution)/shard_map/ppermute | solution.py:388
  14.0 0.9 %collective-permute-start.4 = (f32[8,1024]{1,0:T(8,128)S(1)}, f32[8,1024]{1,0:T(8,128)S(1)}, u32[]{:S(2)}, u32[]{:S(2)}) collective-permute-start(f32[8,1024]{1,0:T(8,128)S(1)} %get-tuple-element.23), channel_id=1, source_target_pairs={{0,240},{16,32},{32,16},{48,64},{64,48},{80,96},{96,80},{112,128},... | collective-permute-start | bytes 98312 | tf_op jit(solution)/shard_map/ppermute | solution.py:398
  14.8 0.8 %collective-permute-start.5 = (f32[8,1024]{1,0:T(8,128)S(1)}, f32[8,1024]{1,0:T(8,128)S(1)}, u32[]{:S(2)}, u32[]{:S(2)}) collective-permute-start(f32[8,1024]{1,0:T(8,128)S(1)} %get-tuple-element.24), channel_id=1, source_target_pairs={{0,16},{16,0},{32,48},{48,32},{64,80},{80,64},{96,112},{112,96},{1... | collective-permute-start | bytes 98312 | tf_op jit(solution)/shard_map/ppermute | solution.py:399
  15.6 2.2 %gram.1 = (f32[32,128]{1,0:T(8,128)S(1)}, f32[2,16,1024]{2,1,0:T(8,128)S(1)}, f32[4,4,16,1024]{3,2,1,0:T(8,128)S(1)}, f32[4,4,16,1024]{3,2,1,0:T(8,128)S(1)}) custom-call(f32[4,4,16,1024]{3,2,1,0:T(8,128)} %steps_hbm.1, f32[4,4,16,1024]{3,2,1,0:T(8,128)} %changes_hbm.1, s32[2,8,512]{2,1,0:T(8,128)} %passive_hbm.1), custom_call_target="tpu_custom_call" | custom-call | flops 8000000 | bytes 4300000 | tf_op jit(solution)/shard_map/gram/pallas_call | solution.py:402
  17.8 2.3 %collective-permute-done.4.rim_odd_ref = f32[8,1024]{1,0:T(8,128)S(1)} collective-permute-done((f32[8,1024]{1,0:T(8,128)S(1)}, f32[8,1024]{1,0:T(8,128)S(1)}, u32[]{:S(2)}, u32[]{:S(2)}) %collective-permute-start.4) | collective-permute-done | bytes 32800 | tf_op jit(solution)/shard_map/ppermute | solution.py:398
  20.1 0.0 collective-permute-done.5.rim_even_ref
  20.1 0.0 collective-permute-done.odd_ref
  20.1 0.0 collective-permute-done.1.even_ref
  20.1 1.4 %sweeps.1 = (f32[4,16,1024]{2,1,0:T(8,128)S(1)}, f32[256,128]{1,0:T(8,128)S(1)}) custom-call(f32[4,16,1024]{2,1,0:T(8,128)S(1)} %get-tuple-element.18.u_ref, f32[3,16,1024]{2,1,0:T(8,128)S(1)} %collective-permute-done.odd_ref, f32[3,16,1024]{2,1,0:T(8,128)S(1)} %collective-permute-done.1.even_ref, f32[16,1024]{1,0:T(8,128)S(1)} %collective-permute-done.2.row_odd_ref, ...), custom_call_target="tpu_custom_call" | custom-call | tf_op jit(solution)/shard_map/sweeps/pallas_call | solution.py:423
  21.5 23.4 %all_to_all.11 = f32[256,1,128]{2,1,0:T(1,128)S(1)} all-to-all(f32[256,1,128]{2,1,0:T(1,128)S(1)} %bitcast.5), channel_id=1, replica_groups=mesh['slab'=16,'tile'=16] {'slab','tile'}, dimensions={0} | all-to-all | bytes 262144 | tf_op jit(solution)/shard_map/all_to_all | solution.py:433
  44.9 0.9 %combine.1 = f32[4,16,1024]{2,1,0:T(8,128)} custom-call(f32[256,128]{1,0:T(8,128)S(1)} %bitcast.4, f32[4,16,1024]{2,1,0:T(8,128)S(1)} %get-tuple-element.30.grad_ref, f32[4,4,16,1024]{3,2,1,0:T(8,128)S(1)} %get-tuple-element.26.steps_ref, f32[4,4,16,1024]{3,2,1,0:T(8,128)S(1)} %get-tuple-element.27.changes_ref), custom_call_target="tpu_custom_call" | custom-call | tf_op jit(solution)/shard_map/combine/pallas_call | solution.py:435
  (1 shorter events, 0.0 us)
Async XLA Ops:
  1.2 18.9 %collective-permute-start = (f32[3,16,1024]{2,1,0:T(8,128)S(1)}, f32[3,16,1024]{2,1,0:T(8,128)S(1)}, u32[]{:S(2)}, u32[]{:S(2)}) collective-permute-start(f32[3,16,1024]{2,1,0:T(8,128)S(1)} %get-tuple-element.19), channel_id=1, source_target_pairs={{0,240},{16,32},{32,16},{48,64},{64,48},{80,96},{96,80},{112,128},... | collective-permute-start | bytes 589832 | tf_op jit(solution)/shard_map/ppermute | solution.py:385
  7.1 13.1 %collective-permute-start.1 = (f32[3,16,1024]{2,1,0:T(8,128)S(1)}, f32[3,16,1024]{2,1,0:T(8,128)S(1)}, u32[]{:S(2)}, u32[]{:S(2)}) collective-permute-start(f32[3,16,1024]{2,1,0:T(8,128)S(1)} %get-tuple-element.20), channel_id=1, source_target_pairs={{0,16},{16,0},{32,48},{48,32},{64,80},{80,64},{96,112},{112,96},{1... | collective-permute-start | bytes 589832 | tf_op jit(solution)/shard_map/ppermute | solution.py:386
  7.1 6.0 %collective-permute-start.2 = (f32[16,1024]{1,0:T(8,128)S(1)}, f32[16,1024]{1,0:T(8,128)S(1)}, u32[]{:S(2)}, u32[]{:S(2)}) collective-permute-start(f32[16,1024]{1,0:T(8,128)S(1)} %get-tuple-element.21), channel_id=1, source_target_pairs={{0,15},{1,2},{2,1},{3,4},{4,3},{5,6},{6,5},{7,8},{8,7},{9,10},{10,... | collective-permute-start | bytes 196616 | tf_op jit(solution)/shard_map/ppermute | solution.py:387
  9.5 4.4 %collective-permute-start.3 = (f32[16,1024]{1,0:T(8,128)S(1)}, f32[16,1024]{1,0:T(8,128)S(1)}, u32[]{:S(2)}, u32[]{:S(2)}) collective-permute-start(f32[16,1024]{1,0:T(8,128)S(1)} %get-tuple-element.22), channel_id=1, source_target_pairs={{0,1},{1,0},{2,3},{3,2},{4,5},{5,4},{6,7},{7,6},{8,9},{9,8},{10,11... | collective-permute-start | bytes 196616 | tf_op jit(solution)/shard_map/ppermute | solution.py:388
  14.0 6.2 %collective-permute-start.4 = (f32[8,1024]{1,0:T(8,128)S(1)}, f32[8,1024]{1,0:T(8,128)S(1)}, u32[]{:S(2)}, u32[]{:S(2)}) collective-permute-start(f32[8,1024]{1,0:T(8,128)S(1)} %get-tuple-element.23), channel_id=1, source_target_pairs={{0,240},{16,32},{32,16},{48,64},{64,48},{80,96},{96,80},{112,128},... | collective-permute-start | bytes 98312 | tf_op jit(solution)/shard_map/ppermute | solution.py:398
  14.8 5.3 %collective-permute-start.5 = (f32[8,1024]{1,0:T(8,128)S(1)}, f32[8,1024]{1,0:T(8,128)S(1)}, u32[]{:S(2)}, u32[]{:S(2)}) collective-permute-start(f32[8,1024]{1,0:T(8,128)S(1)} %get-tuple-element.24), channel_id=1, source_target_pairs={{0,16},{16,0},{32,48},{48,32},{64,80},{80,64},{96,112},{112,96},{1... | collective-permute-start | bytes 98312 | tf_op jit(solution)/shard_map/ppermute | solution.py:399

commit v3 on v2

--- a/solution.py
+++ b/solution.py
@@ -151,7 +151,7 @@
         sums_ref[n : n + 1, :] = jnp.sum(value, axis=0, keepdims=True)
 
 
-def corner_kernel(row_odd_ref, row_even_ref, rim_odd_ref, rim_even_ref):
+def corner_kernel(row_odd_ref, row_even_ref, sums_ref, rim_odd_ref, rim_even_ref):
     cols = rim_odd_ref.shape[1]
     depth = 4
     slab_odd = lax.rem(lax.axis_index("slab"), 2)
@@ -382,21 +382,10 @@
 
     slab_odd, slab_even = swaps(lax.axis_size("slab"))
     tile_odd, tile_even = swaps(lax.axis_size("tile"))
+    row_odd = lax.ppermute(row_odd, "tile", tile_odd)
+    row_even = lax.ppermute(row_even, "tile", tile_even)
     odd = lax.ppermute(odd, "slab", slab_odd)
     even = lax.ppermute(even, "slab", slab_even)
-    row_odd = lax.ppermute(row_odd, "tile", tile_odd)
-    row_even = lax.ppermute(row_even, "tile", tile_even)
-
-    rim_odd, rim_even = pl.pallas_call(
-        corner_kernel,
-        out_shape=(rim, rim),
-        in_specs=[VMEM] * 2,
-        out_specs=[VMEM] * 2,
-        compiler_params=kernel_params(8),
-        name="corners",
-    )(row_odd, row_even)
-    rim_odd = lax.ppermute(rim_odd, "slab", slab_odd)
-    rim_even = lax.ppermute(rim_even, "slab", slab_even)
 
     history = like(history_steps.shape, F32)
     sums, keep, steps, changes = pl.pallas_call(
@@ -415,9 +404,20 @@
             pltpu.SemaphoreType.DMA,
         ],
         compiler_params=kernel_params(8),
-        cost_estimate=pl.CostEstimate(flops=8_000_000, bytes_accessed=4_300_000, transcendentals=0),
+        cost_estimate=pl.CostEstimate(flops=8_000_000_000, bytes_accessed=43_000_000, transcendentals=0),
         name="gram",
     )(in_hbm(history_steps), in_hbm(history_changes), in_hbm(passive_blocks))
+
+    rim_odd, rim_even = pl.pallas_call(
+        corner_kernel,
+        out_shape=(rim, rim),
+        in_specs=[VMEM] * 3,
+        out_specs=[VMEM] * 2,
+        compiler_params=kernel_params(8),
+        name="corners",
+    )(row_odd, row_even, sums)
+    rim_odd = lax.ppermute(rim_odd, "slab", slab_odd)
+    rim_even = lax.ppermute(rim_even, "slab", slab_even)
 
     padded = pltpu.VMEM((depth + 6, rows + 16, cols), F32)
     gradient, line = pl.pallas_call(

time: 46 us -> 44.5 us (0.967)
  blocking collectives: 23.4 us -> 20.5 us
  waiting for transfers between devices: 3.23 us -> 4.53 us
    all_to_all x1, blocking collectives: 23.4 us -> 20.5 us  [per_device(): lines = lax.all_to_all(line, ('slab', 'tile'), 0, 0, tiled=True)]
    ppermute x1, waiting for transfers between devices: 2.32 us -> 4.52 us  [per_device(): rim_odd = lax.ppermute(rim_odd, 'slab', slab_odd)]
    ppermute x1, starting transfers between devices: 5.85 us -> 4.93 us  [per_device(): odd = lax.ppermute(odd, 'slab', slab_odd)]
    ppermute x1, waiting for transfers between devices: 0.9 us -> 0.01 us  [per_device(): row_even = lax.ppermute(row_even, 'tile', tile_even)]
    ppermute x1, starting transfers between devices: 2.47 us -> 3.11 us  [per_device(): row_odd = lax.ppermute(row_odd, 'tile', tile_odd)]
  transfers between devices with their start and end apart: 6 -> 6, of which waited for: 2 -> 1; matrix products, arithmetic and copies ran while one was open for 0% -> 0% of each run, Pallas kernels for 5% -> 5%
where the time goes in v3:
time: 44.5 us; the launch traced here: 44.3 us
  blocking collectives  20.5 us (46%)
  starting transfers between devices  13.5 us (30%)
  Pallas kernels  5.78 us (13%)
  waiting for transfers between devices  4.53 us (10%)
    all_to_all x1, blocking collectives, per_device(): lines = lax.all_to_all(line, ('slab', 'tile'), 0, 0, tiled=True)  20.5 us
    ppermute x1, starting transfers between devices, per_device(): odd = lax.ppermute(odd, 'slab', slab_odd)  4.93 us
    ppermute x1, waiting for transfers between devices, per_device(): rim_odd = lax.ppermute(rim_odd, 'slab', slab_odd)  4.52 us
    ppermute x1, starting transfers between devices, per_device(): row_even = lax.ppermute(row_even, 'tile', tile_even)  3.78 us
    ppermute x1, starting transfers between devices, per_device(): row_odd = lax.ppermute(row_odd, 'tile', tile_odd)  3.11 us
    pallas_call x1, Pallas kernels, per_device(): pl.pallas_call(gram_kernel, out_shape=(like((SUMS, LANES), F32), like((de...  2.2 us
    pallas_call x1, Pallas kernels, per_device(): pl.pallas_call(sweep_kernel, out_shape=(like(shape, F32), like((devices,...  1.38 us
    pallas_call x1, Pallas kernels, per_device(): pl.pallas_call(weight_kernel, out_shape=(like(shape, F32), edges, edges,...  1.2 us
  transfers between devices with their start and end apart: 6, of which 1 were waited for; matrix products, arithmetic and copies ran while one was open for 0% of the time, Pallas kernels for 5%

profile of v3, /device:TPU:1, one launch (start us, length us, event | category | flops | bytes accessed | tf_op | source)
XLA Modules:
  0.0 44.3 jit_solution(17574487951138392856)
XLA Ops:
  0.0 1.2 %weights.1 = (f32[4,16,1024]{2,1,0:T(8,128)S(1)}, f32[16,1024]{1,0:T(8,128)S(1)}, f32[16,1024]{1,0:T(8,128)S(1)}, f32[3,16,1024]{2,1,0:T(8,128)S(1)}, f32[3,16,1024]{2,1,0:T(8,128)S(1)}) custom-call(f32[4,16,1024]{2,1,0:T(8,128)} %sens_hbm.1, f32[4,16,1024]{2,1,0:T(8,128)} %dens_hbm.1), custom_call_target="tpu_custom_call" | custom-call | tf_op jit(solution)/shard_map/weights/pallas_call | solution.py:369
  1.2 3.1 %collective-permute-start.2 = (f32[16,1024]{1,0:T(8,128)S(1)}, f32[16,1024]{1,0:T(8,128)S(1)}, u32[]{:S(2)}, u32[]{:S(2)}) collective-permute-start(f32[16,1024]{1,0:T(8,128)S(1)} %get-tuple-element.21), channel_id=1, source_target_pairs={{0,15},{1,2},{2,1},{3,4},{4,3},{5,6},{6,5},{7,8},{8,7},{9,10},{10,... | collective-permute-start | bytes 196616 | tf_op jit(solution)/shard_map/ppermute | solution.py:385
  4.3 3.8 %collective-permute-start.3 = (f32[16,1024]{1,0:T(8,128)S(1)}, f32[16,1024]{1,0:T(8,128)S(1)}, u32[]{:S(2)}, u32[]{:S(2)}) collective-permute-start(f32[16,1024]{1,0:T(8,128)S(1)} %get-tuple-element.22), channel_id=1, source_target_pairs={{0,1},{1,0},{2,3},{3,2},{4,5},{5,4},{6,7},{7,6},{8,9},{9,8},{10,11... | collective-permute-start | bytes 196616 | tf_op jit(solution)/shard_map/ppermute | solution.py:386
  8.1 4.9 %collective-permute-start = (f32[3,16,1024]{2,1,0:T(8,128)S(1)}, f32[3,16,1024]{2,1,0:T(8,128)S(1)}, u32[]{:S(2)}, u32[]{:S(2)}) collective-permute-start(f32[3,16,1024]{2,1,0:T(8,128)S(1)} %get-tuple-element.19), channel_id=1, source_target_pairs={{0,240},{16,32},{32,16},{48,64},{64,48},{80,96},{96,80},{112,128},... | collective-permute-start | bytes 589832 | tf_op jit(solution)/shard_map/ppermute | solution.py:387
  13.0 0.0 collective-permute-start.1
  13.0 2.2 %gram.1 = (f32[32,128]{1,0:T(8,128)S(1)}, f32[2,16,1024]{2,1,0:T(8,128)S(1)}, f32[4,4,16,1024]{3,2,1,0:T(8,128)S(1)}, f32[4,4,16,1024]{3,2,1,0:T(8,128)S(1)}) custom-call(f32[4,4,16,1024]{3,2,1,0:T(8,128)} %steps_hbm.1, f32[4,4,16,1024]{3,2,1,0:T(8,128)} %changes_hbm.1, s32[2,8,512]{2,1,0:T(8,128)} %passive_hbm.1), custom_call_target="tpu_custom_call" | custom-call | flops 8000000000 | bytes 43000000 | tf_op jit(solution)/shard_map/gram/pallas_call | solution.py:391
  15.2 0.0 collective-permute-done.2.row_odd_ref
  15.2 0.0 collective-permute-done.3.row_even_ref
  15.3 0.1 corners.1
  15.3 0.9 %collective-permute-start.4 = (f32[8,1024]{1,0:T(8,128)S(1)}, f32[8,1024]{1,0:T(8,128)S(1)}, u32[]{:S(2)}, u32[]{:S(2)}) collective-permute-start(f32[8,1024]{1,0:T(8,128)S(1)} %get-tuple-element.24), channel_id=1, source_target_pairs={{0,240},{16,32},{32,16},{48,64},{64,48},{80,96},{96,80},{112,128},... | collective-permute-start | bytes 98312 | tf_op jit(solution)/shard_map/ppermute | solution.py:419
  16.2 0.8 %collective-permute-start.5 = (f32[8,1024]{1,0:T(8,128)S(1)}, f32[8,1024]{1,0:T(8,128)S(1)}, u32[]{:S(2)}, u32[]{:S(2)}) collective-permute-start(f32[8,1024]{1,0:T(8,128)S(1)} %get-tuple-element.25), channel_id=1, source_target_pairs={{0,16},{16,0},{32,48},{48,32},{64,80},{80,64},{96,112},{112,96},{1... | collective-permute-start | bytes 98312 | tf_op jit(solution)/shard_map/ppermute | solution.py:420
  17.0 4.5 %collective-permute-done.4.rim_odd_ref = f32[8,1024]{1,0:T(8,128)S(1)} collective-permute-done((f32[8,1024]{1,0:T(8,128)S(1)}, f32[8,1024]{1,0:T(8,128)S(1)}, u32[]{:S(2)}, u32[]{:S(2)}) %collective-permute-start.4) | collective-permute-done | bytes 32800 | tf_op jit(solution)/shard_map/ppermute | solution.py:419
  21.5 0.0 collective-permute-done.5.rim_even_ref
  21.5 0.0 collective-permute-done.odd_ref
  21.5 0.0 collective-permute-done.1.even_ref
  21.5 1.4 %sweeps.1 = (f32[4,16,1024]{2,1,0:T(8,128)S(1)}, f32[256,128]{1,0:T(8,128)S(1)}) custom-call(f32[4,16,1024]{2,1,0:T(8,128)S(1)} %get-tuple-element.18.u_ref, f32[3,16,1024]{2,1,0:T(8,128)S(1)} %collective-permute-done.odd_ref, f32[3,16,1024]{2,1,0:T(8,128)S(1)} %collective-permute-done.1.even_ref, f32[16,1024]{1,0:T(8,128)S(1)} %collective-permute-done.2.row_odd_ref, ...), custom_call_target="tpu_custom_call" | custom-call | tf_op jit(solution)/shard_map/sweeps/pallas_call | solution.py:423
  22.9 20.5 %all_to_all.11 = f32[256,1,128]{2,1,0:T(1,128)S(1)} all-to-all(f32[256,1,128]{2,1,0:T(1,128)S(1)} %bitcast.5), channel_id=1, replica_groups=mesh['slab'=16,'tile'=16] {'slab','tile'}, dimensions={0} | all-to-all | bytes 262144 | tf_op jit(solution)/shard_map/all_to_all | solution.py:433
  43.4 0.9 %combine.1 = f32[4,16,1024]{2,1,0:T(8,128)} custom-call(f32[256,128]{1,0:T(8,128)S(1)} %bitcast.4, f32[4,16,1024]{2,1,0:T(8,128)S(1)} %get-tuple-element.30.grad_ref, f32[4,4,16,1024]{3,2,1,0:T(8,128)S(1)} %get-tuple-element.27.steps_ref, f32[4,4,16,1024]{3,2,1,0:T(8,128)S(1)} %get-tuple-element.28.changes_ref), custom_call_target="tpu_custom_call" | custom-call | tf_op jit(solution)/shard_map/combine/pallas_call | solution.py:435
Async XLA Ops:
  1.2 14.0 %collective-permute-start.2 = (f32[16,1024]{1,0:T(8,128)S(1)}, f32[16,1024]{1,0:T(8,128)S(1)}, u32[]{:S(2)}, u32[]{:S(2)}) collective-permute-start(f32[16,1024]{1,0:T(8,128)S(1)} %get-tuple-element.21), channel_id=1, source_target_pairs={{0,15},{1,2},{2,1},{3,4},{4,3},{5,6},{6,5},{7,8},{8,7},{9,10},{10,... | collective-permute-start | bytes 196616 | tf_op jit(solution)/shard_map/ppermute | solution.py:385
  4.3 10.9 %collective-permute-start.3 = (f32[16,1024]{1,0:T(8,128)S(1)}, f32[16,1024]{1,0:T(8,128)S(1)}, u32[]{:S(2)}, u32[]{:S(2)}) collective-permute-start(f32[16,1024]{1,0:T(8,128)S(1)} %get-tuple-element.22), channel_id=1, source_target_pairs={{0,1},{1,0},{2,3},{3,2},{4,5},{5,4},{6,7},{7,6},{8,9},{9,8},{10,11... | collective-permute-start | bytes 196616 | tf_op jit(solution)/shard_map/ppermute | solution.py:386
  8.1 13.4 %collective-permute-start = (f32[3,16,1024]{2,1,0:T(8,128)S(1)}, f32[3,16,1024]{2,1,0:T(8,128)S(1)}, u32[]{:S(2)}, u32[]{:S(2)}) collective-permute-start(f32[3,16,1024]{2,1,0:T(8,128)S(1)} %get-tuple-element.19), channel_id=1, source_target_pairs={{0,240},{16,32},{32,16},{48,64},{64,48},{80,96},{96,80},{112,128},... | collective-permute-start | bytes 589832 | tf_op jit(solution)/shard_map/ppermute | solution.py:387
  13.0 8.5 %collective-permute-start.1 = (f32[3,16,1024]{2,1,0:T(8,128)S(1)}, f32[3,16,1024]{2,1,0:T(8,128)S(1)}, u32[]{:S(2)}, u32[]{:S(2)}) collective-permute-start(f32[3,16,1024]{2,1,0:T(8,128)S(1)} %get-tuple-element.20), channel_id=1, source_target_pairs={{0,16},{16,0},{32,48},{48,32},{64,80},{80,64},{96,112},{112,96},{1... | collective-permute-start | bytes 589832 | tf_op jit(solution)/shard_map/ppermute | solution.py:388
  15.3 6.2 %collective-permute-start.4 = (f32[8,1024]{1,0:T(8,128)S(1)}, f32[8,1024]{1,0:T(8,128)S(1)}, u32[]{:S(2)}, u32[]{:S(2)}) collective-permute-start(f32[8,1024]{1,0:T(8,128)S(1)} %get-tuple-element.24), channel_id=1, source_target_pairs={{0,240},{16,32},{32,16},{48,64},{64,48},{80,96},{96,80},{112,128},... | collective-permute-start | bytes 98312 | tf_op jit(solution)/shard_map/ppermute | solution.py:419
  16.2 5.3 %collective-permute-start.5 = (f32[8,1024]{1,0:T(8,128)S(1)}, f32[8,1024]{1,0:T(8,128)S(1)}, u32[]{:S(2)}, u32[]{:S(2)}) collective-permute-start(f32[8,1024]{1,0:T(8,128)S(1)} %get-tuple-element.25), channel_id=1, source_target_pairs={{0,16},{16,0},{32,48},{48,32},{64,80},{80,64},{96,112},{112,96},{1... | collective-permute-start | bytes 98312 | tf_op jit(solution)/shard_map/ppermute | solution.py:420

commit v4 on v2

--- a/solution.py
+++ b/solution.py
@@ -22,7 +22,7 @@
 SG = [2 * len(PAIRS) + n for n in range(MEM)]
 YG = [2 * len(PAIRS) + MEM + n for n in range(MEM)]
 SUMS = 32
-ROWS_SENT = 16
+ROWS_SENT = 24
 
 VMEM = pl.BlockSpec(memory_space=pltpu.VMEM)
 HBM = pl.BlockSpec(memory_space=pltpu.HBM)
@@ -36,8 +36,8 @@
     sens_hbm,
     dens_hbm,
     u_ref,
-    row_odd_ref,
-    row_even_ref,
+    rim_odd_ref,
+    rim_even_ref,
     odd_ref,
     even_ref,
     sens_ref,
@@ -46,7 +46,6 @@
 ):
     depth, rows, cols = u_ref.shape
     slab_odd = lax.rem(lax.axis_index("slab"), 2)
-    tile_odd = lax.rem(lax.axis_index("tile"), 2)
     copies = [
         [
             pltpu.make_async_copy(from_ref.at[z], to_ref.at[z], arrived.at[n, z])
@@ -67,20 +66,17 @@
         slope = sharpness * (1.0 - bend * bend) / denominator
         u_ref[z] = sens_ref[z] * slope / diagonal_value
 
-    odd_ref[...] = u_ref[pl.ds(slab_odd, SWEEPS)]
-    even_ref[...] = u_ref[pl.ds(1 - slab_odd, SWEEPS)]
-
-    def edge_rows(to_ref, start):
-        for z in range(depth):
-            to_ref[3 * z : 3 * z + 3, :] = u_ref[z, start : start + 3, :]
-        to_ref[3 * depth :, :] = jnp.zeros((to_ref.shape[0] - 3 * depth, cols), F32)
-
-    for parity in range(2):
-
-        @pl.when(tile_odd == parity)
-        def _():
-            edge_rows(row_odd_ref, rows - 3 if parity else 0)
-            edge_rows(row_even_ref, 0 if parity else rows - 3)
+    for rim_ref, layers_ref, top in (
+        (rim_odd_ref, odd_ref, slab_odd),
+        (rim_even_ref, even_ref, 1 - slab_odd),
+    ):
+        near, second = (depth - 1) * top, 1 + (depth - 3) * top
+        rim_ref[0:2, :] = u_ref[near, 0:2, :]
+        rim_ref[2:4, :] = u_ref[near, rows - 2 : rows, :]
+        rim_ref[4:5, :] = u_ref[second, 0:1, :]
+        rim_ref[5:6, :] = u_ref[second, rows - 1 : rows, :]
+        rim_ref[6:8, :] = jnp.zeros((2, cols), F32)
+        layers_ref[...] = u_ref[pl.ds(top, SWEEPS)]
 
 
 def gram_kernel(
@@ -151,28 +147,30 @@
         sums_ref[n : n + 1, :] = jnp.sum(value, axis=0, keepdims=True)
 
 
-def corner_kernel(row_odd_ref, row_even_ref, rim_odd_ref, rim_even_ref):
-    cols = rim_odd_ref.shape[1]
-    depth = 4
+def pack_kernel(u_ref, odd_ref, even_ref, row_odd_ref, row_even_ref):
+    depth, rows = u_ref.shape[:2]
     slab_odd = lax.rem(lax.axis_index("slab"), 2)
     tile_odd = lax.rem(lax.axis_index("tile"), 2)
 
     def pack(low_ref, high_ref, out_ref, top):
-        near, second = (3 * (depth - 1), 3 * (depth - 2)) if top else (0, 3)
-        out_ref[0:2, :] = low_ref[near + 1 : near + 3, :]
-        out_ref[2:4, :] = high_ref[near : near + 2, :]
-        out_ref[4:5, :] = low_ref[second + 2 : second + 3, :]
-        out_ref[5:6, :] = high_ref[second : second + 1, :]
-        out_ref[6:8, :] = jnp.zeros((2, cols), F32)
+        for z in range(depth):
+            start = rows - 3 if top else 0
+            out_ref[3 * z : 3 * z + 3, :] = u_ref[z, start : start + 3, :]
+        near, second = (2, 5) if top else (0, 4)
+        out_ref[12:14, :] = low_ref[near : near + 2, :]
+        out_ref[14:16, :] = high_ref[near : near + 2, :]
+        out_ref[16:17, :] = low_ref[second : second + 1, :]
+        out_ref[17:18, :] = high_ref[second : second + 1, :]
+        out_ref[18:24, :] = jnp.zeros((6, out_ref.shape[1]), F32)
 
     for parity in range(2):
         for top in range(2):
 
-            @pl.when((tile_odd == parity) & (slab_odd == top))
+            @pl.when((slab_odd == parity) & (tile_odd == top))
             def _():
-                beside = (row_even_ref, row_odd_ref) if parity else (row_odd_ref, row_even_ref)
-                pack(*beside, rim_odd_ref, top == 1)
-                pack(*beside, rim_even_ref, top == 0)
+                low_ref, high_ref = (even_ref, odd_ref) if parity else (odd_ref, even_ref)
+                pack(low_ref, high_ref, row_odd_ref, top == 1)
+                pack(low_ref, high_ref, row_even_ref, top == 0)
 
 
 def sweep_kernel(
@@ -181,8 +179,6 @@
     even_ref,
     row_odd_ref,
     row_even_ref,
-    rim_odd_ref,
-    rim_even_ref,
     keep_ref,
     steps_ref,
     changes_ref,
@@ -207,31 +203,30 @@
     for z in range(depth):
         start_ref[3 + z, 8 : 8 + rows, :] = u_ref[z]
 
+    def layers(low_ref, high_ref):
+        for z in range(3):
+            start_ref[z, 8 : 8 + rows, :] = low_ref[z] * inside["low_z"]
+            start_ref[7 + z, 8 : 8 + rows, :] = high_ref[z] * inside["high_z"]
+
     def edge(from_ref, first, count, z, factor, high):
         to = 8 + rows if high else 8 - count
         start_ref[z, to : to + count, :] = from_ref[first : first + count, :] * factor
 
-    def below_and_above(from_ref, rim_ref, high):
-        factor = inside["high_z" if high else "low_z"]
-        for z in range(3):
-            start_ref[7 * high + z, 8 : 8 + rows, :] = from_ref[z] * factor
-        near, second = (7, 8) if high else (2, 1)
-        low_factor, high_factor = factor * inside["low_y"], factor * inside["high_y"]
-        edge(rim_ref, 0, 2, near, low_factor, False)
-        edge(rim_ref, 2, 2, near, high_factor, True)
-        edge(rim_ref, 4, 1, second, low_factor, False)
-        edge(rim_ref, 5, 1, second, high_factor, True)
-
     def beside(from_ref, high):
+        factor = inside["high_y" if high else "low_y"]
         for z in range(depth):
-            edge(from_ref, 3 * z, 3, 3 + z, inside["high_y" if high else "low_y"], high)
+            edge(from_ref, 3 * z, 3, 3 + z, factor, high)
+        low_factor, high_factor = factor * inside["low_z"], factor * inside["high_z"]
+        edge(from_ref, 12, 2, 2, low_factor, high)
+        edge(from_ref, 14, 2, 7, high_factor, high)
+        edge(from_ref, 16, 1, 1, low_factor, high)
+        edge(from_ref, 17, 1, 8, high_factor, high)
 
     for parity in range(2):
 
         @pl.when(slab_odd == parity)
         def _():
-            below_and_above(odd_ref, rim_odd_ref, parity == 1)
-            below_and_above(even_ref, rim_even_ref, parity == 0)
+            layers(*((even_ref, odd_ref) if parity else (odd_ref, even_ref)))
 
         @pl.when(tile_odd == parity)
         def _():
@@ -366,9 +361,9 @@
     )
     devices = lax.axis_size("slab") * lax.axis_size("tile")
 
-    u, row_odd, row_even, odd, even = pl.pallas_call(
+    u, rim_odd, rim_even, odd, even = pl.pallas_call(
         weight_kernel,
-        out_shape=(like(shape, F32), edges, edges, layers, layers),
+        out_shape=(like(shape, F32), rim, rim, layers, layers),
         in_specs=[HBM] * 2,
         out_specs=[VMEM] * 5,
         scratch_shapes=[
@@ -380,23 +375,23 @@
         name="weights",
     )(in_hbm(sensitivity), in_hbm(filtered_density))
 
-    slab_odd, slab_even = swaps(lax.axis_size("slab"))
-    tile_odd, tile_even = swaps(lax.axis_size("tile"))
-    odd = lax.ppermute(odd, "slab", slab_odd)
-    even = lax.ppermute(even, "slab", slab_even)
-    row_odd = lax.ppermute(row_odd, "tile", tile_odd)
-    row_even = lax.ppermute(row_even, "tile", tile_even)
-
-    rim_odd, rim_even = pl.pallas_call(
-        corner_kernel,
-        out_shape=(rim, rim),
-        in_specs=[VMEM] * 2,
+    odd_pairs, even_pairs = swaps(lax.axis_size("slab"))
+    rim_odd = lax.ppermute(rim_odd, "slab", odd_pairs)
+    rim_even = lax.ppermute(rim_even, "slab", even_pairs)
+    odd = lax.ppermute(odd, "slab", odd_pairs)
+    even = lax.ppermute(even, "slab", even_pairs)
+
+    row_odd, row_even = pl.pallas_call(
+        pack_kernel,
+        out_shape=(edges, edges),
+        in_specs=[VMEM] * 3,
         out_specs=[VMEM] * 2,
         compiler_params=kernel_params(8),
-        name="corners",
-    )(row_odd, row_even)
-    rim_odd = lax.ppermute(rim_odd, "slab", slab_odd)
-    rim_even = lax.ppermute(rim_even, "slab", slab_even)
+        name="edges",
+    )(u, rim_odd, rim_even)
+    odd_pairs, even_pairs = swaps(lax.axis_size("tile"))
+    row_odd = lax.ppermute(row_odd, "tile", odd_pairs)
+    row_even = lax.ppermute(row_even, "tile", even_pairs)
 
     history = like(history_steps.shape, F32)
     sums, keep, steps, changes = pl.pallas_call(
@@ -415,7 +410,7 @@
             pltpu.SemaphoreType.DMA,
         ],
         compiler_params=kernel_params(8),
-        cost_estimate=pl.CostEstimate(flops=8_000_000, bytes_accessed=4_300_000, transcendentals=0),
+        cost_estimate=pl.CostEstimate(flops=8_000_000_000, bytes_accessed=43_000_000, transcendentals=0),
         name="gram",
     )(in_hbm(history_steps), in_hbm(history_changes), in_hbm(passive_blocks))
 
@@ -423,12 +418,12 @@
     gradient, line = pl.pallas_call(
         sweep_kernel,
         out_shape=(like(shape, F32), like((devices, LANES), F32)),
-        in_specs=[VMEM] * 11,
+        in_specs=[VMEM] * 9,
         out_specs=[VMEM] * 2,
         scratch_shapes=[padded, padded, padded, pltpu.VMEM((SUMS, LANES), F32)],
         compiler_params=kernel_params(16),
         name="sweeps",
-    )(u, odd, even, row_odd, row_even, rim_odd, rim_even, keep, steps, changes, sums)
+    )(u, odd, even, row_odd, row_even, keep, steps, changes, sums)
 
     lines = lax.all_to_all(line, ("slab", "tile"), 0, 0, tiled=True)
 

time: 46 us -> 44.7 us (0.972)
  waiting for transfers between devices: 3.23 us -> 1.6 us
  blocking collectives: 23.4 us -> 24 us
    ppermute x6, waiting for transfers between devices: 3.23 us -> 1.6 us  [the longest x1 1.59 us: per_device(): rim_even = lax.ppermute(rim_even, 'slab', even_pairs)]
    all_to_all x1, blocking collectives: 23.4 us -> 24 us  [per_device(): lines = lax.all_to_all(line, ('slab', 'tile'), 0, 0, tiled=True)]
  transfers between devices with their start and end apart: 6 -> 6, of which waited for: 2 -> 1; matrix products, arithmetic and copies ran while one was open for 0% -> 0% of each run, Pallas kernels for 5% -> 5%
where the time goes in v4:
time: 44.7 us; the launch traced here: 44.5 us
  blocking collectives  24 us (54%)
  starting transfers between devices  13.1 us (29%)
  Pallas kernels  5.77 us (13%)
  waiting for transfers between devices  1.6 us (4%)
    all_to_all x1, blocking collectives, per_device(): lines = lax.all_to_all(line, ('slab', 'tile'), 0, 0, tiled=True)  24 us
    ppermute x1, starting transfers between devices, per_device(): rim_odd = lax.ppermute(rim_odd, 'slab', odd_pairs)  5.85 us
    ppermute x1, starting transfers between devices, per_device(): row_odd = lax.ppermute(row_odd, 'tile', odd_pairs)  3.73 us
    pallas_call x1, Pallas kernels, per_device(): pl.pallas_call(gram_kernel, out_shape=(like((SUMS, LANES), F32), like((de...  2.2 us
    ppermute x1, starting transfers between devices, per_device(): row_even = lax.ppermute(row_even, 'tile', even_pairs)  2.03 us
    ppermute x1, waiting for transfers between devices, per_device(): rim_even = lax.ppermute(rim_even, 'slab', even_pairs)  1.59 us
    pallas_call x1, Pallas kernels, per_device(): pl.pallas_call(sweep_kernel, out_shape=(like(shape, F32), like((devices,...  1.38 us
    pallas_call x1, Pallas kernels, per_device(): pl.pallas_call(weight_kernel, out_shape=(like(shape, F32), rim, rim, laye...  1.18 us
  transfers between devices with their start and end apart: 6, of which 1 were waited for; matrix products, arithmetic and copies ran while one was open for 0% of the time, Pallas kernels for 5%

profile of v4, /device:TPU:1, one launch (start us, length us, event | category | flops | bytes accessed | tf_op | source)
XLA Modules:
  0.0 44.5 jit_solution(8678322821481249521)
XLA Ops:
  0.0 1.2 %weights.1 = (f32[4,16,1024]{2,1,0:T(8,128)S(1)}, f32[8,1024]{1,0:T(8,128)S(1)}, f32[8,1024]{1,0:T(8,128)S(1)}, f32[3,16,1024]{2,1,0:T(8,128)S(1)}, f32[3,16,1024]{2,1,0:T(8,128)S(1)}) custom-call(f32[4,16,1024]{2,1,0:T(8,128)} %sens_hbm.1, f32[4,16,1024]{2,1,0:T(8,128)} %dens_hbm.1), custom_call_target="tpu_custom_call" | custom-call | tf_op jit(solution)/shard_map/weights/pallas_call | solution.py:364
  1.2 5.8 %collective-permute-start.2 = (f32[8,1024]{1,0:T(8,128)S(1)}, f32[8,1024]{1,0:T(8,128)S(1)}, u32[]{:S(2)}, u32[]{:S(2)}) collective-permute-start(f32[8,1024]{1,0:T(8,128)S(1)} %get-tuple-element.21), channel_id=1, source_target_pairs={{0,240},{16,32},{32,16},{48,64},{64,48},{80,96},{96,80},{112,128},... | collective-permute-start | bytes 98312 | tf_op jit(solution)/shard_map/ppermute | solution.py:379
  7.0 0.0 collective-permute-start.3
  7.0 0.8 %collective-permute-start = (f32[3,16,1024]{2,1,0:T(8,128)S(1)}, f32[3,16,1024]{2,1,0:T(8,128)S(1)}, u32[]{:S(2)}, u32[]{:S(2)}) collective-permute-start(f32[3,16,1024]{2,1,0:T(8,128)S(1)} %get-tuple-element.19), channel_id=1, source_target_pairs={{0,240},{16,32},{32,16},{48,64},{64,48},{80,96},{96,80},{112,128},... | collective-permute-start | bytes 589832 | tf_op jit(solution)/shard_map/ppermute | solution.py:381
  7.8 0.7 %collective-permute-start.1 = (f32[3,16,1024]{2,1,0:T(8,128)S(1)}, f32[3,16,1024]{2,1,0:T(8,128)S(1)}, u32[]{:S(2)}, u32[]{:S(2)}) collective-permute-start(f32[3,16,1024]{2,1,0:T(8,128)S(1)} %get-tuple-element.20), channel_id=1, source_target_pairs={{0,16},{16,0},{32,48},{48,32},{64,80},{80,64},{96,112},{112,96},{1... | collective-permute-start | bytes 589832 | tf_op jit(solution)/shard_map/ppermute | solution.py:382
  8.5 0.0 collective-permute-done.2.odd_ref
  8.5 1.6 %collective-permute-done.3.even_ref = f32[8,1024]{1,0:T(8,128)S(1)} collective-permute-done((f32[8,1024]{1,0:T(8,128)S(1)}, f32[8,1024]{1,0:T(8,128)S(1)}, u32[]{:S(2)}, u32[]{:S(2)}) %collective-permute-start.3) | collective-permute-done | bytes 32800 | tf_op jit(solution)/shard_map/ppermute | solution.py:380
  10.1 0.1 edges.1
  10.2 3.7 %collective-permute-start.4 = (f32[24,1024]{1,0:T(8,128)S(1)}, f32[24,1024]{1,0:T(8,128)S(1)}, u32[]{:S(2)}, u32[]{:S(2)}) collective-permute-start(f32[24,1024]{1,0:T(8,128)S(1)} %get-tuple-element.23), channel_id=1, source_target_pairs={{0,15},{1,2},{2,1},{3,4},{4,3},{5,6},{6,5},{7,8},{8,7},{9,10},{10,... | collective-permute-start | bytes 294920 | tf_op jit(solution)/shard_map/ppermute | solution.py:393
  13.9 2.0 %collective-permute-start.5 = (f32[24,1024]{1,0:T(8,128)S(1)}, f32[24,1024]{1,0:T(8,128)S(1)}, u32[]{:S(2)}, u32[]{:S(2)}) collective-permute-start(f32[24,1024]{1,0:T(8,128)S(1)} %get-tuple-element.24), channel_id=1, source_target_pairs={{0,1},{1,0},{2,3},{3,2},{4,5},{5,4},{6,7},{7,6},{8,9},{9,8},{10,11... | collective-permute-start | bytes 294920 | tf_op jit(solution)/shard_map/ppermute | solution.py:394
  15.9 2.2 %gram.1 = (f32[32,128]{1,0:T(8,128)S(1)}, f32[2,16,1024]{2,1,0:T(8,128)S(1)}, f32[4,4,16,1024]{3,2,1,0:T(8,128)S(1)}, f32[4,4,16,1024]{3,2,1,0:T(8,128)S(1)}) custom-call(f32[4,4,16,1024]{3,2,1,0:T(8,128)} %steps_hbm.1, f32[4,4,16,1024]{3,2,1,0:T(8,128)} %changes_hbm.1, s32[2,8,512]{2,1,0:T(8,128)} %passive_hbm.1), custom_call_target="tpu_custom_call" | custom-call | flops 8000000000 | bytes 43000000 | tf_op jit(solution)/shard_map/gram/pallas_call | solution.py:397
  18.1 0.0 collective-permute-done.4.row_odd_ref
  18.1 0.0 collective-permute-done.5.row_even_ref
  18.2 0.0 collective-permute-done.odd_ref
  18.2 0.0 collective-permute-done.1.even_ref
  18.2 1.4 %sweeps.1 = (f32[4,16,1024]{2,1,0:T(8,128)S(1)}, f32[256,128]{1,0:T(8,128)S(1)}) custom-call(f32[4,16,1024]{2,1,0:T(8,128)S(1)} %get-tuple-element.18.u_ref, f32[3,16,1024]{2,1,0:T(8,128)S(1)} %collective-permute-done.odd_ref, f32[3,16,1024]{2,1,0:T(8,128)S(1)} %collective-permute-done.1.even_ref, f32[24,1024]{1,0:T(8,128)S(1)} %collective-permute-done.4.row_odd_ref, ...), custom_call_target="tpu_custom_call" | custom-call | tf_op jit(solution)/shard_map/sweeps/pallas_call | solution.py:418
  19.6 24.0 %all_to_all.11 = f32[256,1,128]{2,1,0:T(1,128)S(1)} all-to-all(f32[256,1,128]{2,1,0:T(1,128)S(1)} %bitcast.5), channel_id=1, replica_groups=mesh['slab'=16,'tile'=16] {'slab','tile'}, dimensions={0} | all-to-all | bytes 262144 | tf_op jit(solution)/shard_map/all_to_all | solution.py:428
  43.6 0.9 %combine.1 = f32[4,16,1024]{2,1,0:T(8,128)} custom-call(f32[256,128]{1,0:T(8,128)S(1)} %bitcast.4, f32[4,16,1024]{2,1,0:T(8,128)S(1)} %get-tuple-element.30.grad_ref, f32[4,4,16,1024]{3,2,1,0:T(8,128)S(1)} %get-tuple-element.26.steps_ref, f32[4,4,16,1024]{3,2,1,0:T(8,128)S(1)} %get-tuple-element.27.changes_ref), custom_call_target="tpu_custom_call" | custom-call | tf_op jit(solution)/shard_map/combine/pallas_call | solution.py:430
Async XLA Ops:
  1.2 7.3 %collective-permute-start.2 = (f32[8,1024]{1,0:T(8,128)S(1)}, f32[8,1024]{1,0:T(8,128)S(1)}, u32[]{:S(2)}, u32[]{:S(2)}) collective-permute-start(f32[8,1024]{1,0:T(8,128)S(1)} %get-tuple-element.21), channel_id=1, source_target_pairs={{0,240},{16,32},{32,16},{48,64},{64,48},{80,96},{96,80},{112,128},... | collective-permute-start | bytes 98312 | tf_op jit(solution)/shard_map/ppermute | solution.py:379
  7.0 3.1 %collective-permute-start.3 = (f32[8,1024]{1,0:T(8,128)S(1)}, f32[8,1024]{1,0:T(8,128)S(1)}, u32[]{:S(2)}, u32[]{:S(2)}) collective-permute-start(f32[8,1024]{1,0:T(8,128)S(1)} %get-tuple-element.22), channel_id=1, source_target_pairs={{0,16},{16,0},{32,48},{48,32},{64,80},{80,64},{96,112},{112,96},{1... | collective-permute-start | bytes 98312 | tf_op jit(solution)/shard_map/ppermute | solution.py:380
  7.0 11.1 %collective-permute-start = (f32[3,16,1024]{2,1,0:T(8,128)S(1)}, f32[3,16,1024]{2,1,0:T(8,128)S(1)}, u32[]{:S(2)}, u32[]{:S(2)}) collective-permute-start(f32[3,16,1024]{2,1,0:T(8,128)S(1)} %get-tuple-element.19), channel_id=1, source_target_pairs={{0,240},{16,32},{32,16},{48,64},{64,48},{80,96},{96,80},{112,128},... | collective-permute-start | bytes 589832 | tf_op jit(solution)/shard_map/ppermute | solution.py:381
  7.8 10.3 %collective-permute-start.1 = (f32[3,16,1024]{2,1,0:T(8,128)S(1)}, f32[3,16,1024]{2,1,0:T(8,128)S(1)}, u32[]{:S(2)}, u32[]{:S(2)}) collective-permute-start(f32[3,16,1024]{2,1,0:T(8,128)S(1)} %get-tuple-element.20), channel_id=1, source_target_pairs={{0,16},{16,0},{32,48},{48,32},{64,80},{80,64},{96,112},{112,96},{1... | collective-permute-start | bytes 589832 | tf_op jit(solution)/shard_map/ppermute | solution.py:382
  10.2 8.0 %collective-permute-start.4 = (f32[24,1024]{1,0:T(8,128)S(1)}, f32[24,1024]{1,0:T(8,128)S(1)}, u32[]{:S(2)}, u32[]{:S(2)}) collective-permute-start(f32[24,1024]{1,0:T(8,128)S(1)} %get-tuple-element.23), channel_id=1, source_target_pairs={{0,15},{1,2},{2,1},{3,4},{4,3},{5,6},{6,5},{7,8},{8,7},{9,10},{10,... | collective-permute-start | bytes 294920 | tf_op jit(solution)/shard_map/ppermute | solution.py:393
  13.9 4.3 %collective-permute-start.5 = (f32[24,1024]{1,0:T(8,128)S(1)}, f32[24,1024]{1,0:T(8,128)S(1)}, u32[]{:S(2)}, u32[]{:S(2)}) collective-permute-start(f32[24,1024]{1,0:T(8,128)S(1)} %get-tuple-element.24), channel_id=1, source_target_pairs={{0,1},{1,0},{2,3},{3,2},{4,5},{5,4},{6,7},{7,6},{8,9},{9,8},{10,11... | collective-permute-start | bytes 294920 | tf_op jit(solution)/shard_map/ppermute | solution.py:394

commit v5 on v4

--- a/solution.py
+++ b/solution.py
@@ -22,7 +22,6 @@
 SG = [2 * len(PAIRS) + n for n in range(MEM)]
 YG = [2 * len(PAIRS) + MEM + n for n in range(MEM)]
 SUMS = 32
-ROWS_SENT = 24
 
 VMEM = pl.BlockSpec(memory_space=pltpu.VMEM)
 HBM = pl.BlockSpec(memory_space=pltpu.HBM)
@@ -44,7 +43,9 @@
     dens_ref,
     arrived,
 ):
-    depth, rows, cols = u_ref.shape
+    depth, rows, cols = sens_ref.shape
+    width = cols // LANES
+    layer = rows * width
     slab_odd = lax.rem(lax.axis_index("slab"), 2)
     copies = [
         [
@@ -64,19 +65,27 @@
             copy.wait()
         bend = jnp.tanh(sharpness * (dens_ref[z] - threshold))
         slope = sharpness * (1.0 - bend * bend) / denominator
-        u_ref[z] = sens_ref[z] * slope / diagonal_value
+        value = sens_ref[z] * slope / diagonal_value
+        for row in range(0, rows, 8):
+            for part in range(width):
+                place = pl.ds(z * layer + row * width + part, 8, width)
+                u_ref[place, :] = value[row : row + 8, part * LANES : (part + 1) * LANES]
 
     for rim_ref, layers_ref, top in (
         (rim_odd_ref, odd_ref, slab_odd),
         (rim_even_ref, even_ref, 1 - slab_odd),
     ):
+
+        def put(first, count, z, row):
+            place = pl.ds(pl.multiple_of(z * layer + row * width, 8), count * width)
+            rim_ref[first * width : (first + count) * width, :] = u_ref[place, :]
+
         near, second = (depth - 1) * top, 1 + (depth - 3) * top
-        rim_ref[0:2, :] = u_ref[near, 0:2, :]
-        rim_ref[2:4, :] = u_ref[near, rows - 2 : rows, :]
-        rim_ref[4:5, :] = u_ref[second, 0:1, :]
-        rim_ref[5:6, :] = u_ref[second, rows - 1 : rows, :]
-        rim_ref[6:8, :] = jnp.zeros((2, cols), F32)
-        layers_ref[...] = u_ref[pl.ds(top, SWEEPS)]
+        put(0, 2, near, 0)
+        put(2, 2, near, rows - 2)
+        put(4, 1, second, 0)
+        put(5, 1, second, rows - 1)
+        layers_ref[...] = u_ref[pl.ds(pl.multiple_of(top * layer, 8), SWEEPS * layer), :]
 
 
 def gram_kernel(
@@ -153,15 +162,14 @@
     tile_odd = lax.rem(lax.axis_index("tile"), 2)
 
     def pack(low_ref, high_ref, out_ref, top):
+        start = rows - 3 if top else 0
         for z in range(depth):
-            start = rows - 3 if top else 0
-            out_ref[3 * z : 3 * z + 3, :] = u_ref[z, start : start + 3, :]
+            out_ref[3 * z : 3 * z + 3] = u_ref[z, start : start + 3]
         near, second = (2, 5) if top else (0, 4)
-        out_ref[12:14, :] = low_ref[near : near + 2, :]
-        out_ref[14:16, :] = high_ref[near : near + 2, :]
-        out_ref[16:17, :] = low_ref[second : second + 1, :]
-        out_ref[17:18, :] = high_ref[second : second + 1, :]
-        out_ref[18:24, :] = jnp.zeros((6, out_ref.shape[1]), F32)
+        out_ref[12:14] = low_ref[near : near + 2]
+        out_ref[14:16] = high_ref[near : near + 2]
+        out_ref[16] = low_ref[second]
+        out_ref[17] = high_ref[second]
 
     for parity in range(2):
         for top in range(2):
@@ -188,9 +196,10 @@
     start_ref,
     one_ref,
     two_ref,
+    last_ref,
     total_ref,
 ):
-    depth, rows, cols = u_ref.shape
+    depth, rows, width = u_ref.shape[:3]
     slab, tile = lax.axis_index("slab"), lax.axis_index("tile")
     slab_odd, tile_odd = lax.rem(slab, 2), lax.rem(tile, 2)
     inside = {
@@ -200,17 +209,15 @@
         "high_y": (tile < lax.axis_size("tile") - 1).astype(F32),
     }
 
-    for z in range(depth):
-        start_ref[3 + z, 8 : 8 + rows, :] = u_ref[z]
+    start_ref[3 : 3 + depth, 3 : 3 + rows] = u_ref[...]
 
     def layers(low_ref, high_ref):
-        for z in range(3):
-            start_ref[z, 8 : 8 + rows, :] = low_ref[z] * inside["low_z"]
-            start_ref[7 + z, 8 : 8 + rows, :] = high_ref[z] * inside["high_z"]
+        start_ref[0:3, 3 : 3 + rows] = low_ref[...] * inside["low_z"]
+        start_ref[3 + depth :, 3 : 3 + rows] = high_ref[...] * inside["high_z"]
 
     def edge(from_ref, first, count, z, factor, high):
-        to = 8 + rows if high else 8 - count
-        start_ref[z, to : to + count, :] = from_ref[first : first + count, :] * factor
+        to = 3 + rows if high else 3 - count
+        start_ref[z, to : to + count] = from_ref[first : first + count] * factor
 
     def beside(from_ref, high):
         factor = inside["high_y" if high else "low_y"]
@@ -218,9 +225,9 @@
             edge(from_ref, 3 * z, 3, 3 + z, factor, high)
         low_factor, high_factor = factor * inside["low_z"], factor * inside["high_z"]
         edge(from_ref, 12, 2, 2, low_factor, high)
-        edge(from_ref, 14, 2, 7, high_factor, high)
+        edge(from_ref, 14, 2, 3 + depth, high_factor, high)
         edge(from_ref, 16, 1, 1, low_factor, high)
-        edge(from_ref, 17, 1, 8, high_factor, high)
+        edge(from_ref, 17, 1, 4 + depth, high_factor, high)
 
     for parity in range(2):
 
@@ -233,58 +240,58 @@
             beside(row_odd_ref, parity == 1)
             beside(row_even_ref, parity == 0)
 
-    column = lax.broadcasted_iota(jnp.int32, (8, cols), 1)
-    first, last = column == 0, column == cols - 1
-
-    def relax(from_ref, z, row):
-        here = from_ref[z, row : row + 8, :]
-        around = from_ref[z - 1, row : row + 8, :] + from_ref[z + 1, row : row + 8, :]
-        if row == 0:
-            below = pltpu.roll(here, 1, 0)
-        else:
-            below = from_ref[z, row - 1 : row + 7, :]
-        if row == rows + 8:
-            above = pltpu.roll(here, 7, 0)
-        else:
-            above = from_ref[z, row + 1 : row + 9, :]
-        around += below + above
-        around += jnp.where(first, 0.0, pltpu.roll(here, 1, 1))
-        around += jnp.where(last, 0.0, pltpu.roll(here, cols - 1, 1))
-        return start_ref[z, row : row + 8, :] + coupling * around
-
-    def outside(z, row):
-        factor = None
+    lane = lax.broadcasted_iota(jnp.int32, (width, LANES), 1)
+    part = lax.broadcasted_iota(jnp.int32, (width, LANES), 0)
+    lane_first, lane_last = lane == 0, lane == LANES - 1
+    first, last = lane_first & (part == 0), lane_last & (part == width - 1)
+
+    def relax(from_ref, z, y):
+        here = from_ref[z, y]
+        around = from_ref[z - 1, y] + from_ref[z + 1, y]
+        around += from_ref[z, y - 1] + from_ref[z, y + 1]
+        before, after = pltpu.roll(here, 1, 1), pltpu.roll(here, LANES - 1, 1)
+        before = jnp.where(lane_first, pltpu.roll(before, 1, 0), before)
+        after = jnp.where(lane_last, pltpu.roll(after, width - 1, 0), after)
+        around += jnp.where(first, 0.0, before) + jnp.where(last, 0.0, after)
+        return start_ref[z, y] + coupling * around
+
+    def factors(z, y):
         if z < 3:
-            factor = inside["low_z"]
-        if z > 6:
-            factor = inside["high_z"]
-        edge_factor = inside["low_y"] if row < 8 else inside["high_y"] if row >= 8 + rows else None
-        if factor is None or edge_factor is None:
-            return edge_factor if factor is None else factor
-        return factor * edge_factor
+            yield inside["low_z"]
+        if z >= 3 + depth:
+            yield inside["high_z"]
+        if y < 3:
+            yield inside["low_y"]
+        if y >= 3 + rows:
+            yield inside["high_y"]
 
     def sweep(from_ref, to_ref, reach):
-        for z in range(3 - reach, 7 + reach):
-            beyond = max(3 - z, z - 6, 0)
-            wide = reach - beyond > 0
-            for row in range(0 if wide else 8, 8 + rows + (8 if wide else 0), 8):
-                value = relax(from_ref, z, row)
-                factor = outside(z, row)
-                to_ref[z, row : row + 8, :] = value if factor is None else value * factor
+        for z in range(3 - reach, 3 + depth + reach):
+            wide = reach - max(3 - z, z - 2 - depth, 0)
+            for y in range(3 - wide, 3 + rows + wide):
+                value = relax(from_ref, z, y)
+                for factor in factors(z, y):
+                    value *= factor
+                to_ref[z, y] = value
 
     sweep(start_ref, one_ref, 2)
     sweep(one_ref, two_ref, 1)
+    for z in range(depth):
+        for y in range(rows):
+            place = (z * rows + y) * width
+            last_ref[place : place + width, :] = relax(two_ref, 3 + z, 3 + y)
 
     sums = [jnp.zeros((8, LANES), F32) for _ in range(2 * MEM)]
     for z in range(depth):
         for row in range(0, rows, 8):
-            value = relax(two_ref, 3 + z, 8 + row) * keep_ref[z // 2, row : row + 8, :]
-            grad_ref[z, row : row + 8, :] = value
-            for col in range(0, cols, LANES):
-                piece = value[:, col : col + LANES]
+            for part in range(width):
+                block = slice(row, row + 8), slice(part * LANES, (part + 1) * LANES)
+                value = last_ref[pl.ds((z * rows + row) * width + part, 8, width), :]
+                value *= keep_ref[z // 2, *block]
+                grad_ref[z, *block] = value
                 for i in range(MEM):
-                    sums[i] += steps_ref[i, z, row : row + 8, col : col + LANES] * piece
-                    sums[MEM + i] += changes_ref[i, z, row : row + 8, col : col + LANES] * piece
+                    sums[i] += steps_ref[i, z, *block] * value
+                    sums[MEM + i] += changes_ref[i, z, *block] * value
     done = 2 * len(PAIRS)
     total_ref[0:done, :] = sums_ref[0:done, :]
     for n, value in enumerate(sums):
@@ -348,7 +355,8 @@
 
 def swaps(count):
     even = [(i, i ^ 1) for i in range(count)]
-    odd = [(i, (i + 1) % count if i % 2 else (i - 1) % count) for i in range(count)]
+    ends = {0: 0, count - 1: count - 1}
+    odd = [(i, ends.get(i, i + 1 if i % 2 else i - 1)) for i in range(count)]
     return odd, even
 
 
@@ -356,14 +364,16 @@
     shape = sensitivity.shape
     depth, rows, cols = shape
     like = jax.ShapeDtypeStruct
-    layers, rim, edges = (
-        like(size, F32) for size in ((SWEEPS, rows, cols), (8, cols), (ROWS_SENT, cols))
+    width = cols // LANES
+    lines, layers, rim = (
+        like((count * width, LANES), F32) for count in (depth * rows, SWEEPS * rows, 6)
     )
+    edges = like((3 * depth + 6, width, LANES), F32)
     devices = lax.axis_size("slab") * lax.axis_size("tile")
 
     u, rim_odd, rim_even, odd, even = pl.pallas_call(
         weight_kernel,
-        out_shape=(like(shape, F32), rim, rim, layers, layers),
+        out_shape=(lines, rim, rim, layers, layers),
         in_specs=[HBM] * 2,
         out_specs=[VMEM] * 5,
         scratch_shapes=[
@@ -374,6 +384,10 @@
         compiler_params=kernel_params(8),
         name="weights",
     )(in_hbm(sensitivity), in_hbm(filtered_density))
+
+    u = u.reshape(depth, rows, width, LANES)
+    rim_odd, rim_even = (array.reshape(6, width, LANES) for array in (rim_odd, rim_even))
+    odd, even = (array.reshape(SWEEPS, rows, width, LANES) for array in (odd, even))
 
     odd_pairs, even_pairs = swaps(lax.axis_size("slab"))
     rim_odd = lax.ppermute(rim_odd, "slab", odd_pairs)
@@ -414,18 +428,24 @@
         name="gram",
     )(in_hbm(history_steps), in_hbm(history_changes), in_hbm(passive_blocks))
 
-    padded = pltpu.VMEM((depth + 6, rows + 16, cols), F32)
+    padded = pltpu.VMEM((depth + 6, rows + 6, width, LANES), F32)
     gradient, line = pl.pallas_call(
         sweep_kernel,
         out_shape=(like(shape, F32), like((devices, LANES), F32)),
         in_specs=[VMEM] * 9,
         out_specs=[VMEM] * 2,
-        scratch_shapes=[padded, padded, padded, pltpu.VMEM((SUMS, LANES), F32)],
+        scratch_shapes=[
+            padded,
+            padded,
+            padded,
+            pltpu.VMEM((depth * rows * width, LANES), F32),
+            pltpu.VMEM((SUMS, LANES), F32),
+        ],
         compiler_params=kernel_params(16),
         name="sweeps",
     )(u, odd, even, row_odd, row_even, keep, steps, changes, sums)
 
-    lines = lax.all_to_all(line, ("slab", "tile"), 0, 0, tiled=True)
+    received = lax.all_to_all(line, ("slab", "tile"), 0, 0, tiled=True)
 
     return pl.pallas_call(
         combine_kernel,
@@ -435,7 +455,7 @@
         scratch_shapes=[pltpu.VMEM(shape, F32), pltpu.SemaphoreType.DMA((depth,))],
         compiler_params=kernel_params(8),
         name="combine",
-    )(lines, gradient, steps, changes)
+    )(received, gradient, steps, changes)
 
 
 def solution(mesh):

time: 44.7 us -> 48.1 us (1.076)
  blocking collectives: 24 us -> 27.7 us
  starting transfers between devices: 13.1 us -> 14.7 us
  waiting for transfers between devices: 1.6 us -> 0.02 us
    ppermute x1, starting transfers between devices: 5.85 us -> 0.66 us  [per_device(): rim_odd = lax.ppermute(rim_odd, 'slab', odd_pairs)]
    ppermute x1, starting transfers between devices: 0.01 us -> 4.58 us  [per_device(): rim_even = lax.ppermute(rim_even, 'slab', even_pairs)]
    all_to_all x1, blocking collectives: 24 us -> 27.7 us  [per_device(): received = lax.all_to_all(line, ('slab', 'tile'), 0, 0, tiled=True)]
    ppermute x1, starting transfers between devices: 0.67 us -> 3.45 us  [per_device(): even = lax.ppermute(even, 'slab', even_pairs)]
    ppermute x1, starting transfers between devices: 2.03 us -> 0.09 us  [per_device(): row_even = lax.ppermute(row_even, 'tile', even_pairs)]
    ppermute x1, waiting for transfers between devices: 1.59 us -> 0.01 us  [per_device(): rim_even = lax.ppermute(rim_even, 'slab', even_pairs)]
    ppermute x1, starting transfers between devices: 3.73 us -> 5.23 us  [per_device(): row_odd = lax.ppermute(row_odd, 'tile', odd_pairs)]
  transfers between devices with their start and end apart: 6 -> 6, of which waited for: 1 -> 0; matrix products, arithmetic and copies ran while one was open for 0% -> 0% of each run, Pallas kernels for 5% -> 5%
where the time goes in v5:
time: 48.1 us; the launch traced here: 47.9 us
  blocking collectives  27.7 us (58%)
  starting transfers between devices  14.7 us (31%)
  Pallas kernels  5.43 us (11%)
    all_to_all x1, blocking collectives, per_device(): received = lax.all_to_all(line, ('slab', 'tile'), 0, 0, tiled=True)  27.7 us
    ppermute x1, starting transfers between devices, per_device(): row_odd = lax.ppermute(row_odd, 'tile', odd_pairs)  5.23 us
    ppermute x1, starting transfers between devices, per_device(): rim_even = lax.ppermute(rim_even, 'slab', even_pairs)  4.58 us
    ppermute x1, starting transfers between devices, per_device(): even = lax.ppermute(even, 'slab', even_pairs)  3.45 us
    pallas_call x1, Pallas kernels, per_device(): pl.pallas_call(gram_kernel, out_shape=(like((SUMS, LANES), F32), like((de...  2.2 us
    pallas_call x1, Pallas kernels, per_device(): pl.pallas_call(weight_kernel, out_shape=(lines, rim, rim, layers, layers)...  1.18 us
    pallas_call x1, Pallas kernels, per_device(): pl.pallas_call(sweep_kernel, out_shape=(like(shape, F32), like((devices,...  1.08 us
  transfers between devices with their start and end apart: 6, of which 0 were waited for; matrix products, arithmetic and copies ran while one was open for 0% of the time, Pallas kernels for 5%

profile of v5, /device:TPU:1, one launch (start us, length us, event | category | flops | bytes accessed | tf_op | source)
XLA Modules:
  0.0 47.9 jit_solution(15239336592269498008)
XLA Ops:
  0.0 1.2 %weights.1 = (f32[512,128]{1,0:T(8,128)S(1)}, f32[48,128]{1,0:T(8,128)S(1)}, f32[48,128]{1,0:T(8,128)S(1)}, f32[384,128]{1,0:T(8,128)S(1)}, f32[384,128]{1,0:T(8,128)S(1)}) custom-call(f32[4,16,1024]{2,1,0:T(8,128)} %sens_hbm.1, f32[4,16,1024]{2,1,0:T(8,128)} %dens_hbm.1), custom_call_target="tpu_custom_call" | custom-call | tf_op jit(solution)/shard_map/weights/pallas_call | solution.py:374
  1.2 0.7 %collective-permute-start.2 = (f32[6,8,128]{2,1,0:T(8,128)S(1)}, f32[6,8,128]{2,1,0:T(8,128)S(1)}, u32[]{:S(2)}, u32[]{:S(2)}) collective-permute-start(f32[6,8,128]{2,1,0:T(8,128)S(1)} %bitcast.16), channel_id=1, source_target_pairs={{0,0},{16,32},{32,16},{48,64},{64,48},{80,96},{96,80},{112,128},{1... | collective-permute-start | bytes 73736 | tf_op jit(solution)/shard_map/ppermute | solution.py:393
  1.9 4.6 %collective-permute-start.3 = (f32[6,8,128]{2,1,0:T(8,128)S(1)}, f32[6,8,128]{2,1,0:T(8,128)S(1)}, u32[]{:S(2)}, u32[]{:S(2)}) collective-permute-start(f32[6,8,128]{2,1,0:T(8,128)S(1)} %bitcast.15), channel_id=1, source_target_pairs={{0,16},{16,0},{32,48},{48,32},{64,80},{80,64},{96,112},{112,96},{1... | collective-permute-start | bytes 73736 | tf_op jit(solution)/shard_map/ppermute | solution.py:394
  6.4 0.7 %collective-permute-start = (f32[3,16,8,128]{3,2,1,0:T(8,128)S(1)}, f32[3,16,8,128]{3,2,1,0:T(8,128)S(1)}, u32[]{:S(2)}, u32[]{:S(2)}) collective-permute-start(f32[3,16,8,128]{3,2,1,0:T(8,128)S(1)} %bitcast.14), channel_id=1, source_target_pairs={{0,0},{16,32},{32,16},{48,64},{64,48},{80,96},{96,80},{112,128},{1... | collective-permute-start | bytes 589832 | tf_op jit(solution)/shard_map/ppermute | solution.py:395
  7.1 3.5 %collective-permute-start.1 = (f32[3,16,8,128]{3,2,1,0:T(8,128)S(1)}, f32[3,16,8,128]{3,2,1,0:T(8,128)S(1)}, u32[]{:S(2)}, u32[]{:S(2)}) collective-permute-start(f32[3,16,8,128]{3,2,1,0:T(8,128)S(1)} %bitcast.13), channel_id=1, source_target_pairs={{0,16},{16,0},{32,48},{48,32},{64,80},{80,64},{96,112},{112,96},{1... | collective-permute-start | bytes 589832 | tf_op jit(solution)/shard_map/ppermute | solution.py:396
  10.6 0.0 collective-permute-done.2.odd_ref
  10.6 0.0 collective-permute-done.3.even_ref
  10.6 5.2 %collective-permute-start.4 = (f32[18,8,128]{2,1,0:T(8,128)S(1)}, f32[18,8,128]{2,1,0:T(8,128)S(1)}, u32[]{:S(2)}, u32[]{:S(2)}) collective-permute-start(f32[18,8,128]{2,1,0:T(8,128)S(1)} %get-tuple-element.23), channel_id=1, source_target_pairs={{0,0},{1,2},{2,1},{3,4},{4,3},{5,6},{6,5},{7,8},{8,7},{9,10},{10,9... | collective-permute-start | bytes 221192 | tf_op jit(solution)/shard_map/ppermute | solution.py:407
  15.8 0.1 collective-permute-start.5
  15.9 2.2 %gram.1 = (f32[32,128]{1,0:T(8,128)S(1)}, f32[2,16,1024]{2,1,0:T(8,128)S(1)}, f32[4,4,16,1024]{3,2,1,0:T(8,128)S(1)}, f32[4,4,16,1024]{3,2,1,0:T(8,128)S(1)}) custom-call(f32[4,4,16,1024]{3,2,1,0:T(8,128)} %steps_hbm.1, f32[4,4,16,1024]{3,2,1,0:T(8,128)} %changes_hbm.1, s32[2,8,512]{2,1,0:T(8,128)} %passive_hbm.1), custom_call_target="tpu_custom_call" | custom-call | flops 8000000000 | bytes 43000000 | tf_op jit(solution)/shard_map/gram/pallas_call | solution.py:411
  18.1 0.0 collective-permute-done.4.row_odd_ref
  18.2 0.0 collective-permute-done.5.row_even_ref
  18.2 0.0 collective-permute-done.odd_ref
  18.2 0.0 collective-permute-done.1.even_ref
  18.2 1.1 %sweeps.1 = (f32[4,16,1024]{2,1,0:T(8,128)S(1)}, f32[256,128]{1,0:T(8,128)S(1)}) custom-call(f32[4,16,8,128]{3,2,1,0:T(8,128)S(1)} %bitcast.10, f32[3,16,8,128]{3,2,1,0:T(8,128)S(1)} %collective-permute-done.odd_ref, f32[3,16,8,128]{3,2,1,0:T(8,128)S(1)} %collective-permute-done.1.even_ref, f32[18,8,128]{2,1,0:T(8,128)S(1)} %collective-permute-done.4.row_odd_ref, ...), custom_call_target="tpu_custom_call" | custom-call | tf_op jit(solution)/shard_map/sweeps/pallas_call | solution.py:432
  19.3 27.7 %all_to_all.11 = f32[256,1,128]{2,1,0:T(1,128)S(1)} all-to-all(f32[256,1,128]{2,1,0:T(1,128)S(1)} %bitcast.12), channel_id=1, replica_groups=mesh['slab'=16,'tile'=16] {'slab','tile'}, dimensions={0} | all-to-all | bytes 262144 | tf_op jit(solution)/shard_map/all_to_all | solution.py:448
  46.9 0.9 %combine.1 = f32[4,16,1024]{2,1,0:T(8,128)} custom-call(f32[256,128]{1,0:T(8,128)S(1)} %bitcast.11, f32[4,16,1024]{2,1,0:T(8,128)S(1)} %get-tuple-element.30.grad_ref, f32[4,4,16,1024]{3,2,1,0:T(8,128)S(1)} %get-tuple-element.26.steps_ref, f32[4,4,16,1024]{3,2,1,0:T(8,128)S(1)} %get-tuple-element.27.changes_ref), custom_call_target="tpu_custom_call" | custom-call | tf_op jit(solution)/shard_map/combine/pallas_call | solution.py:450
  (1 shorter events, 0.0 us)
Async XLA Ops:
  1.2 9.4 %collective-permute-start.2 = (f32[6,8,128]{2,1,0:T(8,128)S(1)}, f32[6,8,128]{2,1,0:T(8,128)S(1)}, u32[]{:S(2)}, u32[]{:S(2)}) collective-permute-start(f32[6,8,128]{2,1,0:T(8,128)S(1)} %bitcast.16), channel_id=1, source_target_pairs={{0,0},{16,32},{32,16},{48,64},{64,48},{80,96},{96,80},{112,128},{1... | collective-permute-start | bytes 73736 | tf_op jit(solution)/shard_map/ppermute | solution.py:393
  1.9 8.7 %collective-permute-start.3 = (f32[6,8,128]{2,1,0:T(8,128)S(1)}, f32[6,8,128]{2,1,0:T(8,128)S(1)}, u32[]{:S(2)}, u32[]{:S(2)}) collective-permute-start(f32[6,8,128]{2,1,0:T(8,128)S(1)} %bitcast.15), channel_id=1, source_target_pairs={{0,16},{16,0},{32,48},{48,32},{64,80},{80,64},{96,112},{112,96},{1... | collective-permute-start | bytes 73736 | tf_op jit(solution)/shard_map/ppermute | solution.py:394
  6.4 11.7 %collective-permute-start = (f32[3,16,8,128]{3,2,1,0:T(8,128)S(1)}, f32[3,16,8,128]{3,2,1,0:T(8,128)S(1)}, u32[]{:S(2)}, u32[]{:S(2)}) collective-permute-start(f32[3,16,8,128]{3,2,1,0:T(8,128)S(1)} %bitcast.14), channel_id=1, source_target_pairs={{0,0},{16,32},{32,16},{48,64},{64,48},{80,96},{96,80},{112,128},{1... | collective-permute-start | bytes 589832 | tf_op jit(solution)/shard_map/ppermute | solution.py:395
  7.1 11.1 %collective-permute-start.1 = (f32[3,16,8,128]{3,2,1,0:T(8,128)S(1)}, f32[3,16,8,128]{3,2,1,0:T(8,128)S(1)}, u32[]{:S(2)}, u32[]{:S(2)}) collective-permute-start(f32[3,16,8,128]{3,2,1,0:T(8,128)S(1)} %bitcast.13), channel_id=1, source_target_pairs={{0,16},{16,0},{32,48},{48,32},{64,80},{80,64},{96,112},{112,96},{1... | collective-permute-start | bytes 589832 | tf_op jit(solution)/shard_map/ppermute | solution.py:396
  10.6 7.6 %collective-permute-start.4 = (f32[18,8,128]{2,1,0:T(8,128)S(1)}, f32[18,8,128]{2,1,0:T(8,128)S(1)}, u32[]{:S(2)}, u32[]{:S(2)}) collective-permute-start(f32[18,8,128]{2,1,0:T(8,128)S(1)} %get-tuple-element.23), channel_id=1, source_target_pairs={{0,0},{1,2},{2,1},{3,4},{4,3},{5,6},{6,5},{7,8},{8,7},{9,10},{10,9... | collective-permute-start | bytes 221192 | tf_op jit(solution)/shard_map/ppermute | solution.py:407
  15.8 2.3 %collective-permute-start.5 = (f32[18,8,128]{2,1,0:T(8,128)S(1)}, f32[18,8,128]{2,1,0:T(8,128)S(1)}, u32[]{:S(2)}, u32[]{:S(2)}) collective-permute-start(f32[18,8,128]{2,1,0:T(8,128)S(1)} %get-tuple-element.24), channel_id=1, source_target_pairs={{0,1},{1,0},{2,3},{3,2},{4,5},{5,4},{6,7},{7,6},{8,9},{9,8},{10,11... | collective-permute-start | bytes 221192 | tf_op jit(solution)/shard_map/ppermute | solution.py:408

commit v6 on v5

--- a/solution.py
+++ b/solution.py
@@ -355,8 +355,7 @@
 
 def swaps(count):
     even = [(i, i ^ 1) for i in range(count)]
-    ends = {0: 0, count - 1: count - 1}
-    odd = [(i, ends.get(i, i + 1 if i % 2 else i - 1)) for i in range(count)]
+    odd = [(i, (i + 1) % count if i % 2 else (i - 1) % count) for i in range(count)]
     return odd, even
 
 

time: 48.1 us -> 43.9 us (0.913)
  blocking collectives: 27.7 us -> 23.7 us
  starting transfers between devices: 14.7 us -> 13.1 us
  waiting for transfers between devices: 0.02 us -> 1.51 us
    ppermute x1, starting transfers between devices: 0.66 us -> 5.85 us  [per_device(): rim_odd = lax.ppermute(rim_odd, 'slab', odd_pairs)]
    ppermute x1, starting transfers between devices: 4.58 us -> 0.01 us  [per_device(): rim_even = lax.ppermute(rim_even, 'slab', even_pairs)]
    all_to_all x1, blocking collectives: 27.7 us -> 23.7 us  [per_device(): received = lax.all_to_all(line, ('slab', 'tile'), 0, 0, tiled=True)]
    ppermute x1, starting transfers between devices: 3.45 us -> 0.67 us  [per_device(): even = lax.ppermute(even, 'slab', even_pairs)]
    ppermute x1, starting transfers between devices: 0.09 us -> 2.12 us  [per_device(): row_even = lax.ppermute(row_even, 'tile', even_pairs)]
    ppermute x1, starting transfers between devices: 5.23 us -> 3.64 us  [per_device(): row_odd = lax.ppermute(row_odd, 'tile', odd_pairs)]
    ppermute x1, waiting for transfers between devices: 0.01 us -> 1.5 us  [per_device(): rim_even = lax.ppermute(rim_even, 'slab', even_pairs)]
  transfers between devices with their start and end apart: 6 -> 6, of which waited for: 0 -> 1; matrix products, arithmetic and copies ran while one was open for 0% -> 0% of each run, Pallas kernels for 5% -> 5%
where the time goes in v6:
time: 43.9 us; the launch traced here: 43.7 us
  blocking collectives  23.7 us (54%)
  starting transfers between devices  13.1 us (30%)
  Pallas kernels  5.42 us (12%)
  waiting for transfers between devices  1.51 us (3%)
    all_to_all x1, blocking collectives, per_device(): received = lax.all_to_all(line, ('slab', 'tile'), 0, 0, tiled=True)  23.7 us
    ppermute x1, starting transfers between devices, per_device(): rim_odd = lax.ppermute(rim_odd, 'slab', odd_pairs)  5.85 us
    ppermute x1, starting transfers between devices, per_device(): row_odd = lax.ppermute(row_odd, 'tile', odd_pairs)  3.64 us
    pallas_call x1, Pallas kernels, per_device(): pl.pallas_call(gram_kernel, out_shape=(like((SUMS, LANES), F32), like((de...  2.2 us
    ppermute x1, starting transfers between devices, per_device(): row_even = lax.ppermute(row_even, 'tile', even_pairs)  2.12 us
    ppermute x1, waiting for transfers between devices, per_device(): rim_even = lax.ppermute(rim_even, 'slab', even_pairs)  1.5 us
    pallas_call x1, Pallas kernels, per_device(): pl.pallas_call(weight_kernel, out_shape=(lines, rim, rim, layers, layers)...  1.18 us
    pallas_call x1, Pallas kernels, per_device(): pl.pallas_call(sweep_kernel, out_shape=(like(shape, F32), like((devices,...  1.08 us
  transfers between devices with their start and end apart: 6, of which 1 were waited for; matrix products, arithmetic and copies ran while one was open for 0% of the time, Pallas kernels for 5%

profile of v6, /device:TPU:1, one launch (start us, length us, event | category | flops | bytes accessed | tf_op | source)
XLA Modules:
  0.0 43.7 jit_solution(18379651849001881127)
XLA Ops:
  0.0 1.2 %weights.1 = (f32[512,128]{1,0:T(8,128)S(1)}, f32[48,128]{1,0:T(8,128)S(1)}, f32[48,128]{1,0:T(8,128)S(1)}, f32[384,128]{1,0:T(8,128)S(1)}, f32[384,128]{1,0:T(8,128)S(1)}) custom-call(f32[4,16,1024]{2,1,0:T(8,128)} %sens_hbm.1, f32[4,16,1024]{2,1,0:T(8,128)} %dens_hbm.1), custom_call_target="tpu_custom_call" | custom-call | tf_op jit(solution)/shard_map/weights/pallas_call | solution.py:373
  1.2 5.8 %collective-permute-start.2 = (f32[6,8,128]{2,1,0:T(8,128)S(1)}, f32[6,8,128]{2,1,0:T(8,128)S(1)}, u32[]{:S(2)}, u32[]{:S(2)}) collective-permute-start(f32[6,8,128]{2,1,0:T(8,128)S(1)} %bitcast.16), channel_id=1, source_target_pairs={{0,240},{16,32},{32,16},{48,64},{64,48},{80,96},{96,80},{112,128},... | collective-permute-start | bytes 73736 | tf_op jit(solution)/shard_map/ppermute | solution.py:392
  7.0 0.0 collective-permute-start.3
  7.0 0.8 %collective-permute-start = (f32[3,16,8,128]{3,2,1,0:T(8,128)S(1)}, f32[3,16,8,128]{3,2,1,0:T(8,128)S(1)}, u32[]{:S(2)}, u32[]{:S(2)}) collective-permute-start(f32[3,16,8,128]{3,2,1,0:T(8,128)S(1)} %bitcast.14), channel_id=1, source_target_pairs={{0,240},{16,32},{32,16},{48,64},{64,48},{80,96},{96,80},{112,128},... | collective-permute-start | bytes 589832 | tf_op jit(solution)/shard_map/ppermute | solution.py:394
  7.8 0.7 %collective-permute-start.1 = (f32[3,16,8,128]{3,2,1,0:T(8,128)S(1)}, f32[3,16,8,128]{3,2,1,0:T(8,128)S(1)}, u32[]{:S(2)}, u32[]{:S(2)}) collective-permute-start(f32[3,16,8,128]{3,2,1,0:T(8,128)S(1)} %bitcast.13), channel_id=1, source_target_pairs={{0,16},{16,0},{32,48},{48,32},{64,80},{80,64},{96,112},{112,96},{1... | collective-permute-start | bytes 589832 | tf_op jit(solution)/shard_map/ppermute | solution.py:395
  8.5 0.0 collective-permute-done.2.odd_ref
  8.5 1.5 %collective-permute-done.3.even_ref = f32[6,8,128]{2,1,0:T(8,128)S(1)} collective-permute-done((f32[6,8,128]{2,1,0:T(8,128)S(1)}, f32[6,8,128]{2,1,0:T(8,128)S(1)}, u32[]{:S(2)}, u32[]{:S(2)}) %collective-permute-start.3) | collective-permute-done | bytes 24608 | tf_op jit(solution)/shard_map/ppermute | solution.py:393
  10.0 3.6 %collective-permute-start.4 = (f32[18,8,128]{2,1,0:T(8,128)S(1)}, f32[18,8,128]{2,1,0:T(8,128)S(1)}, u32[]{:S(2)}, u32[]{:S(2)}) collective-permute-start(f32[18,8,128]{2,1,0:T(8,128)S(1)} %get-tuple-element.23), channel_id=1, source_target_pairs={{0,15},{1,2},{2,1},{3,4},{4,3},{5,6},{6,5},{7,8},{8,7},{9,10},{10,... | collective-permute-start | bytes 221192 | tf_op jit(solution)/shard_map/ppermute | solution.py:406
  13.7 2.1 %collective-permute-start.5 = (f32[18,8,128]{2,1,0:T(8,128)S(1)}, f32[18,8,128]{2,1,0:T(8,128)S(1)}, u32[]{:S(2)}, u32[]{:S(2)}) collective-permute-start(f32[18,8,128]{2,1,0:T(8,128)S(1)} %get-tuple-element.24), channel_id=1, source_target_pairs={{0,1},{1,0},{2,3},{3,2},{4,5},{5,4},{6,7},{7,6},{8,9},{9,8},{10,11... | collective-permute-start | bytes 221192 | tf_op jit(solution)/shard_map/ppermute | solution.py:407
  15.8 2.2 %gram.1 = (f32[32,128]{1,0:T(8,128)S(1)}, f32[2,16,1024]{2,1,0:T(8,128)S(1)}, f32[4,4,16,1024]{3,2,1,0:T(8,128)S(1)}, f32[4,4,16,1024]{3,2,1,0:T(8,128)S(1)}) custom-call(f32[4,4,16,1024]{3,2,1,0:T(8,128)} %steps_hbm.1, f32[4,4,16,1024]{3,2,1,0:T(8,128)} %changes_hbm.1, s32[2,8,512]{2,1,0:T(8,128)} %passive_hbm.1), custom_call_target="tpu_custom_call" | custom-call | flops 8000000000 | bytes 43000000 | tf_op jit(solution)/shard_map/gram/pallas_call | solution.py:410
  18.0 0.0 collective-permute-done.4.row_odd_ref
  18.0 0.0 collective-permute-done.5.row_even_ref
  18.0 0.0 collective-permute-done.odd_ref
  18.0 0.0 collective-permute-done.1.even_ref
  18.0 1.1 %sweeps.1 = (f32[4,16,1024]{2,1,0:T(8,128)S(1)}, f32[256,128]{1,0:T(8,128)S(1)}) custom-call(f32[4,16,8,128]{3,2,1,0:T(8,128)S(1)} %bitcast.10, f32[3,16,8,128]{3,2,1,0:T(8,128)S(1)} %collective-permute-done.odd_ref, f32[3,16,8,128]{3,2,1,0:T(8,128)S(1)} %collective-permute-done.1.even_ref, f32[18,8,128]{2,1,0:T(8,128)S(1)} %collective-permute-done.4.row_odd_ref, ...), custom_call_target="tpu_custom_call" | custom-call | tf_op jit(solution)/shard_map/sweeps/pallas_call | solution.py:431
  19.1 23.7 %all_to_all.11 = f32[256,1,128]{2,1,0:T(1,128)S(1)} all-to-all(f32[256,1,128]{2,1,0:T(1,128)S(1)} %bitcast.12), channel_id=1, replica_groups=mesh['slab'=16,'tile'=16] {'slab','tile'}, dimensions={0} | all-to-all | bytes 262144 | tf_op jit(solution)/shard_map/all_to_all | solution.py:447
  42.8 0.9 %combine.1 = f32[4,16,1024]{2,1,0:T(8,128)} custom-call(f32[256,128]{1,0:T(8,128)S(1)} %bitcast.11, f32[4,16,1024]{2,1,0:T(8,128)S(1)} %get-tuple-element.30.grad_ref, f32[4,4,16,1024]{3,2,1,0:T(8,128)S(1)} %get-tuple-element.26.steps_ref, f32[4,4,16,1024]{3,2,1,0:T(8,128)S(1)} %get-tuple-element.27.changes_ref), custom_call_target="tpu_custom_call" | custom-call | tf_op jit(solution)/shard_map/combine/pallas_call | solution.py:449
  (1 shorter events, 0.0 us)
Async XLA Ops:
  1.2 7.3 %collective-permute-start.2 = (f32[6,8,128]{2,1,0:T(8,128)S(1)}, f32[6,8,128]{2,1,0:T(8,128)S(1)}, u32[]{:S(2)}, u32[]{:S(2)}) collective-permute-start(f32[6,8,128]{2,1,0:T(8,128)S(1)} %bitcast.16), channel_id=1, source_target_pairs={{0,240},{16,32},{32,16},{48,64},{64,48},{80,96},{96,80},{112,128},... | collective-permute-start | bytes 73736 | tf_op jit(solution)/shard_map/ppermute | solution.py:392
  7.0 3.0 %collective-permute-start.3 = (f32[6,8,128]{2,1,0:T(8,128)S(1)}, f32[6,8,128]{2,1,0:T(8,128)S(1)}, u32[]{:S(2)}, u32[]{:S(2)}) collective-permute-start(f32[6,8,128]{2,1,0:T(8,128)S(1)} %bitcast.15), channel_id=1, source_target_pairs={{0,16},{16,0},{32,48},{48,32},{64,80},{80,64},{96,112},{112,96},{1... | collective-permute-start | bytes 73736 | tf_op jit(solution)/shard_map/ppermute | solution.py:393
  7.0 11.0 %collective-permute-start = (f32[3,16,8,128]{3,2,1,0:T(8,128)S(1)}, f32[3,16,8,128]{3,2,1,0:T(8,128)S(1)}, u32[]{:S(2)}, u32[]{:S(2)}) collective-permute-start(f32[3,16,8,128]{3,2,1,0:T(8,128)S(1)} %bitcast.14), channel_id=1, source_target_pairs={{0,240},{16,32},{32,16},{48,64},{64,48},{80,96},{96,80},{112,128},... | collective-permute-start | bytes 589832 | tf_op jit(solution)/shard_map/ppermute | solution.py:394
  7.8 10.2 %collective-permute-start.1 = (f32[3,16,8,128]{3,2,1,0:T(8,128)S(1)}, f32[3,16,8,128]{3,2,1,0:T(8,128)S(1)}, u32[]{:S(2)}, u32[]{:S(2)}) collective-permute-start(f32[3,16,8,128]{3,2,1,0:T(8,128)S(1)} %bitcast.13), channel_id=1, source_target_pairs={{0,16},{16,0},{32,48},{48,32},{64,80},{80,64},{96,112},{112,96},{1... | collective-permute-start | bytes 589832 | tf_op jit(solution)/shard_map/ppermute | solution.py:395
  10.0 8.0 %collective-permute-start.4 = (f32[18,8,128]{2,1,0:T(8,128)S(1)}, f32[18,8,128]{2,1,0:T(8,128)S(1)}, u32[]{:S(2)}, u32[]{:S(2)}) collective-permute-start(f32[18,8,128]{2,1,0:T(8,128)S(1)} %get-tuple-element.23), channel_id=1, source_target_pairs={{0,15},{1,2},{2,1},{3,4},{4,3},{5,6},{6,5},{7,8},{8,7},{9,10},{10,... | collective-permute-start | bytes 221192 | tf_op jit(solution)/shard_map/ppermute | solution.py:406
  13.7 4.3 %collective-permute-start.5 = (f32[18,8,128]{2,1,0:T(8,128)S(1)}, f32[18,8,128]{2,1,0:T(8,128)S(1)}, u32[]{:S(2)}, u32[]{:S(2)}) collective-permute-start(f32[18,8,128]{2,1,0:T(8,128)S(1)} %get-tuple-element.24), channel_id=1, source_target_pairs={{0,1},{1,0},{2,3},{3,2},{4,5},{5,4},{6,7},{7,6},{8,9},{9,8},{10,11... | collective-permute-start | bytes 221192 | tf_op jit(solution)/shard_map/ppermute | solution.py:407

commit v7 on v6

--- a/solution.py
+++ b/solution.py
@@ -15,6 +15,7 @@
 coupling = radius_square / diagonal_value
 
 F32 = jnp.float32
+MESH_AXES = ("slab", "tile")
 LANES = 128
 PAIRS = [(i, j) for i in range(MEM) for j in range(i, MEM)]
 SY = {pair: n for n, pair in enumerate(PAIRS)}
@@ -353,10 +354,29 @@
     return pltpu.with_memory_space_constraint(array, pltpu.HBM)
 
 
-def swaps(count):
-    even = [(i, i ^ 1) for i in range(count)]
-    odd = [(i, (i + 1) % count if i % 2 else (i - 1) % count) for i in range(count)]
-    return odd, even
+def swaps():
+    slabs, tiles = lax.axis_size("slab"), lax.axis_size("tile")
+    places = [(slab, tile) for slab in range(slabs) for tile in range(tiles)]
+    spare = max(slabs // 4, 1)
+
+    def pairs(partner):
+        targets = [partner(*place) for place in places]
+        return [(i, slab * tiles + tile) for i, (slab, tile) in enumerate(targets)]
+
+    def slab_odd(slab, tile):
+        beside = slab + 1 if slab % 2 else slab - 1
+        return (beside, tile) if 0 <= beside < slabs else (slab, tile ^ 1)
+
+    def tile_odd(slab, tile):
+        beside = tile + 1 if tile % 2 else tile - 1
+        return (slab, beside) if 0 <= beside < tiles else (slab ^ spare, tile)
+
+    return (
+        pairs(slab_odd),
+        pairs(lambda slab, tile: (slab ^ 1, tile)),
+        pairs(tile_odd),
+        pairs(lambda slab, tile: (slab, tile ^ 1)),
+    )
 
 
 def per_device(sensitivity, filtered_density, passive_blocks, history_steps, history_changes):
@@ -388,11 +408,11 @@
     rim_odd, rim_even = (array.reshape(6, width, LANES) for array in (rim_odd, rim_even))
     odd, even = (array.reshape(SWEEPS, rows, width, LANES) for array in (odd, even))
 
-    odd_pairs, even_pairs = swaps(lax.axis_size("slab"))
-    rim_odd = lax.ppermute(rim_odd, "slab", odd_pairs)
-    rim_even = lax.ppermute(rim_even, "slab", even_pairs)
-    odd = lax.ppermute(odd, "slab", odd_pairs)
-    even = lax.ppermute(even, "slab", even_pairs)
+    slab_odd, slab_even, tile_odd, tile_even = swaps()
+    rim_odd = lax.ppermute(rim_odd, MESH_AXES, slab_odd)
+    rim_even = lax.ppermute(rim_even, MESH_AXES, slab_even)
+    odd = lax.ppermute(odd, MESH_AXES, slab_odd)
+    even = lax.ppermute(even, MESH_AXES, slab_even)
 
     row_odd, row_even = pl.pallas_call(
         pack_kernel,
@@ -402,9 +422,8 @@
         compiler_params=kernel_params(8),
         name="edges",
     )(u, rim_odd, rim_even)
-    odd_pairs, even_pairs = swaps(lax.axis_size("tile"))
-    row_odd = lax.ppermute(row_odd, "tile", odd_pairs)
-    row_even = lax.ppermute(row_even, "tile", even_pairs)
+    row_odd = lax.ppermute(row_odd, MESH_AXES, tile_odd)
+    row_even = lax.ppermute(row_even, MESH_AXES, tile_even)
 
     history = like(history_steps.shape, F32)
     sums, keep, steps, changes = pl.pallas_call(
@@ -444,7 +463,7 @@
         name="sweeps",
     )(u, odd, even, row_odd, row_even, keep, steps, changes, sums)
 
-    received = lax.all_to_all(line, ("slab", "tile"), 0, 0, tiled=True)
+    received = lax.all_to_all(line, MESH_AXES, 0, 0, tiled=True)
 
     return pl.pallas_call(
         combine_kernel,

time: 43.9 us -> 42.9 us (0.977)
  starting transfers between devices: 13.1 us -> 9.44 us
  blocking collectives: 23.7 us -> 27.2 us
  waiting for transfers between devices: 1.51 us -> 0.57 us
    ppermute x6, starting transfers between devices: 13.1 us -> 9.44 us  [the longest x1 3.33 us: per_device(): rim_odd = lax.ppermute(rim_odd, MESH_AXES, slab_odd)]
    all_to_all x1, blocking collectives: 23.7 us -> 27.2 us  [per_device(): received = lax.all_to_all(line, MESH_AXES, 0, 0, tiled=True)]
    ppermute x6, waiting for transfers between devices: 1.51 us -> 0.57 us  [the longest x1 0.55 us: per_device(): rim_even = lax.ppermute(rim_even, MESH_AXES, slab_even)]
where the time goes in v7:
time: 42.9 us; the launch traced here: 42.7 us
  blocking collectives  27.2 us (63%)
  starting transfers between devices  9.44 us (22%)
  Pallas kernels  5.42 us (13%)
  waiting for transfers between devices  0.57 us (1%)
    all_to_all x1, blocking collectives, per_device(): received = lax.all_to_all(line, MESH_AXES, 0, 0, tiled=True)  27.2 us
    ppermute x1, starting transfers between devices, per_device(): rim_odd = lax.ppermute(rim_odd, MESH_AXES, slab_odd)  3.33 us
    ppermute x1, starting transfers between devices, per_device(): row_odd = lax.ppermute(row_odd, MESH_AXES, tile_odd)  2.86 us
    pallas_call x1, Pallas kernels, per_device(): pl.pallas_call(gram_kernel, out_shape=(like((SUMS, LANES), F32), like((de...  2.2 us
    ppermute x1, starting transfers between devices, per_device(): odd = lax.ppermute(odd, MESH_AXES, slab_odd)  1.24 us
    pallas_call x1, Pallas kernels, per_device(): pl.pallas_call(weight_kernel, out_shape=(lines, rim, rim, layers, layers)...  1.18 us
    ppermute x1, starting transfers between devices, per_device(): row_even = lax.ppermute(row_even, MESH_AXES, tile_even)  1.11 us
    pallas_call x1, Pallas kernels, per_device(): pl.pallas_call(sweep_kernel, out_shape=(like(shape, F32), like((devices,...  1.08 us
  transfers between devices with their start and end apart: 6, of which 1 were waited for; matrix products, arithmetic and copies ran while one was open for 0% of the time, Pallas kernels for 5%

profile of v7, /device:TPU:1, one launch (start us, length us, event | category | flops | bytes accessed | tf_op | source)
XLA Modules:
  0.0 42.7 jit_solution(8727716878017566285)
XLA Ops:
  0.0 1.2 %weights.1 = (f32[512,128]{1,0:T(8,128)S(1)}, f32[48,128]{1,0:T(8,128)S(1)}, f32[48,128]{1,0:T(8,128)S(1)}, f32[384,128]{1,0:T(8,128)S(1)}, f32[384,128]{1,0:T(8,128)S(1)}) custom-call(f32[4,16,1024]{2,1,0:T(8,128)} %sens_hbm.1, f32[4,16,1024]{2,1,0:T(8,128)} %dens_hbm.1), custom_call_target="tpu_custom_call" | custom-call | tf_op jit(solution)/shard_map/weights/pallas_call | solution.py:393
  1.2 3.3 %collective-permute-start.2 = (f32[6,8,128]{2,1,0:T(8,128)S(1)}, f32[6,8,128]{2,1,0:T(8,128)S(1)}, u32[]{:S(2)}, u32[]{:S(2)}) collective-permute-start(f32[6,8,128]{2,1,0:T(8,128)S(1)} %bitcast.16), channel_id=1, source_target_pairs={{0,1},{1,0},{2,3},{3,2},{4,5},{5,4},{6,7},{7,6},{8,9},{9,8},{10,11... | collective-permute-start | bytes 73736 | tf_op jit(solution)/shard_map/ppermute | solution.py:412
  4.5 0.0 collective-permute-start.3
  4.5 1.2 %collective-permute-start = (f32[3,16,8,128]{3,2,1,0:T(8,128)S(1)}, f32[3,16,8,128]{3,2,1,0:T(8,128)S(1)}, u32[]{:S(2)}, u32[]{:S(2)}) collective-permute-start(f32[3,16,8,128]{3,2,1,0:T(8,128)S(1)} %bitcast.14), channel_id=1, source_target_pairs={{0,1},{1,0},{2,3},{3,2},{4,5},{5,4},{6,7},{7,6},{8,9},{9,8},{10,11... | collective-permute-start | bytes 589832 | tf_op jit(solution)/shard_map/ppermute | solution.py:414
  5.8 0.9 %collective-permute-start.1 = (f32[3,16,8,128]{3,2,1,0:T(8,128)S(1)}, f32[3,16,8,128]{3,2,1,0:T(8,128)S(1)}, u32[]{:S(2)}, u32[]{:S(2)}) collective-permute-start(f32[3,16,8,128]{3,2,1,0:T(8,128)S(1)} %bitcast.13), channel_id=1, source_target_pairs={{0,16},{1,17},{2,18},{3,19},{4,20},{5,21},{6,22},{7,23},{8,24},{9,... | collective-permute-start | bytes 589832 | tf_op jit(solution)/shard_map/ppermute | solution.py:415
  6.7 0.0 collective-permute-done.2.odd_ref
  6.7 0.6 %collective-permute-done.3.even_ref = f32[6,8,128]{2,1,0:T(8,128)S(1)} collective-permute-done((f32[6,8,128]{2,1,0:T(8,128)S(1)}, f32[6,8,128]{2,1,0:T(8,128)S(1)}, u32[]{:S(2)}, u32[]{:S(2)}) %collective-permute-start.3) | collective-permute-done | bytes 24608 | tf_op jit(solution)/shard_map/ppermute | solution.py:413
  7.2 2.9 %collective-permute-start.4 = (f32[18,8,128]{2,1,0:T(8,128)S(1)}, f32[18,8,128]{2,1,0:T(8,128)S(1)}, u32[]{:S(2)}, u32[]{:S(2)}) collective-permute-start(f32[18,8,128]{2,1,0:T(8,128)S(1)} %get-tuple-element.23), channel_id=1, source_target_pairs={{0,64},{1,2},{2,1},{3,4},{4,3},{5,6},{6,5},{7,8},{8,7},{9,10},{10,... | collective-permute-start | bytes 221192 | tf_op jit(solution)/shard_map/ppermute | solution.py:425
  10.1 1.1 %collective-permute-start.5 = (f32[18,8,128]{2,1,0:T(8,128)S(1)}, f32[18,8,128]{2,1,0:T(8,128)S(1)}, u32[]{:S(2)}, u32[]{:S(2)}) collective-permute-start(f32[18,8,128]{2,1,0:T(8,128)S(1)} %get-tuple-element.24), channel_id=1, source_target_pairs={{0,1},{1,0},{2,3},{3,2},{4,5},{5,4},{6,7},{7,6},{8,9},{9,8},{10,11... | collective-permute-start | bytes 221192 | tf_op jit(solution)/shard_map/ppermute | solution.py:426
  11.2 2.2 %gram.1 = (f32[32,128]{1,0:T(8,128)S(1)}, f32[2,16,1024]{2,1,0:T(8,128)S(1)}, f32[4,4,16,1024]{3,2,1,0:T(8,128)S(1)}, f32[4,4,16,1024]{3,2,1,0:T(8,128)S(1)}) custom-call(f32[4,4,16,1024]{3,2,1,0:T(8,128)} %steps_hbm.1, f32[4,4,16,1024]{3,2,1,0:T(8,128)} %changes_hbm.1, s32[2,8,512]{2,1,0:T(8,128)} %passive_hbm.1), custom_call_target="tpu_custom_call" | custom-call | flops 8000000000 | bytes 43000000 | tf_op jit(solution)/shard_map/gram/pallas_call | solution.py:429
  13.4 0.0 collective-permute-done.4.row_odd_ref
  13.4 0.0 collective-permute-done.5.row_even_ref
  13.4 0.0 collective-permute-done.odd_ref
  13.4 0.0 collective-permute-done.1.even_ref
  13.5 1.1 %sweeps.1 = (f32[4,16,1024]{2,1,0:T(8,128)S(1)}, f32[256,128]{1,0:T(8,128)S(1)}) custom-call(f32[4,16,8,128]{3,2,1,0:T(8,128)S(1)} %bitcast.10, f32[3,16,8,128]{3,2,1,0:T(8,128)S(1)} %collective-permute-done.odd_ref, f32[3,16,8,128]{3,2,1,0:T(8,128)S(1)} %collective-permute-done.1.even_ref, f32[18,8,128]{2,1,0:T(8,128)S(1)} %collective-permute-done.4.row_odd_ref, ...), custom_call_target="tpu_custom_call" | custom-call | tf_op jit(solution)/shard_map/sweeps/pallas_call | solution.py:450
  14.5 27.2 %all_to_all.11 = f32[256,1,128]{2,1,0:T(1,128)S(1)} all-to-all(f32[256,1,128]{2,1,0:T(1,128)S(1)} %bitcast.12), channel_id=1, replica_groups=mesh['slab'=16,'tile'=16] {'slab','tile'}, dimensions={0} | all-to-all | bytes 262144 | tf_op jit(solution)/shard_map/all_to_all | solution.py:466
  41.8 0.9 %combine.1 = f32[4,16,1024]{2,1,0:T(8,128)} custom-call(f32[256,128]{1,0:T(8,128)S(1)} %bitcast.11, f32[4,16,1024]{2,1,0:T(8,128)S(1)} %get-tuple-element.30.grad_ref, f32[4,4,16,1024]{3,2,1,0:T(8,128)S(1)} %get-tuple-element.26.steps_ref, f32[4,4,16,1024]{3,2,1,0:T(8,128)S(1)} %get-tuple-element.27.changes_ref), custom_call_target="tpu_custom_call" | custom-call | tf_op jit(solution)/shard_map/combine/pallas_call | solution.py:468
  (1 shorter events, 0.0 us)
Async XLA Ops:
  1.2 5.5 %collective-permute-start.2 = (f32[6,8,128]{2,1,0:T(8,128)S(1)}, f32[6,8,128]{2,1,0:T(8,128)S(1)}, u32[]{:S(2)}, u32[]{:S(2)}) collective-permute-start(f32[6,8,128]{2,1,0:T(8,128)S(1)} %bitcast.16), channel_id=1, source_target_pairs={{0,1},{1,0},{2,3},{3,2},{4,5},{5,4},{6,7},{7,6},{8,9},{9,8},{10,11... | collective-permute-start | bytes 73736 | tf_op jit(solution)/shard_map/ppermute | solution.py:412
  4.5 2.7 %collective-permute-start.3 = (f32[6,8,128]{2,1,0:T(8,128)S(1)}, f32[6,8,128]{2,1,0:T(8,128)S(1)}, u32[]{:S(2)}, u32[]{:S(2)}) collective-permute-start(f32[6,8,128]{2,1,0:T(8,128)S(1)} %bitcast.15), channel_id=1, source_target_pairs={{0,16},{1,17},{2,18},{3,19},{4,20},{5,21},{6,22},{7,23},{8,24},{9,... | collective-permute-start | bytes 73736 | tf_op jit(solution)/shard_map/ppermute | solution.py:413
  4.5 8.9 %collective-permute-start = (f32[3,16,8,128]{3,2,1,0:T(8,128)S(1)}, f32[3,16,8,128]{3,2,1,0:T(8,128)S(1)}, u32[]{:S(2)}, u32[]{:S(2)}) collective-permute-start(f32[3,16,8,128]{3,2,1,0:T(8,128)S(1)} %bitcast.14), channel_id=1, source_target_pairs={{0,1},{1,0},{2,3},{3,2},{4,5},{5,4},{6,7},{7,6},{8,9},{9,8},{10,11... | collective-permute-start | bytes 589832 | tf_op jit(solution)/shard_map/ppermute | solution.py:414
  5.8 7.7 %collective-permute-start.1 = (f32[3,16,8,128]{3,2,1,0:T(8,128)S(1)}, f32[3,16,8,128]{3,2,1,0:T(8,128)S(1)}, u32[]{:S(2)}, u32[]{:S(2)}) collective-permute-start(f32[3,16,8,128]{3,2,1,0:T(8,128)S(1)} %bitcast.13), channel_id=1, source_target_pairs={{0,16},{1,17},{2,18},{3,19},{4,20},{5,21},{6,22},{7,23},{8,24},{9,... | collective-permute-start | bytes 589832 | tf_op jit(solution)/shard_map/ppermute | solution.py:415
  7.2 6.2 %collective-permute-start.4 = (f32[18,8,128]{2,1,0:T(8,128)S(1)}, f32[18,8,128]{2,1,0:T(8,128)S(1)}, u32[]{:S(2)}, u32[]{:S(2)}) collective-permute-start(f32[18,8,128]{2,1,0:T(8,128)S(1)} %get-tuple-element.23), channel_id=1, source_target_pairs={{0,64},{1,2},{2,1},{3,4},{4,3},{5,6},{6,5},{7,8},{8,7},{9,10},{10,... | collective-permute-start | bytes 221192 | tf_op jit(solution)/shard_map/ppermute | solution.py:425
  10.1 3.3 %collective-permute-start.5 = (f32[18,8,128]{2,1,0:T(8,128)S(1)}, f32[18,8,128]{2,1,0:T(8,128)S(1)}, u32[]{:S(2)}, u32[]{:S(2)}) collective-permute-start(f32[18,8,128]{2,1,0:T(8,128)S(1)} %get-tuple-element.24), channel_id=1, source_target_pairs={{0,1},{1,0},{2,3},{3,2},{4,5},{5,4},{6,7},{7,6},{8,9},{9,8},{10,11... | collective-permute-start | bytes 221192 | tf_op jit(solution)/shard_map/ppermute | solution.py:426

commit v8 on v7

--- a/solution.py
+++ b/solution.py
@@ -182,12 +182,82 @@
                 pack(low_ref, high_ref, row_even_ref, top == 0)
 
 
-def sweep_kernel(
-    u_ref,
-    odd_ref,
-    even_ref,
+def grid_ends():
+    slab, tile = lax.axis_index("slab"), lax.axis_index("tile")
+    return {
+        "low_z": (slab > 0).astype(F32),
+        "high_z": (slab < lax.axis_size("slab") - 1).astype(F32),
+        "low_y": (tile > 0).astype(F32),
+        "high_y": (tile < lax.axis_size("tile") - 1).astype(F32),
+    }
+
+
+def line_sweep(width, depth, rows, inside):
+    lane = lax.broadcasted_iota(jnp.int32, (width, LANES), 1)
+    group = lax.broadcasted_iota(jnp.int32, (width, LANES), 0)
+    lane_first, lane_last = lane == 0, lane == LANES - 1
+    first, last = lane_first & (group == 0), lane_last & (group == width - 1)
+
+    def relax(start, field, z, y):
+        here = field(z, y)
+        around = field(z - 1, y) + field(z + 1, y)
+        around += field(z, y - 1) + field(z, y + 1)
+        before, after = pltpu.roll(here, 1, 1), pltpu.roll(here, LANES - 1, 1)
+        before = jnp.where(lane_first, pltpu.roll(before, 1, 0), before)
+        after = jnp.where(lane_last, pltpu.roll(after, width - 1, 0), after)
+        around += jnp.where(first, 0.0, before) + jnp.where(last, 0.0, after)
+        value = start(z, y) + coupling * around
+        if z < 3:
+            value *= inside["low_z"]
+        if z >= 3 + depth:
+            value *= inside["high_z"]
+        if y < 3:
+            value *= inside["low_y"]
+        if y >= 3 + rows:
+            value *= inside["high_y"]
+        return value
+
+    return relax
+
+
+def inner_kernel(u_ref, odd_ref, even_ref, start_ref, one_ref, two_ref, last_ref):
+    depth, rows, width = u_ref.shape[:3]
+    slab_odd = lax.rem(lax.axis_index("slab"), 2)
+    inside = grid_ends()
+    start_ref[3 : 3 + depth] = u_ref[...]
+    for parity in range(2):
+
+        @pl.when(slab_odd == parity)
+        def _():
+            low_ref, high_ref = (even_ref, odd_ref) if parity else (odd_ref, even_ref)
+            start_ref[0:3] = low_ref[...] * inside["low_z"]
+            start_ref[3 + depth :] = high_ref[...] * inside["high_z"]
+
+    relax = line_sweep(width, depth, rows, inside)
+
+    def reader(ref):
+        return lambda z, y: ref[z, y - 3]
+
+    start, one, two = reader(start_ref), reader(one_ref), reader(two_ref)
+    for z in range(1, 5 + depth):
+        for y in range(4, 2 + rows):
+            one_ref[z, y - 3] = relax(start, start, z, y)
+    for z in range(2, 4 + depth):
+        for y in range(5, 1 + rows):
+            two_ref[z, y - 3] = relax(start, one, z, y)
+    for z in range(3, 3 + depth):
+        for y in range(6, rows):
+            place = ((z - 3) * rows + y - 3) * width
+            last_ref[place : place + width, :] = relax(start, two, z, y)
+
+
+def outer_kernel(
     row_odd_ref,
     row_even_ref,
+    inner_start_ref,
+    inner_one_ref,
+    inner_two_ref,
+    inner_last_ref,
     keep_ref,
     steps_ref,
     changes_ref,
@@ -200,21 +270,10 @@
     last_ref,
     total_ref,
 ):
-    depth, rows, width = u_ref.shape[:3]
-    slab, tile = lax.axis_index("slab"), lax.axis_index("tile")
-    slab_odd, tile_odd = lax.rem(slab, 2), lax.rem(tile, 2)
-    inside = {
-        "low_z": (slab > 0).astype(F32),
-        "high_z": (slab < lax.axis_size("slab") - 1).astype(F32),
-        "low_y": (tile > 0).astype(F32),
-        "high_y": (tile < lax.axis_size("tile") - 1).astype(F32),
-    }
-
-    start_ref[3 : 3 + depth, 3 : 3 + rows] = u_ref[...]
-
-    def layers(low_ref, high_ref):
-        start_ref[0:3, 3 : 3 + rows] = low_ref[...] * inside["low_z"]
-        start_ref[3 + depth :, 3 : 3 + rows] = high_ref[...] * inside["high_z"]
+    depth, rows = grad_ref.shape[:2]
+    width = start_ref.shape[2]
+    tile_odd = lax.rem(lax.axis_index("tile"), 2)
+    inside = grid_ends()
 
     def edge(from_ref, first, count, z, factor, high):
         to = 3 + rows if high else 3 - count
@@ -232,55 +291,42 @@
 
     for parity in range(2):
 
-        @pl.when(slab_odd == parity)
-        def _():
-            layers(*((even_ref, odd_ref) if parity else (odd_ref, even_ref)))
-
         @pl.when(tile_odd == parity)
         def _():
             beside(row_odd_ref, parity == 1)
             beside(row_even_ref, parity == 0)
 
-    lane = lax.broadcasted_iota(jnp.int32, (width, LANES), 1)
-    part = lax.broadcasted_iota(jnp.int32, (width, LANES), 0)
-    lane_first, lane_last = lane == 0, lane == LANES - 1
-    first, last = lane_first & (part == 0), lane_last & (part == width - 1)
-
-    def relax(from_ref, z, y):
-        here = from_ref[z, y]
-        around = from_ref[z - 1, y] + from_ref[z + 1, y]
-        around += from_ref[z, y - 1] + from_ref[z, y + 1]
-        before, after = pltpu.roll(here, 1, 1), pltpu.roll(here, LANES - 1, 1)
-        before = jnp.where(lane_first, pltpu.roll(before, 1, 0), before)
-        after = jnp.where(lane_last, pltpu.roll(after, width - 1, 0), after)
-        around += jnp.where(first, 0.0, before) + jnp.where(last, 0.0, after)
-        return start_ref[z, y] + coupling * around
-
-    def factors(z, y):
-        if z < 3:
-            yield inside["low_z"]
-        if z >= 3 + depth:
-            yield inside["high_z"]
-        if y < 3:
-            yield inside["low_y"]
-        if y >= 3 + rows:
-            yield inside["high_y"]
-
-    def sweep(from_ref, to_ref, reach):
+    relax = line_sweep(width, depth, rows, inside)
+
+    def reader(inner_ref, outer_ref, level):
+        def read(z, y):
+            inner = 3 + level <= y < 3 + rows - level
+            return inner_ref[z, y - 3] if inner else outer_ref[z, y]
+
+        return read
+
+    start = reader(inner_start_ref, start_ref, 0)
+    one = reader(inner_one_ref, one_ref, 1)
+    two = reader(inner_two_ref, two_ref, 2)
+
+    def edge_lines(level):
+        reach = SWEEPS - level
         for z in range(3 - reach, 3 + depth + reach):
             wide = reach - max(3 - z, z - 2 - depth, 0)
             for y in range(3 - wide, 3 + rows + wide):
-                value = relax(from_ref, z, y)
-                for factor in factors(z, y):
-                    value *= factor
-                to_ref[z, y] = value
-
-    sweep(start_ref, one_ref, 2)
-    sweep(one_ref, two_ref, 1)
+                if not 3 + level <= y < 3 + rows - level:
+                    yield z, y
+
+    for z, y in edge_lines(1):
+        one_ref[z, y] = relax(start, start, z, y)
+    for z, y in edge_lines(2):
+        two_ref[z, y] = relax(start, one, z, y)
     for z in range(depth):
-        for y in range(rows):
-            place = (z * rows + y) * width
-            last_ref[place : place + width, :] = relax(two_ref, 3 + z, 3 + y)
+        place = slice((z * rows + 3) * width, (z * rows + rows - 3) * width)
+        last_ref[place, :] = inner_last_ref[place, :]
+    for z, y in edge_lines(3):
+        place = ((z - 3) * rows + y - 3) * width
+        last_ref[place : place + width, :] = relax(start, two, z, y)
 
     sums = [jnp.zeros((8, LANES), F32) for _ in range(2 * MEM)]
     for z in range(depth):
@@ -446,11 +492,21 @@
         name="gram",
     )(in_hbm(history_steps), in_hbm(history_changes), in_hbm(passive_blocks))
 
+    field = like((depth + 6, rows, width, LANES), F32)
+    inner = pl.pallas_call(
+        inner_kernel,
+        out_shape=(field, field, field, lines),
+        in_specs=[VMEM] * 3,
+        out_specs=[VMEM] * 4,
+        compiler_params=kernel_params(8),
+        name="inner",
+    )(u, odd, even)
+
     padded = pltpu.VMEM((depth + 6, rows + 6, width, LANES), F32)
     gradient, line = pl.pallas_call(
-        sweep_kernel,
+        outer_kernel,
         out_shape=(like(shape, F32), like((devices, LANES), F32)),
-        in_specs=[VMEM] * 9,
+        in_specs=[VMEM] * 10,
         out_specs=[VMEM] * 2,
         scratch_shapes=[
             padded,
@@ -460,8 +516,8 @@
             pltpu.VMEM((SUMS, LANES), F32),
         ],
         compiler_params=kernel_params(16),
-        name="sweeps",
-    )(u, odd, even, row_odd, row_even, keep, steps, changes, sums)
+        name="outer",
+    )(row_odd, row_even, *inner, keep, steps, changes, sums)
 
     received = lax.all_to_all(line, MESH_AXES, 0, 0, tiled=True)
 

time: 42.9 us -> 42.4 us (0.988)
  blocking collectives: 27.2 us -> 26.6 us
    all_to_all x1, blocking collectives: 27.2 us -> 26.6 us  [per_device(): received = lax.all_to_all(line, MESH_AXES, 0, 0, tiled=True)]
    pallas_call x1 -> x2, Pallas kernels: 1.08 us -> 1.18 us  [the longest x1 0.59 us: per_device(): pl.pallas_call(inner_kernel, out_shape=(field, field, field, lines), in_s...]
  transfers between devices with their start and end apart: 6 -> 6, of which waited for: 1 -> 1; matrix products, arithmetic and copies ran while one was open for 0% -> 0% of each run, Pallas kernels for 5% -> 7%
where the time goes in v8:
time: 42.4 us; the launch traced here: 42.2 us
  blocking collectives  26.6 us (63%)
  starting transfers between devices  9.44 us (22%)
  Pallas kernels  5.52 us (13%)
  waiting for transfers between devices  0.57 us (1%)
    all_to_all x1, blocking collectives, per_device(): received = lax.all_to_all(line, MESH_AXES, 0, 0, tiled=True)  26.6 us
    ppermute x1, starting transfers between devices, per_device(): rim_odd = lax.ppermute(rim_odd, MESH_AXES, slab_odd)  3.33 us
    ppermute x1, starting transfers between devices, per_device(): row_odd = lax.ppermute(row_odd, MESH_AXES, tile_odd)  2.86 us
    pallas_call x1, Pallas kernels, per_device(): pl.pallas_call(gram_kernel, out_shape=(like((SUMS, LANES), F32), like((de...  2.2 us
    ppermute x1, starting transfers between devices, per_device(): odd = lax.ppermute(odd, MESH_AXES, slab_odd)  1.24 us
    pallas_call x1, Pallas kernels, per_device(): pl.pallas_call(weight_kernel, out_shape=(lines, rim, rim, layers, layers)...  1.18 us
    ppermute x1, starting transfers between devices, per_device(): row_even = lax.ppermute(row_even, MESH_AXES, tile_even)  1.11 us
    pallas_call x1, Pallas kernels, per_device(): pl.pallas_call(combine_kernel, out_shape=like(shape, F32), in_specs=[VMEM...  0.95 us
  transfers between devices with their start and end apart: 6, of which 1 were waited for; matrix products, arithmetic and copies ran while one was open for 0% of the time, Pallas kernels for 7%

profile of v8, /device:TPU:1, one launch (start us, length us, event | category | flops | bytes accessed | tf_op | source)
XLA Modules:
  0.0 42.2 jit_solution(12558215255096877611)
XLA Ops:
  0.0 1.2 %weights.1 = (f32[512,128]{1,0:T(8,128)S(1)}, f32[48,128]{1,0:T(8,128)S(1)}, f32[48,128]{1,0:T(8,128)S(1)}, f32[384,128]{1,0:T(8,128)S(1)}, f32[384,128]{1,0:T(8,128)S(1)}) custom-call(f32[4,16,1024]{2,1,0:T(8,128)} %sens_hbm.1, f32[4,16,1024]{2,1,0:T(8,128)} %dens_hbm.1), custom_call_target="tpu_custom_call" | custom-call | tf_op jit(solution)/shard_map/weights/pallas_call | solution.py:439
  1.2 3.3 %collective-permute-start = (f32[6,8,128]{2,1,0:T(8,128)S(1)}, f32[6,8,128]{2,1,0:T(8,128)S(1)}, u32[]{:S(2)}, u32[]{:S(2)}) collective-permute-start(f32[6,8,128]{2,1,0:T(8,128)S(1)} %bitcast.16), channel_id=1, source_target_pairs={{0,1},{1,0},{2,3},{3,2},{4,5},{5,4},{6,7},{7,6},{8,9},{9,8},{10,11... | collective-permute-start | bytes 73736 | tf_op jit(solution)/shard_map/ppermute | solution.py:458
  4.5 0.0 collective-permute-start.1
  4.5 1.2 %collective-permute-start.4 = (f32[3,16,8,128]{3,2,1,0:T(8,128)S(1)}, f32[3,16,8,128]{3,2,1,0:T(8,128)S(1)}, u32[]{:S(2)}, u32[]{:S(2)}) collective-permute-start(f32[3,16,8,128]{3,2,1,0:T(8,128)S(1)} %bitcast.14), channel_id=1, source_target_pairs={{0,1},{1,0},{2,3},{3,2},{4,5},{5,4},{6,7},{7,6},{8,9},{9,8},{10,11... | collective-permute-start | bytes 589832 | tf_op jit(solution)/shard_map/ppermute | solution.py:460
  5.8 0.9 %collective-permute-start.5 = (f32[3,16,8,128]{3,2,1,0:T(8,128)S(1)}, f32[3,16,8,128]{3,2,1,0:T(8,128)S(1)}, u32[]{:S(2)}, u32[]{:S(2)}) collective-permute-start(f32[3,16,8,128]{3,2,1,0:T(8,128)S(1)} %bitcast.13), channel_id=1, source_target_pairs={{0,16},{1,17},{2,18},{3,19},{4,20},{5,21},{6,22},{7,23},{8,24},{9,... | collective-permute-start | bytes 589832 | tf_op jit(solution)/shard_map/ppermute | solution.py:461
  6.7 0.0 collective-permute-done.odd_ref
  6.7 0.6 %collective-permute-done.1.even_ref = f32[6,8,128]{2,1,0:T(8,128)S(1)} collective-permute-done((f32[6,8,128]{2,1,0:T(8,128)S(1)}, f32[6,8,128]{2,1,0:T(8,128)S(1)}, u32[]{:S(2)}, u32[]{:S(2)}) %collective-permute-start.1) | collective-permute-done | bytes 24608 | tf_op jit(solution)/shard_map/ppermute | solution.py:459
  7.2 2.9 %collective-permute-start.2 = (f32[18,8,128]{2,1,0:T(8,128)S(1)}, f32[18,8,128]{2,1,0:T(8,128)S(1)}, u32[]{:S(2)}, u32[]{:S(2)}) collective-permute-start(f32[18,8,128]{2,1,0:T(8,128)S(1)} %get-tuple-element.25), channel_id=1, source_target_pairs={{0,64},{1,2},{2,1},{3,4},{4,3},{5,6},{6,5},{7,8},{8,7},{9,10},{10,... | collective-permute-start | bytes 221192 | tf_op jit(solution)/shard_map/ppermute | solution.py:471
  10.1 1.1 %collective-permute-start.3 = (f32[18,8,128]{2,1,0:T(8,128)S(1)}, f32[18,8,128]{2,1,0:T(8,128)S(1)}, u32[]{:S(2)}, u32[]{:S(2)}) collective-permute-start(f32[18,8,128]{2,1,0:T(8,128)S(1)} %get-tuple-element.26), channel_id=1, source_target_pairs={{0,1},{1,0},{2,3},{3,2},{4,5},{5,4},{6,7},{7,6},{8,9},{9,8},{10,11... | collective-permute-start | bytes 221192 | tf_op jit(solution)/shard_map/ppermute | solution.py:472
  11.2 2.2 %gram.1 = (f32[32,128]{1,0:T(8,128)S(1)}, f32[2,16,1024]{2,1,0:T(8,128)S(1)}, f32[4,4,16,1024]{3,2,1,0:T(8,128)S(1)}, f32[4,4,16,1024]{3,2,1,0:T(8,128)S(1)}) custom-call(f32[4,4,16,1024]{3,2,1,0:T(8,128)} %steps_hbm.1, f32[4,4,16,1024]{3,2,1,0:T(8,128)} %changes_hbm.1, s32[2,8,512]{2,1,0:T(8,128)} %passive_hbm.1), custom_call_target="tpu_custom_call" | custom-call | flops 8000000000 | bytes 43000000 | tf_op jit(solution)/shard_map/gram/pallas_call | solution.py:475
  13.4 0.0 collective-permute-done.4.odd_ref
  13.4 0.0 collective-permute-done.5.even_ref
  13.4 0.6 %inner.1 = (f32[10,16,8,128]{3,2,1,0:T(8,128)S(1)}, f32[10,16,8,128]{3,2,1,0:T(8,128)S(1)}, f32[10,16,8,128]{3,2,1,0:T(8,128)S(1)}, f32[512,128]{1,0:T(8,128)S(1)}) custom-call(f32[4,16,8,128]{3,2,1,0:T(8,128)S(1)} %bitcast.10, f32[3,16,8,128]{3,2,1,0:T(8,128)S(1)} %collective-permute-done.4.odd_ref, f32[3,16,8,128]{3,2,1,0:T(8,128)S(1)} %collective-permute-done.5.even_ref), custom_call_target="tpu_custom_call" | custom-call | tf_op jit(solution)/shard_map/inner/pallas_call | solution.py:496
  14.0 0.0 collective-permute-done.2.row_odd_ref
  14.0 0.0 collective-permute-done.3.row_even_ref
  14.1 0.6 %outer.1 = (f32[4,16,1024]{2,1,0:T(8,128)S(1)}, f32[256,128]{1,0:T(8,128)S(1)}) custom-call(f32[18,8,128]{2,1,0:T(8,128)S(1)} %collective-permute-done.2.row_odd_ref, f32[18,8,128]{2,1,0:T(8,128)S(1)} %collective-permute-done.3.row_even_ref, f32[10,16,8,128]{3,2,1,0:T(8,128)S(1)} %get-tuple-element.29.inner_start_ref, ...), custom_call_target="tpu_custom_call" | custom-call | tf_op jit(solution)/shard_map/outer/pallas_call | solution.py:506
  14.6 26.6 %all_to_all.11 = f32[256,1,128]{2,1,0:T(1,128)S(1)} all-to-all(f32[256,1,128]{2,1,0:T(1,128)S(1)} %bitcast.12), channel_id=1, replica_groups=mesh['slab'=16,'tile'=16] {'slab','tile'}, dimensions={0} | all-to-all | bytes 262144 | tf_op jit(solution)/shard_map/all_to_all | solution.py:522
  41.2 0.9 %combine.1 = f32[4,16,1024]{2,1,0:T(8,128)} custom-call(f32[256,128]{1,0:T(8,128)S(1)} %bitcast.11, f32[4,16,1024]{2,1,0:T(8,128)S(1)} %get-tuple-element.38.grad_ref, f32[4,4,16,1024]{3,2,1,0:T(8,128)S(1)} %get-tuple-element.34.steps_ref, f32[4,4,16,1024]{3,2,1,0:T(8,128)S(1)} %get-tuple-element.35.changes_ref), custom_call_target="tpu_custom_call" | custom-call | tf_op jit(solution)/shard_map/combine/pallas_call | solution.py:524
  (1 shorter events, 0.0 us)
Async XLA Ops:
  1.2 5.5 %collective-permute-start = (f32[6,8,128]{2,1,0:T(8,128)S(1)}, f32[6,8,128]{2,1,0:T(8,128)S(1)}, u32[]{:S(2)}, u32[]{:S(2)}) collective-permute-start(f32[6,8,128]{2,1,0:T(8,128)S(1)} %bitcast.16), channel_id=1, source_target_pairs={{0,1},{1,0},{2,3},{3,2},{4,5},{5,4},{6,7},{7,6},{8,9},{9,8},{10,11... | collective-permute-start | bytes 73736 | tf_op jit(solution)/shard_map/ppermute | solution.py:458
  4.5 2.7 %collective-permute-start.1 = (f32[6,8,128]{2,1,0:T(8,128)S(1)}, f32[6,8,128]{2,1,0:T(8,128)S(1)}, u32[]{:S(2)}, u32[]{:S(2)}) collective-permute-start(f32[6,8,128]{2,1,0:T(8,128)S(1)} %bitcast.15), channel_id=1, source_target_pairs={{0,16},{1,17},{2,18},{3,19},{4,20},{5,21},{6,22},{7,23},{8,24},{9,... | collective-permute-start | bytes 73736 | tf_op jit(solution)/shard_map/ppermute | solution.py:459
  4.5 8.9 %collective-permute-start.4 = (f32[3,16,8,128]{3,2,1,0:T(8,128)S(1)}, f32[3,16,8,128]{3,2,1,0:T(8,128)S(1)}, u32[]{:S(2)}, u32[]{:S(2)}) collective-permute-start(f32[3,16,8,128]{3,2,1,0:T(8,128)S(1)} %bitcast.14), channel_id=1, source_target_pairs={{0,1},{1,0},{2,3},{3,2},{4,5},{5,4},{6,7},{7,6},{8,9},{9,8},{10,11... | collective-permute-start | bytes 589832 | tf_op jit(solution)/shard_map/ppermute | solution.py:460
  5.8 7.7 %collective-permute-start.5 = (f32[3,16,8,128]{3,2,1,0:T(8,128)S(1)}, f32[3,16,8,128]{3,2,1,0:T(8,128)S(1)}, u32[]{:S(2)}, u32[]{:S(2)}) collective-permute-start(f32[3,16,8,128]{3,2,1,0:T(8,128)S(1)} %bitcast.13), channel_id=1, source_target_pairs={{0,16},{1,17},{2,18},{3,19},{4,20},{5,21},{6,22},{7,23},{8,24},{9,... | collective-permute-start | bytes 589832 | tf_op jit(solution)/shard_map/ppermute | solution.py:461
  7.2 6.8 %collective-permute-start.2 = (f32[18,8,128]{2,1,0:T(8,128)S(1)}, f32[18,8,128]{2,1,0:T(8,128)S(1)}, u32[]{:S(2)}, u32[]{:S(2)}) collective-permute-start(f32[18,8,128]{2,1,0:T(8,128)S(1)} %get-tuple-element.25), channel_id=1, source_target_pairs={{0,64},{1,2},{2,1},{3,4},{4,3},{5,6},{6,5},{7,8},{8,7},{9,10},{10,... | collective-permute-start | bytes 221192 | tf_op jit(solution)/shard_map/ppermute | solution.py:471
  10.1 3.9 %collective-permute-start.3 = (f32[18,8,128]{2,1,0:T(8,128)S(1)}, f32[18,8,128]{2,1,0:T(8,128)S(1)}, u32[]{:S(2)}, u32[]{:S(2)}) collective-permute-start(f32[18,8,128]{2,1,0:T(8,128)S(1)} %get-tuple-element.26), channel_id=1, source_target_pairs={{0,1},{1,0},{2,3},{3,2},{4,5},{5,4},{6,7},{7,6},{8,9},{9,8},{10,11... | collective-permute-start | bytes 221192 | tf_op jit(solution)/shard_map/ppermute | solution.py:472

commit v9 on v8

--- a/solution.py
+++ b/solution.py
@@ -430,15 +430,14 @@
     depth, rows, cols = shape
     like = jax.ShapeDtypeStruct
     width = cols // LANES
-    lines, layers, rim = (
+    field_lines, layers, rim = (
         like((count * width, LANES), F32) for count in (depth * rows, SWEEPS * rows, 6)
     )
     edges = like((3 * depth + 6, width, LANES), F32)
-    devices = lax.axis_size("slab") * lax.axis_size("tile")
 
     u, rim_odd, rim_even, odd, even = pl.pallas_call(
         weight_kernel,
-        out_shape=(lines, rim, rim, layers, layers),
+        out_shape=(field_lines, rim, rim, layers, layers),
         in_specs=[HBM] * 2,
         out_specs=[VMEM] * 5,
         scratch_shapes=[
@@ -495,7 +494,7 @@
     field = like((depth + 6, rows, width, LANES), F32)
     inner = pl.pallas_call(
         inner_kernel,
-        out_shape=(field, field, field, lines),
+        out_shape=(field, field, field, field_lines),
         in_specs=[VMEM] * 3,
         out_specs=[VMEM] * 4,
         compiler_params=kernel_params(8),
@@ -505,7 +504,7 @@
     padded = pltpu.VMEM((depth + 6, rows + 6, width, LANES), F32)
     gradient, line = pl.pallas_call(
         outer_kernel,
-        out_shape=(like(shape, F32), like((devices, LANES), F32)),
+        out_shape=(like(shape, F32), like((8, LANES), F32)),
         in_specs=[VMEM] * 10,
         out_specs=[VMEM] * 2,
         scratch_shapes=[
@@ -519,7 +518,14 @@
         name="outer",
     )(row_odd, row_even, *inner, keep, steps, changes, sums)
 
-    received = lax.all_to_all(line, MESH_AXES, 0, 0, tiled=True)
+    slabs, tiles = lax.axis_size("slab"), lax.axis_size("tile")
+    groups = [
+        [slab * tiles + tile for tile in range(core, tiles, 2) for slab in range(slabs)]
+        for core in range(2)
+    ]
+    line = line + lax.ppermute(line, MESH_AXES, tile_even)
+    lines = jnp.broadcast_to(line[:1], (len(groups[0]), LANES))
+    received = lax.all_to_all(lines, MESH_AXES, 0, 0, axis_index_groups=groups, tiled=True)
 
     return pl.pallas_call(
         combine_kernel,

time: 42.4 us -> 42.4 us (level)
  blocking collectives: 26.6 us -> 25.4 us
  waiting for transfers between devices: 0.57 us -> 1.72 us
    ppermute x0 -> x1, waiting for transfers between devices: none -> 1.15 us  [per_device(): line = line + lax.ppermute(line, MESH_AXES, tile_even)]
    all_to_all x1, blocking collectives: 26.6 us -> 25.4 us  [per_device(): lax.all_to_all(lines, MESH_AXES, 0, 0, axis_index_groups=groups, tiled=True)]
  transfers between devices with their start and end apart: 6 -> 7, of which waited for: 1 -> 2; matrix products, arithmetic and copies ran while one was open for 0% -> 0% of each run, Pallas kernels for 7% -> 7%
where the time goes in v9:
time: 42.4 us; the launch traced here: 42.2 us
  blocking collectives  25.4 us (60%)
  starting transfers between devices  9.46 us (22%)
  Pallas kernels  5.49 us (13%)
  waiting for transfers between devices  1.72 us (4%)
    all_to_all x1, blocking collectives, per_device(): lax.all_to_all(lines, MESH_AXES, 0, 0, axis_index_groups=groups, tiled=True)  25.4 us
    ppermute x1, starting transfers between devices, per_device(): rim_odd = lax.ppermute(rim_odd, MESH_AXES, slab_odd)  3.33 us
    ppermute x1, starting transfers between devices, per_device(): row_odd = lax.ppermute(row_odd, MESH_AXES, tile_odd)  2.86 us
    pallas_call x1, Pallas kernels, per_device(): pl.pallas_call(gram_kernel, out_shape=(like((SUMS, LANES), F32), like((de...  2.2 us
    ppermute x1, starting transfers between devices, per_device(): odd = lax.ppermute(odd, MESH_AXES, slab_odd)  1.24 us
    pallas_call x1, Pallas kernels, per_device(): pl.pallas_call(weight_kernel, out_shape=(field_lines, rim, rim, layers, l...  1.18 us
    ppermute x1, waiting for transfers between devices, per_device(): line = line + lax.ppermute(line, MESH_AXES, tile_even)  1.15 us
    ppermute x1, starting transfers between devices, per_device(): row_even = lax.ppermute(row_even, MESH_AXES, tile_even)  1.11 us
  transfers between devices with their start and end apart: 7, of which 2 were waited for; matrix products, arithmetic and copies ran while one was open for 0% of the time, Pallas kernels for 7%

profile of v9, /device:TPU:1, one launch (start us, length us, event | category | flops | bytes accessed | tf_op | source)
XLA Modules:
  0.0 42.2 jit_solution(11230890239359383959)
XLA Ops:
  0.0 1.2 %weights.1 = (f32[512,128]{1,0:T(8,128)S(1)}, f32[48,128]{1,0:T(8,128)S(1)}, f32[48,128]{1,0:T(8,128)S(1)}, f32[384,128]{1,0:T(8,128)S(1)}, f32[384,128]{1,0:T(8,128)S(1)}) custom-call(f32[4,16,1024]{2,1,0:T(8,128)} %sens_hbm.1, f32[4,16,1024]{2,1,0:T(8,128)} %dens_hbm.1), custom_call_target="tpu_custom_call" | custom-call | tf_op jit(solution)/shard_map/weights/pallas_call | solution.py:438
  1.2 3.3 %collective-permute-start = (f32[6,8,128]{2,1,0:T(8,128)S(1)}, f32[6,8,128]{2,1,0:T(8,128)S(1)}, u32[]{:S(2)}, u32[]{:S(2)}) collective-permute-start(f32[6,8,128]{2,1,0:T(8,128)S(1)} %bitcast.14), channel_id=1, source_target_pairs={{0,1},{1,0},{2,3},{3,2},{4,5},{5,4},{6,7},{7,6},{8,9},{9,8},{10,11... | collective-permute-start | bytes 73736 | tf_op jit(solution)/shard_map/ppermute | solution.py:457
  4.5 0.0 collective-permute-start.1
  4.5 1.2 %collective-permute-start.4 = (f32[3,16,8,128]{3,2,1,0:T(8,128)S(1)}, f32[3,16,8,128]{3,2,1,0:T(8,128)S(1)}, u32[]{:S(2)}, u32[]{:S(2)}) collective-permute-start(f32[3,16,8,128]{3,2,1,0:T(8,128)S(1)} %bitcast.12), channel_id=1, source_target_pairs={{0,1},{1,0},{2,3},{3,2},{4,5},{5,4},{6,7},{7,6},{8,9},{9,8},{10,11... | collective-permute-start | bytes 589832 | tf_op jit(solution)/shard_map/ppermute | solution.py:459
  5.8 0.9 %collective-permute-start.5 = (f32[3,16,8,128]{3,2,1,0:T(8,128)S(1)}, f32[3,16,8,128]{3,2,1,0:T(8,128)S(1)}, u32[]{:S(2)}, u32[]{:S(2)}) collective-permute-start(f32[3,16,8,128]{3,2,1,0:T(8,128)S(1)} %bitcast.11), channel_id=1, source_target_pairs={{0,16},{1,17},{2,18},{3,19},{4,20},{5,21},{6,22},{7,23},{8,24},{9,... | collective-permute-start | bytes 589832 | tf_op jit(solution)/shard_map/ppermute | solution.py:460
  6.7 0.0 collective-permute-done.odd_ref
  6.7 0.6 %collective-permute-done.1.even_ref = f32[6,8,128]{2,1,0:T(8,128)S(1)} collective-permute-done((f32[6,8,128]{2,1,0:T(8,128)S(1)}, f32[6,8,128]{2,1,0:T(8,128)S(1)}, u32[]{:S(2)}, u32[]{:S(2)}) %collective-permute-start.1) | collective-permute-done | bytes 24608 | tf_op jit(solution)/shard_map/ppermute | solution.py:458
  7.2 2.9 %collective-permute-start.2 = (f32[18,8,128]{2,1,0:T(8,128)S(1)}, f32[18,8,128]{2,1,0:T(8,128)S(1)}, u32[]{:S(2)}, u32[]{:S(2)}) collective-permute-start(f32[18,8,128]{2,1,0:T(8,128)S(1)} %get-tuple-element.25), channel_id=1, source_target_pairs={{0,64},{1,2},{2,1},{3,4},{4,3},{5,6},{6,5},{7,8},{8,7},{9,10},{10,... | collective-permute-start | bytes 221192 | tf_op jit(solution)/shard_map/ppermute | solution.py:470
  10.1 1.1 %collective-permute-start.3 = (f32[18,8,128]{2,1,0:T(8,128)S(1)}, f32[18,8,128]{2,1,0:T(8,128)S(1)}, u32[]{:S(2)}, u32[]{:S(2)}) collective-permute-start(f32[18,8,128]{2,1,0:T(8,128)S(1)} %get-tuple-element.26), channel_id=1, source_target_pairs={{0,1},{1,0},{2,3},{3,2},{4,5},{5,4},{6,7},{7,6},{8,9},{9,8},{10,11... | collective-permute-start | bytes 221192 | tf_op jit(solution)/shard_map/ppermute | solution.py:471
  11.2 2.2 %gram.1 = (f32[32,128]{1,0:T(8,128)S(1)}, f32[2,16,1024]{2,1,0:T(8,128)S(1)}, f32[4,4,16,1024]{3,2,1,0:T(8,128)S(1)}, f32[4,4,16,1024]{3,2,1,0:T(8,128)S(1)}) custom-call(f32[4,4,16,1024]{3,2,1,0:T(8,128)} %steps_hbm.1, f32[4,4,16,1024]{3,2,1,0:T(8,128)} %changes_hbm.1, s32[2,8,512]{2,1,0:T(8,128)} %passive_hbm.1), custom_call_target="tpu_custom_call" | custom-call | flops 8000000000 | bytes 43000000 | tf_op jit(solution)/shard_map/gram/pallas_call | solution.py:474
  13.4 0.0 collective-permute-done.4.odd_ref
  13.4 0.0 collective-permute-done.5.even_ref
  13.4 0.6 %inner.1 = (f32[10,16,8,128]{3,2,1,0:T(8,128)S(1)}, f32[10,16,8,128]{3,2,1,0:T(8,128)S(1)}, f32[10,16,8,128]{3,2,1,0:T(8,128)S(1)}, f32[512,128]{1,0:T(8,128)S(1)}) custom-call(f32[4,16,8,128]{3,2,1,0:T(8,128)S(1)} %bitcast.9, f32[3,16,8,128]{3,2,1,0:T(8,128)S(1)} %collective-permute-done.4.odd_ref, f32[3,16,8,128]{3,2,1,0:T(8,128)S(1)} %collective-permute-done.5.even_ref), custom_call_target="tpu_custom_call" | custom-call | tf_op jit(solution)/shard_map/inner/pallas_call | solution.py:495
  14.0 0.0 collective-permute-done.2.row_odd_ref
  14.0 0.0 collective-permute-done.3.row_even_ref
  14.1 0.6 %outer.1 = (f32[4,16,1024]{2,1,0:T(8,128)S(1)}, f32[8,128]{1,0:T(8,128)S(1)}) custom-call(f32[18,8,128]{2,1,0:T(8,128)S(1)} %collective-permute-done.2.row_odd_ref, f32[18,8,128]{2,1,0:T(8,128)S(1)} %collective-permute-done.3.row_even_ref, f32[10,16,8,128]{3,2,1,0:T(8,128)S(1)} %get-tuple-element.29.inner_start_ref, ...), custom_call_target="tpu_custom_call" | custom-call | tf_op jit(solution)/shard_map/outer/pallas_call | solution.py:505
  14.6 0.0 collective-permute-start.6
  14.7 1.2 %collective-permute-done.6 = f32[8,128]{1,0:T(8,128)S(1)} collective-permute-done((f32[8,128]{1,0:T(8,128)S(1)}, f32[8,128]{1,0:T(8,128)S(1)}, u32[]{:S(2)}, u32[]{:S(2)}) %collective-permute-start.6) | collective-permute-done | bytes 4128 | tf_op jit(solution)/shard_map/ppermute | solution.py:526
  15.9 25.4 %all_to_all.8 = f32[128,1,128]{2,1,0:T(1,128)S(1)} all-to-all(f32[128,1,128]{2,1,0:T(1,128)S(1)} %broadcast_in_dim.2), channel_id=1, replica_groups={{0,16,32,48,64,80,96,112,128,144,160,176,192,208,224,240,2,18,34,50,66,..., dimensions={0} | all-to-all | bytes 131072 | tf_op jit(solution)/shard_map/all_to_all | solution.py:528
  41.3 0.9 %combine.1 = f32[4,16,1024]{2,1,0:T(8,128)} custom-call(f32[128,128]{1,0:T(8,128)S(1)} %bitcast.10, f32[4,16,1024]{2,1,0:T(8,128)S(1)} %get-tuple-element.38.grad_ref, f32[4,4,16,1024]{3,2,1,0:T(8,128)S(1)} %get-tuple-element.34.steps_ref, f32[4,4,16,1024]{3,2,1,0:T(8,128)S(1)} %get-tuple-element.35.changes_ref), custom_call_target="tpu_custom_call" | custom-call | tf_op jit(solution)/shard_map/combine/pallas_call | solution.py:530
  (4 shorter events, 0.1 us)
Async XLA Ops:
  1.2 5.5 %collective-permute-start = (f32[6,8,128]{2,1,0:T(8,128)S(1)}, f32[6,8,128]{2,1,0:T(8,128)S(1)}, u32[]{:S(2)}, u32[]{:S(2)}) collective-permute-start(f32[6,8,128]{2,1,0:T(8,128)S(1)} %bitcast.14), channel_id=1, source_target_pairs={{0,1},{1,0},{2,3},{3,2},{4,5},{5,4},{6,7},{7,6},{8,9},{9,8},{10,11... | collective-permute-start | bytes 73736 | tf_op jit(solution)/shard_map/ppermute | solution.py:457
  4.5 2.7 %collective-permute-start.1 = (f32[6,8,128]{2,1,0:T(8,128)S(1)}, f32[6,8,128]{2,1,0:T(8,128)S(1)}, u32[]{:S(2)}, u32[]{:S(2)}) collective-permute-start(f32[6,8,128]{2,1,0:T(8,128)S(1)} %bitcast.13), channel_id=1, source_target_pairs={{0,16},{1,17},{2,18},{3,19},{4,20},{5,21},{6,22},{7,23},{8,24},{9,... | collective-permute-start | bytes 73736 | tf_op jit(solution)/shard_map/ppermute | solution.py:458
  4.5 8.9 %collective-permute-start.4 = (f32[3,16,8,128]{3,2,1,0:T(8,128)S(1)}, f32[3,16,8,128]{3,2,1,0:T(8,128)S(1)}, u32[]{:S(2)}, u32[]{:S(2)}) collective-permute-start(f32[3,16,8,128]{3,2,1,0:T(8,128)S(1)} %bitcast.12), channel_id=1, source_target_pairs={{0,1},{1,0},{2,3},{3,2},{4,5},{5,4},{6,7},{7,6},{8,9},{9,8},{10,11... | collective-permute-start | bytes 589832 | tf_op jit(solution)/shard_map/ppermute | solution.py:459
  5.8 7.7 %collective-permute-start.5 = (f32[3,16,8,128]{3,2,1,0:T(8,128)S(1)}, f32[3,16,8,128]{3,2,1,0:T(8,128)S(1)}, u32[]{:S(2)}, u32[]{:S(2)}) collective-permute-start(f32[3,16,8,128]{3,2,1,0:T(8,128)S(1)} %bitcast.11), channel_id=1, source_target_pairs={{0,16},{1,17},{2,18},{3,19},{4,20},{5,21},{6,22},{7,23},{8,24},{9,... | collective-permute-start | bytes 589832 | tf_op jit(solution)/shard_map/ppermute | solution.py:460
  7.2 6.8 %collective-permute-start.2 = (f32[18,8,128]{2,1,0:T(8,128)S(1)}, f32[18,8,128]{2,1,0:T(8,128)S(1)}, u32[]{:S(2)}, u32[]{:S(2)}) collective-permute-start(f32[18,8,128]{2,1,0:T(8,128)S(1)} %get-tuple-element.25), channel_id=1, source_target_pairs={{0,64},{1,2},{2,1},{3,4},{4,3},{5,6},{6,5},{7,8},{8,7},{9,10},{10,... | collective-permute-start | bytes 221192 | tf_op jit(solution)/shard_map/ppermute | solution.py:470
  10.1 3.9 %collective-permute-start.3 = (f32[18,8,128]{2,1,0:T(8,128)S(1)}, f32[18,8,128]{2,1,0:T(8,128)S(1)}, u32[]{:S(2)}, u32[]{:S(2)}) collective-permute-start(f32[18,8,128]{2,1,0:T(8,128)S(1)} %get-tuple-element.26), channel_id=1, source_target_pairs={{0,1},{1,0},{2,3},{3,2},{4,5},{5,4},{6,7},{7,6},{8,9},{9,8},{10,11... | collective-permute-start | bytes 221192 | tf_op jit(solution)/shard_map/ppermute | solution.py:471
  14.6 1.2 %collective-permute-start.6 = (f32[8,128]{1,0:T(8,128)S(1)}, f32[8,128]{1,0:T(8,128)S(1)}, u32[]{:S(2)}, u32[]{:S(2)}) collective-permute-start(f32[8,128]{1,0:T(8,128)S(1)} %get-tuple-element.37), channel_id=1, source_target_pairs={{0,1},{1,0},{2,3},{3,2},{4,5},{5,4},{6,7},{7,6},{8,9},{9,8},{10,11... | collective-permute-start | bytes 12296 | tf_op jit(solution)/shard_map/ppermute | solution.py:526

commit v10 on v8

--- a/solution.py
+++ b/solution.py
@@ -38,8 +38,7 @@
     u_ref,
     rim_odd_ref,
     rim_even_ref,
-    odd_ref,
-    even_ref,
+    far_ref,
     sens_ref,
     dens_ref,
     arrived,
@@ -72,21 +71,17 @@
                 place = pl.ds(z * layer + row * width + part, 8, width)
                 u_ref[place, :] = value[row : row + 8, part * LANES : (part + 1) * LANES]
 
-    for rim_ref, layers_ref, top in (
-        (rim_odd_ref, odd_ref, slab_odd),
-        (rim_even_ref, even_ref, 1 - slab_odd),
-    ):
+    for rim_ref, top in ((rim_odd_ref, slab_odd), (rim_even_ref, 1 - slab_odd)):
 
         def put(first, count, z, row):
             place = pl.ds(pl.multiple_of(z * layer + row * width, 8), count * width)
             rim_ref[first * width : (first + count) * width, :] = u_ref[place, :]
 
         near, second = (depth - 1) * top, 1 + (depth - 3) * top
-        put(0, 2, near, 0)
-        put(2, 2, near, rows - 2)
-        put(4, 1, second, 0)
-        put(5, 1, second, rows - 1)
-        layers_ref[...] = u_ref[pl.ds(pl.multiple_of(top * layer, 8), SWEEPS * layer), :]
+        put(0, rows, near, 0)
+        put(rows, 1, second, 0)
+        put(rows + 1, 1, second, rows - 1)
+    far_ref[...] = u_ref[layer : (depth - 1) * layer, :]
 
 
 def gram_kernel(
@@ -166,7 +161,7 @@
         start = rows - 3 if top else 0
         for z in range(depth):
             out_ref[3 * z : 3 * z + 3] = u_ref[z, start : start + 3]
-        near, second = (2, 5) if top else (0, 4)
+        near, second = (rows - 2, rows + 1) if top else (0, rows)
         out_ref[12:14] = low_ref[near : near + 2]
         out_ref[14:16] = high_ref[near : near + 2]
         out_ref[16] = low_ref[second]
@@ -220,7 +215,9 @@
     return relax
 
 
-def inner_kernel(u_ref, odd_ref, even_ref, start_ref, one_ref, two_ref, last_ref):
+def inner_kernel(
+    u_ref, rim_odd_ref, rim_even_ref, even_ref, odd_ref, start_ref, one_ref, two_ref, last_ref
+):
     depth, rows, width = u_ref.shape[:3]
     slab_odd = lax.rem(lax.axis_index("slab"), 2)
     inside = grid_ends()
@@ -229,9 +226,12 @@
 
         @pl.when(slab_odd == parity)
         def _():
-            low_ref, high_ref = (even_ref, odd_ref) if parity else (odd_ref, even_ref)
-            start_ref[0:3] = low_ref[...] * inside["low_z"]
-            start_ref[3 + depth :] = high_ref[...] * inside["high_z"]
+            pairs = (rim_odd_ref, odd_ref), (rim_even_ref, even_ref)
+            (low_rim, low_far), (high_rim, high_far) = pairs[::-1] if parity else pairs
+            start_ref[0:2] = low_far[...] * inside["low_z"]
+            start_ref[2] = low_rim[0:rows] * inside["low_z"]
+            start_ref[3 + depth] = high_rim[0:rows] * inside["high_z"]
+            start_ref[4 + depth :] = high_far[...] * inside["high_z"]
 
     relax = line_sweep(width, depth, rows, inside)
 
@@ -430,17 +430,17 @@
     depth, rows, cols = shape
     like = jax.ShapeDtypeStruct
     width = cols // LANES
-    lines, layers, rim = (
-        like((count * width, LANES), F32) for count in (depth * rows, SWEEPS * rows, 6)
+    lines, far, rim = (
+        like((count * width, LANES), F32) for count in (depth * rows, 2 * rows, rows + 2)
     )
     edges = like((3 * depth + 6, width, LANES), F32)
     devices = lax.axis_size("slab") * lax.axis_size("tile")
 
-    u, rim_odd, rim_even, odd, even = pl.pallas_call(
+    u, rim_odd, rim_even, far = pl.pallas_call(
         weight_kernel,
-        out_shape=(lines, rim, rim, layers, layers),
+        out_shape=(lines, rim, rim, far),
         in_specs=[HBM] * 2,
-        out_specs=[VMEM] * 5,
+        out_specs=[VMEM] * 4,
         scratch_shapes=[
             pltpu.VMEM(shape, F32),
             pltpu.VMEM(shape, F32),
@@ -451,14 +451,16 @@
     )(in_hbm(sensitivity), in_hbm(filtered_density))
 
     u = u.reshape(depth, rows, width, LANES)
-    rim_odd, rim_even = (array.reshape(6, width, LANES) for array in (rim_odd, rim_even))
-    odd, even = (array.reshape(SWEEPS, rows, width, LANES) for array in (odd, even))
+    rim_odd, rim_even = (
+        array.reshape(rows + 2, width, LANES) for array in (rim_odd, rim_even)
+    )
+    far = far.reshape(2, rows, width, LANES)
 
     slab_odd, slab_even, tile_odd, tile_even = swaps()
     rim_odd = lax.ppermute(rim_odd, MESH_AXES, slab_odd)
     rim_even = lax.ppermute(rim_even, MESH_AXES, slab_even)
-    odd = lax.ppermute(odd, MESH_AXES, slab_odd)
-    even = lax.ppermute(even, MESH_AXES, slab_even)
+    odd = lax.ppermute(far, MESH_AXES, slab_odd)
+    even = lax.ppermute(far, MESH_AXES, slab_even)
 
     row_odd, row_even = pl.pallas_call(
         pack_kernel,
@@ -496,11 +498,11 @@
     inner = pl.pallas_call(
         inner_kernel,
         out_shape=(field, field, field, lines),
-        in_specs=[VMEM] * 3,
+        in_specs=[VMEM] * 5,
         out_specs=[VMEM] * 4,
         compiler_params=kernel_params(8),
         name="inner",
-    )(u, odd, even)
+    )(u, rim_odd, rim_even, even, odd)
 
     padded = pltpu.VMEM((depth + 6, rows + 6, width, LANES), F32)
     gradient, line = pl.pallas_call(

time: 42.4 us -> 43.4 us (1.024)
  waiting for transfers between devices: 0.57 us -> 1.7 us
    ppermute x1, starting transfers between devices: 2.86 us -> 1.73 us  [per_device(): row_odd = lax.ppermute(row_odd, MESH_AXES, tile_odd)]
    ppermute x1, waiting for transfers between devices: 0.55 us -> 1.69 us  [per_device(): rim_even = lax.ppermute(rim_even, MESH_AXES, slab_even)]
    ppermute x1, starting transfers between devices: 1.11 us -> 2.16 us  [per_device(): row_even = lax.ppermute(row_even, MESH_AXES, tile_even)]
  transfers between devices with their start and end apart: 6 -> 6, of which waited for: 1 -> 1; matrix products, arithmetic and copies ran while one was open for 0% -> 0% of each run, Pallas kernels for 7% -> 6%
where the time goes in v10:
time: 43.4 us; the launch traced here: 43.2 us
  blocking collectives  26.6 us (61%)
  starting transfers between devices  9.36 us (22%)
  Pallas kernels  5.51 us (13%)
  waiting for transfers between devices  1.7 us (4%)
    all_to_all x1, blocking collectives, per_device(): received = lax.all_to_all(line, MESH_AXES, 0, 0, tiled=True)  26.6 us
    ppermute x1, starting transfers between devices, per_device(): rim_odd = lax.ppermute(rim_odd, MESH_AXES, slab_odd)  3.33 us
    pallas_call x1, Pallas kernels, per_device(): pl.pallas_call(gram_kernel, out_shape=(like((SUMS, LANES), F32), like((de...  2.2 us
    ppermute x1, starting transfers between devices, per_device(): row_even = lax.ppermute(row_even, MESH_AXES, tile_even)  2.16 us
    ppermute x1, starting transfers between devices, per_device(): row_odd = lax.ppermute(row_odd, MESH_AXES, tile_odd)  1.73 us
    ppermute x1, waiting for transfers between devices, per_device(): rim_even = lax.ppermute(rim_even, MESH_AXES, slab_even)  1.69 us
    ppermute x1, starting transfers between devices, per_device(): odd = lax.ppermute(far, MESH_AXES, slab_odd)  1.24 us
    pallas_call x1, Pallas kernels, per_device(): pl.pallas_call(weight_kernel, out_shape=(lines, rim, rim, far), in_specs=...  1.17 us
  transfers between devices with their start and end apart: 6, of which 1 were waited for; matrix products, arithmetic and copies ran while one was open for 0% of the time, Pallas kernels for 6%

profile of v10, /device:TPU:1, one launch (start us, length us, event | category | flops | bytes accessed | tf_op | source)
XLA Modules:
  0.0 43.2 jit_solution(16149819180031054566)
XLA Ops:
  0.0 1.2 %weights.1 = (f32[512,128]{1,0:T(8,128)S(1)}, f32[144,128]{1,0:T(8,128)S(1)}, f32[144,128]{1,0:T(8,128)S(1)}, f32[256,128]{1,0:T(8,128)S(1)}) custom-call(f32[4,16,1024]{2,1,0:T(8,128)} %sens_hbm.1, f32[4,16,1024]{2,1,0:T(8,128)} %dens_hbm.1), custom_call_target="tpu_custom_call" | custom-call | tf_op jit(solution)/shard_map/weights/pallas_call | solution.py:439
  1.2 3.3 %collective-permute-start = (f32[18,8,128]{2,1,0:T(8,128)S(1)}, f32[18,8,128]{2,1,0:T(8,128)S(1)}, u32[]{:S(2)}, u32[]{:S(2)}) collective-permute-start(f32[18,8,128]{2,1,0:T(8,128)S(1)} %bitcast.15), channel_id=1, source_target_pairs={{0,1},{1,0},{2,3},{3,2},{4,5},{5,4},{6,7},{7,6},{8,9},{9,8},{10,11... | collective-permute-start | bytes 221192 | tf_op jit(solution)/shard_map/ppermute | solution.py:460
  4.5 0.0 collective-permute-start.1
  4.5 1.2 %collective-permute-start.5 = (f32[2,16,8,128]{3,2,1,0:T(8,128)S(1)}, f32[2,16,8,128]{3,2,1,0:T(8,128)S(1)}, u32[]{:S(2)}, u32[]{:S(2)}) collective-permute-start(f32[2,16,8,128]{3,2,1,0:T(8,128)S(1)} %bitcast.12), channel_id=1, source_target_pairs={{0,1},{1,0},{2,3},{3,2},{4,5},{5,4},{6,7},{7,6},{8,9},{9,8},{10,11... | collective-permute-start | bytes 393224 | tf_op jit(solution)/shard_map/ppermute | solution.py:462
  5.8 0.9 %collective-permute-start.4 = (f32[2,16,8,128]{3,2,1,0:T(8,128)S(1)}, f32[2,16,8,128]{3,2,1,0:T(8,128)S(1)}, u32[]{:S(2)}, u32[]{:S(2)}) collective-permute-start(f32[2,16,8,128]{3,2,1,0:T(8,128)S(1)} %bitcast.13), channel_id=1, source_target_pairs={{0,16},{1,17},{2,18},{3,19},{4,20},{5,21},{6,22},{7,23},{8,24},{9,... | collective-permute-start | bytes 393224 | tf_op jit(solution)/shard_map/ppermute | solution.py:463
  6.6 0.0 collective-permute-done.odd_ref.rim_odd_ref
  6.6 1.7 %collective-permute-done.1.even_ref.rim_even_ref = f32[18,8,128]{2,1,0:T(8,128)S(1)} collective-permute-done((f32[18,8,128]{2,1,0:T(8,128)S(1)}, f32[18,8,128]{2,1,0:T(8,128)S(1)}, u32[]{:S(2)}, u32[]{:S(2)}) %collective-permute-start.1) | collective-permute-done | bytes 73760 | tf_op jit(solution)/shard_map/ppermute | solution.py:461
  8.4 1.7 %collective-permute-start.2 = (f32[18,8,128]{2,1,0:T(8,128)S(1)}, f32[18,8,128]{2,1,0:T(8,128)S(1)}, u32[]{:S(2)}, u32[]{:S(2)}) collective-permute-start(f32[18,8,128]{2,1,0:T(8,128)S(1)} %get-tuple-element.24), channel_id=1, source_target_pairs={{0,64},{1,2},{2,1},{3,4},{4,3},{5,6},{6,5},{7,8},{8,7},{9,10},{10,... | collective-permute-start | bytes 221192 | tf_op jit(solution)/shard_map/ppermute | solution.py:473
  10.1 2.2 %collective-permute-start.3 = (f32[18,8,128]{2,1,0:T(8,128)S(1)}, f32[18,8,128]{2,1,0:T(8,128)S(1)}, u32[]{:S(2)}, u32[]{:S(2)}) collective-permute-start(f32[18,8,128]{2,1,0:T(8,128)S(1)} %get-tuple-element.25), channel_id=1, source_target_pairs={{0,1},{1,0},{2,3},{3,2},{4,5},{5,4},{6,7},{7,6},{8,9},{9,8},{10,11... | collective-permute-start | bytes 221192 | tf_op jit(solution)/shard_map/ppermute | solution.py:474
  12.3 2.2 %gram.1 = (f32[32,128]{1,0:T(8,128)S(1)}, f32[2,16,1024]{2,1,0:T(8,128)S(1)}, f32[4,4,16,1024]{3,2,1,0:T(8,128)S(1)}, f32[4,4,16,1024]{3,2,1,0:T(8,128)S(1)}) custom-call(f32[4,4,16,1024]{3,2,1,0:T(8,128)} %steps_hbm.1, f32[4,4,16,1024]{3,2,1,0:T(8,128)} %changes_hbm.1, s32[2,8,512]{2,1,0:T(8,128)} %passive_hbm.1), custom_call_target="tpu_custom_call" | custom-call | flops 8000000000 | bytes 43000000 | tf_op jit(solution)/shard_map/gram/pallas_call | solution.py:477
  14.5 0.0 collective-permute-done.5.odd_ref
  14.5 0.0 collective-permute-done.4.even_ref
  14.5 0.6 %inner.1 = (f32[10,16,8,128]{3,2,1,0:T(8,128)S(1)}, f32[10,16,8,128]{3,2,1,0:T(8,128)S(1)}, f32[10,16,8,128]{3,2,1,0:T(8,128)S(1)}, f32[512,128]{1,0:T(8,128)S(1)}) custom-call(f32[4,16,8,128]{3,2,1,0:T(8,128)S(1)} %bitcast.9, f32[18,8,128]{2,1,0:T(8,128)S(1)} %collective-permute-done.odd_ref.rim_odd_ref, ...), custom_call_target="tpu_custom_call" | custom-call | tf_op jit(solution)/shard_map/inner/pallas_call | solution.py:498
  15.1 0.0 collective-permute-done.2.row_odd_ref
  15.1 0.0 collective-permute-done.3.row_even_ref
  15.1 0.6 %outer.1 = (f32[4,16,1024]{2,1,0:T(8,128)S(1)}, f32[256,128]{1,0:T(8,128)S(1)}) custom-call(f32[18,8,128]{2,1,0:T(8,128)S(1)} %collective-permute-done.2.row_odd_ref, f32[18,8,128]{2,1,0:T(8,128)S(1)} %collective-permute-done.3.row_even_ref, f32[10,16,8,128]{3,2,1,0:T(8,128)S(1)} %get-tuple-element.27.inner_start_ref, ...), custom_call_target="tpu_custom_call" | custom-call | tf_op jit(solution)/shard_map/outer/pallas_call | solution.py:508
  15.7 26.6 %all_to_all.11 = f32[256,1,128]{2,1,0:T(1,128)S(1)} all-to-all(f32[256,1,128]{2,1,0:T(1,128)S(1)} %bitcast.11), channel_id=1, replica_groups=mesh['slab'=16,'tile'=16] {'slab','tile'}, dimensions={0} | all-to-all | bytes 262144 | tf_op jit(solution)/shard_map/all_to_all | solution.py:524
  42.3 0.9 %combine.1 = f32[4,16,1024]{2,1,0:T(8,128)} custom-call(f32[256,128]{1,0:T(8,128)S(1)} %bitcast.10, f32[4,16,1024]{2,1,0:T(8,128)S(1)} %get-tuple-element.36.grad_ref, f32[4,4,16,1024]{3,2,1,0:T(8,128)S(1)} %get-tuple-element.32.steps_ref, f32[4,4,16,1024]{3,2,1,0:T(8,128)S(1)} %get-tuple-element.33.changes_ref), custom_call_target="tpu_custom_call" | custom-call | tf_op jit(solution)/shard_map/combine/pallas_call | solution.py:526
  (1 shorter events, 0.0 us)
Async XLA Ops:
  1.2 5.5 %collective-permute-start = (f32[18,8,128]{2,1,0:T(8,128)S(1)}, f32[18,8,128]{2,1,0:T(8,128)S(1)}, u32[]{:S(2)}, u32[]{:S(2)}) collective-permute-start(f32[18,8,128]{2,1,0:T(8,128)S(1)} %bitcast.15), channel_id=1, source_target_pairs={{0,1},{1,0},{2,3},{3,2},{4,5},{5,4},{6,7},{7,6},{8,9},{9,8},{10,11... | collective-permute-start | bytes 221192 | tf_op jit(solution)/shard_map/ppermute | solution.py:460
  4.5 3.8 %collective-permute-start.1 = (f32[18,8,128]{2,1,0:T(8,128)S(1)}, f32[18,8,128]{2,1,0:T(8,128)S(1)}, u32[]{:S(2)}, u32[]{:S(2)}) collective-permute-start(f32[18,8,128]{2,1,0:T(8,128)S(1)} %bitcast.14), channel_id=1, source_target_pairs={{0,16},{1,17},{2,18},{3,19},{4,20},{5,21},{6,22},{7,23},{8,24},{9,... | collective-permute-start | bytes 221192 | tf_op jit(solution)/shard_map/ppermute | solution.py:461
  4.5 9.9 %collective-permute-start.5 = (f32[2,16,8,128]{3,2,1,0:T(8,128)S(1)}, f32[2,16,8,128]{3,2,1,0:T(8,128)S(1)}, u32[]{:S(2)}, u32[]{:S(2)}) collective-permute-start(f32[2,16,8,128]{3,2,1,0:T(8,128)S(1)} %bitcast.12), channel_id=1, source_target_pairs={{0,1},{1,0},{2,3},{3,2},{4,5},{5,4},{6,7},{7,6},{8,9},{9,8},{10,11... | collective-permute-start | bytes 393224 | tf_op jit(solution)/shard_map/ppermute | solution.py:462
  5.8 8.7 %collective-permute-start.4 = (f32[2,16,8,128]{3,2,1,0:T(8,128)S(1)}, f32[2,16,8,128]{3,2,1,0:T(8,128)S(1)}, u32[]{:S(2)}, u32[]{:S(2)}) collective-permute-start(f32[2,16,8,128]{3,2,1,0:T(8,128)S(1)} %bitcast.13), channel_id=1, source_target_pairs={{0,16},{1,17},{2,18},{3,19},{4,20},{5,21},{6,22},{7,23},{8,24},{9,... | collective-permute-start | bytes 393224 | tf_op jit(solution)/shard_map/ppermute | solution.py:463
  8.4 6.7 %collective-permute-start.2 = (f32[18,8,128]{2,1,0:T(8,128)S(1)}, f32[18,8,128]{2,1,0:T(8,128)S(1)}, u32[]{:S(2)}, u32[]{:S(2)}) collective-permute-start(f32[18,8,128]{2,1,0:T(8,128)S(1)} %get-tuple-element.24), channel_id=1, source_target_pairs={{0,64},{1,2},{2,1},{3,4},{4,3},{5,6},{6,5},{7,8},{8,7},{9,10},{10,... | collective-permute-start | bytes 221192 | tf_op jit(solution)/shard_map/ppermute | solution.py:473
  10.1 5.0 %collective-permute-start.3 = (f32[18,8,128]{2,1,0:T(8,128)S(1)}, f32[18,8,128]{2,1,0:T(8,128)S(1)}, u32[]{:S(2)}, u32[]{:S(2)}) collective-permute-start(f32[18,8,128]{2,1,0:T(8,128)S(1)} %get-tuple-element.25), channel_id=1, source_target_pairs={{0,1},{1,0},{2,3},{3,2},{4,5},{5,4},{6,7},{7,6},{8,9},{9,8},{10,11... | collective-permute-start | bytes 221192 | tf_op jit(solution)/shard_map/ppermute | solution.py:474

commit v11 on v10

--- a/solution.py
+++ b/solution.py
@@ -216,7 +216,7 @@
 
 
 def inner_kernel(
-    u_ref, rim_odd_ref, rim_even_ref, even_ref, odd_ref, start_ref, one_ref, two_ref, last_ref
+    u_ref, rim_odd_ref, rim_even_ref, odd_ref, even_ref, start_ref, one_ref, two_ref, last_ref
 ):
     depth, rows, width = u_ref.shape[:3]
     slab_odd = lax.rem(lax.axis_index("slab"), 2)
@@ -502,7 +502,7 @@
         out_specs=[VMEM] * 4,
         compiler_params=kernel_params(8),
         name="inner",
-    )(u, rim_odd, rim_even, even, odd)
+    )(u, rim_odd, rim_even, odd, even)
 
     padded = pltpu.VMEM((depth + 6, rows + 6, width, LANES), F32)
     gradient, line = pl.pallas_call(

time: 43.4 us -> 42.6 us (0.982)
  blocking collectives: 26.6 us -> 25.8 us
    all_to_all x1, blocking collectives: 26.6 us -> 25.8 us  [per_device(): received = lax.all_to_all(line, MESH_AXES, 0, 0, tiled=True)]
    ppermute x1, starting transfers between devices: 1.24 us -> 0.64 us  [per_device(): odd = lax.ppermute(far, MESH_AXES, slab_odd)]
    ppermute x1, starting transfers between devices: 0.89 us -> 1.47 us  [per_device(): even = lax.ppermute(far, MESH_AXES, slab_even)]
  transfers between devices with their start and end apart: 6 -> 6, of which waited for: 1 -> 1; matrix products, arithmetic and copies ran while one was open for 0% -> 0% of each run, Pallas kernels for 6% -> 7%
where the time goes in v11:
time: 42.6 us; the launch traced here: 42.4 us
  blocking collectives  25.8 us (61%)
  starting transfers between devices  9.34 us (22%)
  Pallas kernels  5.51 us (13%)
  waiting for transfers between devices  1.71 us (4%)
    all_to_all x1, blocking collectives, per_device(): received = lax.all_to_all(line, MESH_AXES, 0, 0, tiled=True)  25.8 us
    ppermute x1, starting transfers between devices, per_device(): rim_odd = lax.ppermute(rim_odd, MESH_AXES, slab_odd)  3.33 us
    pallas_call x1, Pallas kernels, per_device(): pl.pallas_call(gram_kernel, out_shape=(like((SUMS, LANES), F32), like((de...  2.2 us
    ppermute x1, starting transfers between devices, per_device(): row_even = lax.ppermute(row_even, MESH_AXES, tile_even)  2.06 us
    ppermute x1, starting transfers between devices, per_device(): row_odd = lax.ppermute(row_odd, MESH_AXES, tile_odd)  1.82 us
    ppermute x1, waiting for transfers between devices, per_device(): rim_even = lax.ppermute(rim_even, MESH_AXES, slab_even)  1.7 us
    ppermute x1, starting transfers between devices, per_device(): even = lax.ppermute(far, MESH_AXES, slab_even)  1.47 us
    pallas_call x1, Pallas kernels, per_device(): pl.pallas_call(weight_kernel, out_shape=(lines, rim, rim, far), in_specs=...  1.17 us
  transfers between devices with their start and end apart: 6, of which 1 were waited for; matrix products, arithmetic and copies ran while one was open for 0% of the time, Pallas kernels for 7%

profile of v11, /device:TPU:1, one launch (start us, length us, event | category | flops | bytes accessed | tf_op | source)
XLA Modules:
  0.0 42.4 jit_solution(7140676437127911877)
XLA Ops:
  0.0 1.2 %weights.1 = (f32[512,128]{1,0:T(8,128)S(1)}, f32[144,128]{1,0:T(8,128)S(1)}, f32[144,128]{1,0:T(8,128)S(1)}, f32[256,128]{1,0:T(8,128)S(1)}) custom-call(f32[4,16,1024]{2,1,0:T(8,128)} %sens_hbm.1, f32[4,16,1024]{2,1,0:T(8,128)} %dens_hbm.1), custom_call_target="tpu_custom_call" | custom-call | tf_op jit(solution)/shard_map/weights/pallas_call | solution.py:439
  1.2 3.3 %collective-permute-start = (f32[18,8,128]{2,1,0:T(8,128)S(1)}, f32[18,8,128]{2,1,0:T(8,128)S(1)}, u32[]{:S(2)}, u32[]{:S(2)}) collective-permute-start(f32[18,8,128]{2,1,0:T(8,128)S(1)} %bitcast.15), channel_id=1, source_target_pairs={{0,1},{1,0},{2,3},{3,2},{4,5},{5,4},{6,7},{7,6},{8,9},{9,8},{10,11... | collective-permute-start | bytes 221192 | tf_op jit(solution)/shard_map/ppermute | solution.py:460
  4.5 0.0 collective-permute-start.1
  4.5 1.5 %collective-permute-start.5 = (f32[2,16,8,128]{3,2,1,0:T(8,128)S(1)}, f32[2,16,8,128]{3,2,1,0:T(8,128)S(1)}, u32[]{:S(2)}, u32[]{:S(2)}) collective-permute-start(f32[2,16,8,128]{3,2,1,0:T(8,128)S(1)} %bitcast.12), channel_id=1, source_target_pairs={{0,16},{1,17},{2,18},{3,19},{4,20},{5,21},{6,22},{7,23},{8,24},{9,... | collective-permute-start | bytes 393224 | tf_op jit(solution)/shard_map/ppermute | solution.py:463
  6.0 0.6 %collective-permute-start.4 = (f32[2,16,8,128]{3,2,1,0:T(8,128)S(1)}, f32[2,16,8,128]{3,2,1,0:T(8,128)S(1)}, u32[]{:S(2)}, u32[]{:S(2)}) collective-permute-start(f32[2,16,8,128]{3,2,1,0:T(8,128)S(1)} %bitcast.13), channel_id=1, source_target_pairs={{0,1},{1,0},{2,3},{3,2},{4,5},{5,4},{6,7},{7,6},{8,9},{9,8},{10,11... | collective-permute-start | bytes 393224 | tf_op jit(solution)/shard_map/ppermute | solution.py:462
  6.6 0.0 collective-permute-done.odd_ref.rim_odd_ref
  6.6 1.7 %collective-permute-done.1.even_ref.rim_even_ref = f32[18,8,128]{2,1,0:T(8,128)S(1)} collective-permute-done((f32[18,8,128]{2,1,0:T(8,128)S(1)}, f32[18,8,128]{2,1,0:T(8,128)S(1)}, u32[]{:S(2)}, u32[]{:S(2)}) %collective-permute-start.1) | collective-permute-done | bytes 73760 | tf_op jit(solution)/shard_map/ppermute | solution.py:461
  8.4 1.8 %collective-permute-start.2 = (f32[18,8,128]{2,1,0:T(8,128)S(1)}, f32[18,8,128]{2,1,0:T(8,128)S(1)}, u32[]{:S(2)}, u32[]{:S(2)}) collective-permute-start(f32[18,8,128]{2,1,0:T(8,128)S(1)} %get-tuple-element.24), channel_id=1, source_target_pairs={{0,64},{1,2},{2,1},{3,4},{4,3},{5,6},{6,5},{7,8},{8,7},{9,10},{10,... | collective-permute-start | bytes 221192 | tf_op jit(solution)/shard_map/ppermute | solution.py:473
  10.2 2.1 %collective-permute-start.3 = (f32[18,8,128]{2,1,0:T(8,128)S(1)}, f32[18,8,128]{2,1,0:T(8,128)S(1)}, u32[]{:S(2)}, u32[]{:S(2)}) collective-permute-start(f32[18,8,128]{2,1,0:T(8,128)S(1)} %get-tuple-element.25), channel_id=1, source_target_pairs={{0,1},{1,0},{2,3},{3,2},{4,5},{5,4},{6,7},{7,6},{8,9},{9,8},{10,11... | collective-permute-start | bytes 221192 | tf_op jit(solution)/shard_map/ppermute | solution.py:474
  12.2 2.2 %gram.1 = (f32[32,128]{1,0:T(8,128)S(1)}, f32[2,16,1024]{2,1,0:T(8,128)S(1)}, f32[4,4,16,1024]{3,2,1,0:T(8,128)S(1)}, f32[4,4,16,1024]{3,2,1,0:T(8,128)S(1)}) custom-call(f32[4,4,16,1024]{3,2,1,0:T(8,128)} %steps_hbm.1, f32[4,4,16,1024]{3,2,1,0:T(8,128)} %changes_hbm.1, s32[2,8,512]{2,1,0:T(8,128)} %passive_hbm.1), custom_call_target="tpu_custom_call" | custom-call | flops 8000000000 | bytes 43000000 | tf_op jit(solution)/shard_map/gram/pallas_call | solution.py:477
  14.4 0.0 collective-permute-done.5.even_ref
  14.5 0.0 collective-permute-done.4.odd_ref
  14.5 0.6 %inner.1 = (f32[10,16,8,128]{3,2,1,0:T(8,128)S(1)}, f32[10,16,8,128]{3,2,1,0:T(8,128)S(1)}, f32[10,16,8,128]{3,2,1,0:T(8,128)S(1)}, f32[512,128]{1,0:T(8,128)S(1)}) custom-call(f32[4,16,8,128]{3,2,1,0:T(8,128)S(1)} %bitcast.9, f32[18,8,128]{2,1,0:T(8,128)S(1)} %collective-permute-done.odd_ref.rim_odd_ref, ...), custom_call_target="tpu_custom_call" | custom-call | tf_op jit(solution)/shard_map/inner/pallas_call | solution.py:498
  15.1 0.0 collective-permute-done.2.row_odd_ref
  15.1 0.0 collective-permute-done.3.row_even_ref
  15.1 0.6 %outer.1 = (f32[4,16,1024]{2,1,0:T(8,128)S(1)}, f32[256,128]{1,0:T(8,128)S(1)}) custom-call(f32[18,8,128]{2,1,0:T(8,128)S(1)} %collective-permute-done.2.row_odd_ref, f32[18,8,128]{2,1,0:T(8,128)S(1)} %collective-permute-done.3.row_even_ref, f32[10,16,8,128]{3,2,1,0:T(8,128)S(1)} %get-tuple-element.27.inner_start_ref, ...), custom_call_target="tpu_custom_call" | custom-call | tf_op jit(solution)/shard_map/outer/pallas_call | solution.py:508
  15.7 25.8 %all_to_all.11 = f32[256,1,128]{2,1,0:T(1,128)S(1)} all-to-all(f32[256,1,128]{2,1,0:T(1,128)S(1)} %bitcast.11), channel_id=1, replica_groups=mesh['slab'=16,'tile'=16] {'slab','tile'}, dimensions={0} | all-to-all | bytes 262144 | tf_op jit(solution)/shard_map/all_to_all | solution.py:524
  41.5 0.9 %combine.1 = f32[4,16,1024]{2,1,0:T(8,128)} custom-call(f32[256,128]{1,0:T(8,128)S(1)} %bitcast.10, f32[4,16,1024]{2,1,0:T(8,128)S(1)} %get-tuple-element.36.grad_ref, f32[4,4,16,1024]{3,2,1,0:T(8,128)S(1)} %get-tuple-element.32.steps_ref, f32[4,4,16,1024]{3,2,1,0:T(8,128)S(1)} %get-tuple-element.33.changes_ref), custom_call_target="tpu_custom_call" | custom-call | tf_op jit(solution)/shard_map/combine/pallas_call | solution.py:526
  (1 shorter events, 0.0 us)
Async XLA Ops:
  1.2 5.5 %collective-permute-start = (f32[18,8,128]{2,1,0:T(8,128)S(1)}, f32[18,8,128]{2,1,0:T(8,128)S(1)}, u32[]{:S(2)}, u32[]{:S(2)}) collective-permute-start(f32[18,8,128]{2,1,0:T(8,128)S(1)} %bitcast.15), channel_id=1, source_target_pairs={{0,1},{1,0},{2,3},{3,2},{4,5},{5,4},{6,7},{7,6},{8,9},{9,8},{10,11... | collective-permute-start | bytes 221192 | tf_op jit(solution)/shard_map/ppermute | solution.py:460
  4.5 3.8 %collective-permute-start.1 = (f32[18,8,128]{2,1,0:T(8,128)S(1)}, f32[18,8,128]{2,1,0:T(8,128)S(1)}, u32[]{:S(2)}, u32[]{:S(2)}) collective-permute-start(f32[18,8,128]{2,1,0:T(8,128)S(1)} %bitcast.14), channel_id=1, source_target_pairs={{0,16},{1,17},{2,18},{3,19},{4,20},{5,21},{6,22},{7,23},{8,24},{9,... | collective-permute-start | bytes 221192 | tf_op jit(solution)/shard_map/ppermute | solution.py:461
  4.5 9.9 %collective-permute-start.5 = (f32[2,16,8,128]{3,2,1,0:T(8,128)S(1)}, f32[2,16,8,128]{3,2,1,0:T(8,128)S(1)}, u32[]{:S(2)}, u32[]{:S(2)}) collective-permute-start(f32[2,16,8,128]{3,2,1,0:T(8,128)S(1)} %bitcast.12), channel_id=1, source_target_pairs={{0,16},{1,17},{2,18},{3,19},{4,20},{5,21},{6,22},{7,23},{8,24},{9,... | collective-permute-start | bytes 393224 | tf_op jit(solution)/shard_map/ppermute | solution.py:463
  6.0 8.5 %collective-permute-start.4 = (f32[2,16,8,128]{3,2,1,0:T(8,128)S(1)}, f32[2,16,8,128]{3,2,1,0:T(8,128)S(1)}, u32[]{:S(2)}, u32[]{:S(2)}) collective-permute-start(f32[2,16,8,128]{3,2,1,0:T(8,128)S(1)} %bitcast.13), channel_id=1, source_target_pairs={{0,1},{1,0},{2,3},{3,2},{4,5},{5,4},{6,7},{7,6},{8,9},{9,8},{10,11... | collective-permute-start | bytes 393224 | tf_op jit(solution)/shard_map/ppermute | solution.py:462
  8.4 6.7 %collective-permute-start.2 = (f32[18,8,128]{2,1,0:T(8,128)S(1)}, f32[18,8,128]{2,1,0:T(8,128)S(1)}, u32[]{:S(2)}, u32[]{:S(2)}) collective-permute-start(f32[18,8,128]{2,1,0:T(8,128)S(1)} %get-tuple-element.24), channel_id=1, source_target_pairs={{0,64},{1,2},{2,1},{3,4},{4,3},{5,6},{6,5},{7,8},{8,7},{9,10},{10,... | collective-permute-start | bytes 221192 | tf_op jit(solution)/shard_map/ppermute | solution.py:473
  10.2 4.9 %collective-permute-start.3 = (f32[18,8,128]{2,1,0:T(8,128)S(1)}, f32[18,8,128]{2,1,0:T(8,128)S(1)}, u32[]{:S(2)}, u32[]{:S(2)}) collective-permute-start(f32[18,8,128]{2,1,0:T(8,128)S(1)} %get-tuple-element.25), channel_id=1, source_target_pairs={{0,1},{1,0},{2,3},{3,2},{4,5},{5,4},{6,7},{7,6},{8,9},{9,8},{10,11... | collective-permute-start | bytes 221192 | tf_op jit(solution)/shard_map/ppermute | solution.py:474

commit v12 on v8

--- a/solution.py
+++ b/solution.py
@@ -89,40 +89,14 @@
         layers_ref[...] = u_ref[pl.ds(pl.multiple_of(top * layer, 8), SWEEPS * layer), :]
 
 
-def gram_kernel(
-    steps_hbm,
-    changes_hbm,
-    passive_hbm,
-    sums_ref,
-    keep_ref,
-    steps_ref,
-    changes_ref,
-    passive_ref,
-    arrived,
-    passive_arrived,
-):
+def gram_kernel(steps_ref, changes_ref, passive_ref, sums_ref, keep_ref):
     depth, rows, cols = steps_ref.shape[1:]
-    passive_copy = pltpu.make_async_copy(passive_hbm, passive_ref, passive_arrived)
-    copies = [
-        [
-            pltpu.make_async_copy(from_ref.at[:, z], to_ref.at[:, z], arrived.at[n, z])
-            for n, (from_ref, to_ref) in enumerate(
-                ((steps_hbm, steps_ref), (changes_hbm, changes_ref))
-            )
-        ]
-        for z in range(depth)
-    ]
-    passive_copy.start()
-    for pair in copies:
-        for copy in pair:
-            copy.start()
 
     def doubling(shape, dim):
         place = lax.broadcasted_iota(jnp.int32, shape, dim) // 2
         matches = place == lax.broadcasted_iota(jnp.int32, shape, 1 - dim)
         return matches.astype(F32).astype(jnp.bfloat16)
 
-    passive_copy.wait()
     half_rows = passive_ref.shape[1]
     twice_rows = doubling((2 * half_rows, half_rows), 0)
     twice_cols = doubling((LANES, 2 * LANES), 1)
@@ -137,8 +111,6 @@
 
     sums = (jnp.zeros((8, LANES), F32),) * (2 * len(PAIRS))
     for z in range(depth):
-        for copy in copies[z]:
-            copy.wait()
 
         def step(block, sums):
             row = pl.ds(pl.multiple_of(block * 8, 8), 8)
@@ -466,31 +438,25 @@
         in_specs=[VMEM] * 3,
         out_specs=[VMEM] * 2,
         compiler_params=kernel_params(8),
+        cost_estimate=pl.CostEstimate(
+            flops=8_000_000_000, bytes_accessed=43_000_000, transcendentals=0
+        ),
         name="edges",
     )(u, rim_odd, rim_even)
     row_odd = lax.ppermute(row_odd, MESH_AXES, tile_odd)
     row_even = lax.ppermute(row_even, MESH_AXES, tile_even)
 
-    history = like(history_steps.shape, F32)
-    sums, keep, steps, changes = pl.pallas_call(
+    sums, keep = pl.pallas_call(
         gram_kernel,
-        out_shape=(
-            like((SUMS, LANES), F32),
-            like((depth // 2, rows, cols), F32),
-            history,
-            history,
+        out_shape=(like((SUMS, LANES), F32), like((depth // 2, rows, cols), F32)),
+        in_specs=[VMEM] * 3,
+        out_specs=[VMEM] * 2,
+        compiler_params=kernel_params(8),
+        cost_estimate=pl.CostEstimate(
+            flops=8_000_000_000, bytes_accessed=43_000_000, transcendentals=0
         ),
-        in_specs=[HBM] * 3,
-        out_specs=[VMEM] * 4,
-        scratch_shapes=[
-            pltpu.VMEM(passive_blocks.shape, jnp.int32),
-            pltpu.SemaphoreType.DMA((2, depth)),
-            pltpu.SemaphoreType.DMA,
-        ],
-        compiler_params=kernel_params(8),
-        cost_estimate=pl.CostEstimate(flops=8_000_000_000, bytes_accessed=43_000_000, transcendentals=0),
         name="gram",
-    )(in_hbm(history_steps), in_hbm(history_changes), in_hbm(passive_blocks))
+    )(history_steps, history_changes, passive_blocks)
 
     field = like((depth + 6, rows, width, LANES), F32)
     inner = pl.pallas_call(
@@ -517,7 +483,7 @@
         ],
         compiler_params=kernel_params(16),
         name="outer",
-    )(row_odd, row_even, *inner, keep, steps, changes, sums)
+    )(row_odd, row_even, *inner, keep, history_steps, history_changes, sums)
 
     received = lax.all_to_all(line, MESH_AXES, 0, 0, tiled=True)
 
@@ -529,7 +495,7 @@
         scratch_shapes=[pltpu.VMEM(shape, F32), pltpu.SemaphoreType.DMA((depth,))],
         compiler_params=kernel_params(8),
         name="combine",
-    )(received, gradient, steps, changes)
+    )(received, gradient, history_steps, history_changes)
 
 
 def solution(mesh):

time: 42.4 us -> 42.4 us (level)
  Pallas kernels: 5.52 us -> 4.12 us
  blocking collectives: 26.6 us -> 28 us
    all_to_all x1, blocking collectives: 26.6 us -> 28 us  [per_device(): received = lax.all_to_all(line, MESH_AXES, 0, 0, tiled=True)]
    pallas_call x1, Pallas kernels: 2.2 us -> 0.8 us  [per_device(): pl.pallas_call(gram_kernel, out_shape=(like((SUMS, LANES), F32), like((de...]
  transfers between devices with their start and end apart: 6 -> 6, of which waited for: 1 -> 1; matrix products, arithmetic and copies ran while one was open for 0% -> 0% of each run, Pallas kernels for 7% -> 3%
where the time goes in v12:
time: 42.4 us; the launch traced here: 42.2 us
  blocking collectives  28 us (66%)
  starting transfers between devices  9.44 us (22%)
  Pallas kernels  4.12 us (10%)
  waiting for transfers between devices  0.57 us (1%)
    all_to_all x1, blocking collectives, per_device(): received = lax.all_to_all(line, MESH_AXES, 0, 0, tiled=True)  28 us
    ppermute x1, starting transfers between devices, per_device(): rim_odd = lax.ppermute(rim_odd, MESH_AXES, slab_odd)  3.33 us
    ppermute x1, starting transfers between devices, per_device(): row_odd = lax.ppermute(row_odd, MESH_AXES, tile_odd)  2.9 us
    ppermute x1, starting transfers between devices, per_device(): odd = lax.ppermute(odd, MESH_AXES, slab_odd)  1.24 us
    pallas_call x1, Pallas kernels, per_device(): pl.pallas_call(weight_kernel, out_shape=(lines, rim, rim, layers, layers)...  1.18 us
    ppermute x1, starting transfers between devices, per_device(): row_even = lax.ppermute(row_even, MESH_AXES, tile_even)  1.07 us
    pallas_call x1, Pallas kernels, per_device(): pl.pallas_call(combine_kernel, out_shape=like(shape, F32), in_specs=[VMEM...  0.95 us
    ppermute x1, starting transfers between devices, per_device(): even = lax.ppermute(even, MESH_AXES, slab_even)  0.89 us
  transfers between devices with their start and end apart: 6, of which 1 were waited for; matrix products, arithmetic and copies ran while one was open for 0% of the time, Pallas kernels for 3%

profile of v12, /device:TPU:1, one launch (start us, length us, event | category | flops | bytes accessed | tf_op | source)
XLA Modules:
  0.0 42.2 jit_solution(3769354989084719909)
XLA Ops:
  0.0 1.2 %weights.1 = (f32[512,128]{1,0:T(8,128)S(1)}, f32[48,128]{1,0:T(8,128)S(1)}, f32[48,128]{1,0:T(8,128)S(1)}, f32[384,128]{1,0:T(8,128)S(1)}, f32[384,128]{1,0:T(8,128)S(1)}) custom-call(f32[4,16,1024]{2,1,0:T(8,128)} %sens_hbm.1, f32[4,16,1024]{2,1,0:T(8,128)} %dens_hbm.1), custom_call_target="tpu_custom_call" | custom-call | tf_op jit(solution)/shard_map/weights/pallas_call | solution.py:411
  1.2 3.3 %collective-permute-start = (f32[6,8,128]{2,1,0:T(8,128)S(1)}, f32[6,8,128]{2,1,0:T(8,128)S(1)}, u32[]{:S(2)}, u32[]{:S(2)}) collective-permute-start(f32[6,8,128]{2,1,0:T(8,128)S(1)} %bitcast.16), channel_id=1, source_target_pairs={{0,1},{1,0},{2,3},{3,2},{4,5},{5,4},{6,7},{7,6},{8,9},{9,8},{10,11... | collective-permute-start | bytes 73736 | tf_op jit(solution)/shard_map/ppermute | solution.py:430
  4.5 0.0 collective-permute-start.1
  4.5 1.2 %collective-permute-start.4 = (f32[3,16,8,128]{3,2,1,0:T(8,128)S(1)}, f32[3,16,8,128]{3,2,1,0:T(8,128)S(1)}, u32[]{:S(2)}, u32[]{:S(2)}) collective-permute-start(f32[3,16,8,128]{3,2,1,0:T(8,128)S(1)} %bitcast.14), channel_id=1, source_target_pairs={{0,1},{1,0},{2,3},{3,2},{4,5},{5,4},{6,7},{7,6},{8,9},{9,8},{10,11... | collective-permute-start | bytes 589832 | tf_op jit(solution)/shard_map/ppermute | solution.py:432
  5.8 0.9 %collective-permute-start.5 = (f32[3,16,8,128]{3,2,1,0:T(8,128)S(1)}, f32[3,16,8,128]{3,2,1,0:T(8,128)S(1)}, u32[]{:S(2)}, u32[]{:S(2)}) collective-permute-start(f32[3,16,8,128]{3,2,1,0:T(8,128)S(1)} %bitcast.13), channel_id=1, source_target_pairs={{0,16},{1,17},{2,18},{3,19},{4,20},{5,21},{6,22},{7,23},{8,24},{9,... | collective-permute-start | bytes 589832 | tf_op jit(solution)/shard_map/ppermute | solution.py:433
  6.7 0.0 collective-permute-done.odd_ref
  6.7 0.6 %collective-permute-done.1.even_ref = f32[6,8,128]{2,1,0:T(8,128)S(1)} collective-permute-done((f32[6,8,128]{2,1,0:T(8,128)S(1)}, f32[6,8,128]{2,1,0:T(8,128)S(1)}, u32[]{:S(2)}, u32[]{:S(2)}) %collective-permute-start.1) | collective-permute-done | bytes 24608 | tf_op jit(solution)/shard_map/ppermute | solution.py:431
  7.2 0.0 copy-start
  7.2 0.0 copy-start.1
  7.2 0.0 copy-start.2
  7.2 2.9 %collective-permute-start.2 = (f32[18,8,128]{2,1,0:T(8,128)S(1)}, f32[18,8,128]{2,1,0:T(8,128)S(1)}, u32[]{:S(2)}, u32[]{:S(2)}) collective-permute-start(f32[18,8,128]{2,1,0:T(8,128)S(1)} %get-tuple-element.23), channel_id=1, source_target_pairs={{0,64},{1,2},{2,1},{3,4},{4,3},{5,6},{6,5},{7,8},{8,7},{9,10},{10,... | collective-permute-start | bytes 221192 | tf_op jit(solution)/shard_map/ppermute | solution.py:446
  10.1 1.1 %collective-permute-start.3 = (f32[18,8,128]{2,1,0:T(8,128)S(1)}, f32[18,8,128]{2,1,0:T(8,128)S(1)}, u32[]{:S(2)}, u32[]{:S(2)}) collective-permute-start(f32[18,8,128]{2,1,0:T(8,128)S(1)} %get-tuple-element.24), channel_id=1, source_target_pairs={{0,1},{1,0},{2,3},{3,2},{4,5},{5,4},{6,7},{7,6},{8,9},{9,8},{10,11... | collective-permute-start | bytes 221192 | tf_op jit(solution)/shard_map/ppermute | solution.py:447
  11.2 0.0 copy-done
  11.2 0.0 copy-done.1
  11.2 0.0 copy-done.2
  11.2 0.8 %gram.1 = (f32[32,128]{1,0:T(8,128)S(1)}, f32[2,16,1024]{2,1,0:T(8,128)S(1)}) custom-call(f32[4,4,16,1024]{3,2,1,0:T(8,128)S(1)} %copy-done, f32[4,4,16,1024]{3,2,1,0:T(8,128)S(1)} %copy-done.1, s32[2,8,512]{2,1,0:T(8,128)S(1)} %copy-done.2), custom_call_target="tpu_custom_call" | custom-call | flops 8000000000 | bytes 43000000 | tf_op jit(solution)/shard_map/gram/pallas_call | solution.py:449
  12.0 0.0 collective-permute-done.4.odd_ref
  12.0 0.0 collective-permute-done.5.even_ref
  12.1 0.6 %inner.1 = (f32[10,16,8,128]{3,2,1,0:T(8,128)S(1)}, f32[10,16,8,128]{3,2,1,0:T(8,128)S(1)}, f32[10,16,8,128]{3,2,1,0:T(8,128)S(1)}, f32[512,128]{1,0:T(8,128)S(1)}) custom-call(f32[4,16,8,128]{3,2,1,0:T(8,128)S(1)} %bitcast.11, f32[3,16,8,128]{3,2,1,0:T(8,128)S(1)} %collective-permute-done.4.odd_ref, f32[3,16,8,128]{3,2,1,0:T(8,128)S(1)} %collective-permute-done.5.even_ref), custom_call_target="tpu_custom_call" | custom-call | tf_op jit(solution)/shard_map/inner/pallas_call | solution.py:462
  12.7 0.0 collective-permute-done.2.row_odd_ref
  12.7 0.0 collective-permute-done.3.row_even_ref
  12.7 0.6 %outer.1 = (f32[4,16,1024]{2,1,0:T(8,128)S(1)}, f32[256,128]{1,0:T(8,128)S(1)}) custom-call(f32[18,8,128]{2,1,0:T(8,128)S(1)} %collective-permute-done.2.row_odd_ref, f32[18,8,128]{2,1,0:T(8,128)S(1)} %collective-permute-done.3.row_even_ref, f32[10,16,8,128]{3,2,1,0:T(8,128)S(1)} %get-tuple-element.27.inner_start_ref, ...), custom_call_target="tpu_custom_call" | custom-call | tf_op jit(solution)/shard_map/outer/pallas_call | solution.py:472
  13.3 28.0 %all_to_all.11 = f32[256,1,128]{2,1,0:T(1,128)S(1)} all-to-all(f32[256,1,128]{2,1,0:T(1,128)S(1)} %bitcast.12), channel_id=1, replica_groups=mesh['slab'=16,'tile'=16] {'slab','tile'}, dimensions={0} | all-to-all | bytes 262144 | tf_op jit(solution)/shard_map/all_to_all | solution.py:488
  41.3 0.9 %combine.1 = f32[4,16,1024]{2,1,0:T(8,128)} custom-call(f32[256,128]{1,0:T(8,128)S(1)} %bitcast.9, f32[4,16,1024]{2,1,0:T(8,128)S(1)} %get-tuple-element.34.grad_ref, f32[4,4,16,1024]{3,2,1,0:T(8,128)S(1)} %copy-done, f32[4,4,16,1024]{3,2,1,0:T(8,128)S(1)} %copy-done.1), custom_call_target="tpu_custom_call" | custom-call | tf_op jit(solution)/shard_map/combine/pallas_call | solution.py:490
  (1 shorter events, 0.0 us)
Async XLA Ops:
  1.2 5.5 %collective-permute-start = (f32[6,8,128]{2,1,0:T(8,128)S(1)}, f32[6,8,128]{2,1,0:T(8,128)S(1)}, u32[]{:S(2)}, u32[]{:S(2)}) collective-permute-start(f32[6,8,128]{2,1,0:T(8,128)S(1)} %bitcast.16), channel_id=1, source_target_pairs={{0,1},{1,0},{2,3},{3,2},{4,5},{5,4},{6,7},{7,6},{8,9},{9,8},{10,11... | collective-permute-start | bytes 73736 | tf_op jit(solution)/shard_map/ppermute | solution.py:430
  4.5 2.7 %collective-permute-start.1 = (f32[6,8,128]{2,1,0:T(8,128)S(1)}, f32[6,8,128]{2,1,0:T(8,128)S(1)}, u32[]{:S(2)}, u32[]{:S(2)}) collective-permute-start(f32[6,8,128]{2,1,0:T(8,128)S(1)} %bitcast.15), channel_id=1, source_target_pairs={{0,16},{1,17},{2,18},{3,19},{4,20},{5,21},{6,22},{7,23},{8,24},{9,... | collective-permute-start | bytes 73736 | tf_op jit(solution)/shard_map/ppermute | solution.py:431
  4.5 7.5 %collective-permute-start.4 = (f32[3,16,8,128]{3,2,1,0:T(8,128)S(1)}, f32[3,16,8,128]{3,2,1,0:T(8,128)S(1)}, u32[]{:S(2)}, u32[]{:S(2)}) collective-permute-start(f32[3,16,8,128]{3,2,1,0:T(8,128)S(1)} %bitcast.14), channel_id=1, source_target_pairs={{0,1},{1,0},{2,3},{3,2},{4,5},{5,4},{6,7},{7,6},{8,9},{9,8},{10,11... | collective-permute-start | bytes 589832 | tf_op jit(solution)/shard_map/ppermute | solution.py:432
  5.8 6.3 %collective-permute-start.5 = (f32[3,16,8,128]{3,2,1,0:T(8,128)S(1)}, f32[3,16,8,128]{3,2,1,0:T(8,128)S(1)}, u32[]{:S(2)}, u32[]{:S(2)}) collective-permute-start(f32[3,16,8,128]{3,2,1,0:T(8,128)S(1)} %bitcast.13), channel_id=1, source_target_pairs={{0,16},{1,17},{2,18},{3,19},{4,20},{5,21},{6,22},{7,23},{8,24},{9,... | collective-permute-start | bytes 589832 | tf_op jit(solution)/shard_map/ppermute | solution.py:433
  7.2 4.0 %copy-start = (f32[4,4,16,1024]{3,2,1,0:T(8,128)S(1)}, f32[4,4,16,1024]{3,2,1,0:T(8,128)}, u32[]{:S(2)}) copy-start(f32[4,4,16,1024]{3,2,1,0:T(8,128)} %steps_ref.5) | copy-start | bytes 3145732
  7.2 4.0 %copy-start.1 = (f32[4,4,16,1024]{3,2,1,0:T(8,128)S(1)}, f32[4,4,16,1024]{3,2,1,0:T(8,128)}, u32[]{:S(2)}) copy-start(f32[4,4,16,1024]{3,2,1,0:T(8,128)} %changes_ref.5) | copy-start | bytes 3145732
  7.2 4.0 %copy-start.2 = (s32[2,8,512]{2,1,0:T(8,128)S(1)}, s32[2,8,512]{2,1,0:T(8,128)}, u32[]{:S(2)}) copy-start(s32[2,8,512]{2,1,0:T(8,128)} %passive_ref.1) | copy-start | bytes 98308
  7.2 5.4 %collective-permute-start.2 = (f32[18,8,128]{2,1,0:T(8,128)S(1)}, f32[18,8,128]{2,1,0:T(8,128)S(1)}, u32[]{:S(2)}, u32[]{:S(2)}) collective-permute-start(f32[18,8,128]{2,1,0:T(8,128)S(1)} %get-tuple-element.23), channel_id=1, source_target_pairs={{0,64},{1,2},{2,1},{3,4},{4,3},{5,6},{6,5},{7,8},{8,7},{9,10},{10,... | collective-permute-start | bytes 221192 | tf_op jit(solution)/shard_map/ppermute | solution.py:446
  10.1 2.5 %collective-permute-start.3 = (f32[18,8,128]{2,1,0:T(8,128)S(1)}, f32[18,8,128]{2,1,0:T(8,128)S(1)}, u32[]{:S(2)}, u32[]{:S(2)}) collective-permute-start(f32[18,8,128]{2,1,0:T(8,128)S(1)} %get-tuple-element.24), channel_id=1, source_target_pairs={{0,1},{1,0},{2,3},{3,2},{4,5},{5,4},{6,7},{7,6},{8,9},{9,8},{10,11... | collective-permute-start | bytes 221192 | tf_op jit(solution)/shard_map/ppermute | solution.py:447

commit v13 on v12

--- a/solution.py
+++ b/solution.py
@@ -38,8 +38,7 @@
     u_ref,
     rim_odd_ref,
     rim_even_ref,
-    odd_ref,
-    even_ref,
+    far_ref,
     sens_ref,
     dens_ref,
     arrived,
@@ -72,21 +71,17 @@
                 place = pl.ds(z * layer + row * width + part, 8, width)
                 u_ref[place, :] = value[row : row + 8, part * LANES : (part + 1) * LANES]
 
-    for rim_ref, layers_ref, top in (
-        (rim_odd_ref, odd_ref, slab_odd),
-        (rim_even_ref, even_ref, 1 - slab_odd),
-    ):
+    for rim_ref, top in ((rim_odd_ref, slab_odd), (rim_even_ref, 1 - slab_odd)):
 
         def put(first, count, z, row):
             place = pl.ds(pl.multiple_of(z * layer + row * width, 8), count * width)
             rim_ref[first * width : (first + count) * width, :] = u_ref[place, :]
 
         near, second = (depth - 1) * top, 1 + (depth - 3) * top
-        put(0, 2, near, 0)
-        put(2, 2, near, rows - 2)
-        put(4, 1, second, 0)
-        put(5, 1, second, rows - 1)
-        layers_ref[...] = u_ref[pl.ds(pl.multiple_of(top * layer, 8), SWEEPS * layer), :]
+        put(0, rows, near, 0)
+        put(rows, 1, second, 0)
+        put(rows + 1, 1, second, rows - 1)
+    far_ref[...] = u_ref[layer : (depth - 1) * layer, :]
 
 
 def gram_kernel(steps_ref, changes_ref, passive_ref, sums_ref, keep_ref):
@@ -138,7 +133,7 @@
         start = rows - 3 if top else 0
         for z in range(depth):
             out_ref[3 * z : 3 * z + 3] = u_ref[z, start : start + 3]
-        near, second = (2, 5) if top else (0, 4)
+        near, second = (rows - 2, rows + 1) if top else (0, rows)
         out_ref[12:14] = low_ref[near : near + 2]
         out_ref[14:16] = high_ref[near : near + 2]
         out_ref[16] = low_ref[second]
@@ -192,7 +187,9 @@
     return relax
 
 
-def inner_kernel(u_ref, odd_ref, even_ref, start_ref, one_ref, two_ref, last_ref):
+def inner_kernel(
+    u_ref, rim_odd_ref, rim_even_ref, odd_ref, even_ref, start_ref, one_ref, two_ref, last_ref
+):
     depth, rows, width = u_ref.shape[:3]
     slab_odd = lax.rem(lax.axis_index("slab"), 2)
     inside = grid_ends()
@@ -201,9 +198,12 @@
 
         @pl.when(slab_odd == parity)
         def _():
-            low_ref, high_ref = (even_ref, odd_ref) if parity else (odd_ref, even_ref)
-            start_ref[0:3] = low_ref[...] * inside["low_z"]
-            start_ref[3 + depth :] = high_ref[...] * inside["high_z"]
+            pairs = (rim_odd_ref, odd_ref), (rim_even_ref, even_ref)
+            (low_rim, low_far), (high_rim, high_far) = pairs[::-1] if parity else pairs
+            start_ref[0:2] = low_far[...] * inside["low_z"]
+            start_ref[2] = low_rim[0:rows] * inside["low_z"]
+            start_ref[3 + depth] = high_rim[0:rows] * inside["high_z"]
+            start_ref[4 + depth :] = high_far[...] * inside["high_z"]
 
     relax = line_sweep(width, depth, rows, inside)
 
@@ -402,17 +402,17 @@
     depth, rows, cols = shape
     like = jax.ShapeDtypeStruct
     width = cols // LANES
-    lines, layers, rim = (
-        like((count * width, LANES), F32) for count in (depth * rows, SWEEPS * rows, 6)
+    lines, far, rim = (
+        like((count * width, LANES), F32) for count in (depth * rows, 2 * rows, rows + 2)
     )
     edges = like((3 * depth + 6, width, LANES), F32)
     devices = lax.axis_size("slab") * lax.axis_size("tile")
 
-    u, rim_odd, rim_even, odd, even = pl.pallas_call(
+    u, rim_odd, rim_even, far = pl.pallas_call(
         weight_kernel,
-        out_shape=(lines, rim, rim, layers, layers),
+        out_shape=(lines, rim, rim, far),
         in_specs=[HBM] * 2,
-        out_specs=[VMEM] * 5,
+        out_specs=[VMEM] * 4,
         scratch_shapes=[
             pltpu.VMEM(shape, F32),
             pltpu.VMEM(shape, F32),
@@ -423,14 +423,16 @@
     )(in_hbm(sensitivity), in_hbm(filtered_density))
 
     u = u.reshape(depth, rows, width, LANES)
-    rim_odd, rim_even = (array.reshape(6, width, LANES) for array in (rim_odd, rim_even))
-    odd, even = (array.reshape(SWEEPS, rows, width, LANES) for array in (odd, even))
+    rim_odd, rim_even = (
+        array.reshape(rows + 2, width, LANES) for array in (rim_odd, rim_even)
+    )
+    far = far.reshape(2, rows, width, LANES)
 
     slab_odd, slab_even, tile_odd, tile_even = swaps()
     rim_odd = lax.ppermute(rim_odd, MESH_AXES, slab_odd)
     rim_even = lax.ppermute(rim_even, MESH_AXES, slab_even)
-    odd = lax.ppermute(odd, MESH_AXES, slab_odd)
-    even = lax.ppermute(even, MESH_AXES, slab_even)
+    odd = lax.ppermute(far, MESH_AXES, slab_odd)
+    even = lax.ppermute(far, MESH_AXES, slab_even)
 
     row_odd, row_even = pl.pallas_call(
         pack_kernel,
@@ -462,11 +464,11 @@
     inner = pl.pallas_call(
         inner_kernel,
         out_shape=(field, field, field, lines),
-        in_specs=[VMEM] * 3,
+        in_specs=[VMEM] * 5,
         out_specs=[VMEM] * 4,
         compiler_params=kernel_params(8),
         name="inner",
-    )(u, odd, even)
+    )(u, rim_odd, rim_even, odd, even)
 
     padded = pltpu.VMEM((depth + 6, rows + 6, width, LANES), F32)
     gradient, line = pl.pallas_call(

time: 42.4 us -> 43.4 us (1.024)
  waiting for transfers between devices: 0.57 us -> 1.7 us
    ppermute x1, starting transfers between devices: 2.9 us -> 1.77 us  [per_device(): row_odd = lax.ppermute(row_odd, MESH_AXES, tile_odd)]
    ppermute x1, waiting for transfers between devices: 0.55 us -> 1.69 us  [per_device(): rim_even = lax.ppermute(rim_even, MESH_AXES, slab_even)]
    ppermute x1, starting transfers between devices: 1.07 us -> 2.12 us  [per_device(): row_even = lax.ppermute(row_even, MESH_AXES, tile_even)]
where the time goes in v13:
time: 43.4 us; the launch traced here: 43.3 us
  blocking collectives  28 us (65%)
  starting transfers between devices  9.36 us (22%)
  Pallas kernels  4.12 us (9%)
  waiting for transfers between devices  1.7 us (4%)
    all_to_all x1, blocking collectives, per_device(): received = lax.all_to_all(line, MESH_AXES, 0, 0, tiled=True)  28 us
    ppermute x1, starting transfers between devices, per_device(): rim_odd = lax.ppermute(rim_odd, MESH_AXES, slab_odd)  3.33 us
    ppermute x1, starting transfers between devices, per_device(): row_even = lax.ppermute(row_even, MESH_AXES, tile_even)  2.12 us
    ppermute x1, starting transfers between devices, per_device(): row_odd = lax.ppermute(row_odd, MESH_AXES, tile_odd)  1.77 us
    ppermute x1, waiting for transfers between devices, per_device(): rim_even = lax.ppermute(rim_even, MESH_AXES, slab_even)  1.69 us
    ppermute x1, starting transfers between devices, per_device(): odd = lax.ppermute(far, MESH_AXES, slab_odd)  1.24 us
    pallas_call x1, Pallas kernels, per_device(): pl.pallas_call(weight_kernel, out_shape=(lines, rim, rim, far), in_specs=...  1.17 us
    pallas_call x1, Pallas kernels, per_device(): pl.pallas_call(combine_kernel, out_shape=like(shape, F32), in_specs=[VMEM...  0.95 us
  transfers between devices with their start and end apart: 6, of which 1 were waited for; matrix products, arithmetic and copies ran while one was open for 0% of the time, Pallas kernels for 3%

profile of v13, /device:TPU:1, one launch (start us, length us, event | category | flops | bytes accessed | tf_op | source)
XLA Modules:
  0.0 43.3 jit_solution(2098184066040857290)
XLA Ops:
  0.0 1.2 %weights.1 = (f32[512,128]{1,0:T(8,128)S(1)}, f32[144,128]{1,0:T(8,128)S(1)}, f32[144,128]{1,0:T(8,128)S(1)}, f32[256,128]{1,0:T(8,128)S(1)}) custom-call(f32[4,16,1024]{2,1,0:T(8,128)} %sens_hbm.1, f32[4,16,1024]{2,1,0:T(8,128)} %dens_hbm.1), custom_call_target="tpu_custom_call" | custom-call | tf_op jit(solution)/shard_map/weights/pallas_call | solution.py:411
  1.2 3.3 %collective-permute-start = (f32[18,8,128]{2,1,0:T(8,128)S(1)}, f32[18,8,128]{2,1,0:T(8,128)S(1)}, u32[]{:S(2)}, u32[]{:S(2)}) collective-permute-start(f32[18,8,128]{2,1,0:T(8,128)S(1)} %bitcast.15), channel_id=1, source_target_pairs={{0,1},{1,0},{2,3},{3,2},{4,5},{5,4},{6,7},{7,6},{8,9},{9,8},{10,11... | collective-permute-start | bytes 221192 | tf_op jit(solution)/shard_map/ppermute | solution.py:432
  4.5 0.0 collective-permute-start.1
  4.5 1.2 %collective-permute-start.4 = (f32[2,16,8,128]{3,2,1,0:T(8,128)S(1)}, f32[2,16,8,128]{3,2,1,0:T(8,128)S(1)}, u32[]{:S(2)}, u32[]{:S(2)}) collective-permute-start(f32[2,16,8,128]{3,2,1,0:T(8,128)S(1)} %bitcast.12), channel_id=1, source_target_pairs={{0,1},{1,0},{2,3},{3,2},{4,5},{5,4},{6,7},{7,6},{8,9},{9,8},{10,11... | collective-permute-start | bytes 393224 | tf_op jit(solution)/shard_map/ppermute | solution.py:434
  5.8 0.9 %collective-permute-start.5 = (f32[2,16,8,128]{3,2,1,0:T(8,128)S(1)}, f32[2,16,8,128]{3,2,1,0:T(8,128)S(1)}, u32[]{:S(2)}, u32[]{:S(2)}) collective-permute-start(f32[2,16,8,128]{3,2,1,0:T(8,128)S(1)} %bitcast.13), channel_id=1, source_target_pairs={{0,16},{1,17},{2,18},{3,19},{4,20},{5,21},{6,22},{7,23},{8,24},{9,... | collective-permute-start | bytes 393224 | tf_op jit(solution)/shard_map/ppermute | solution.py:435
  6.6 0.0 collective-permute-done.odd_ref.rim_odd_ref
  6.6 1.7 %collective-permute-done.1.even_ref.rim_even_ref = f32[18,8,128]{2,1,0:T(8,128)S(1)} collective-permute-done((f32[18,8,128]{2,1,0:T(8,128)S(1)}, f32[18,8,128]{2,1,0:T(8,128)S(1)}, u32[]{:S(2)}, u32[]{:S(2)}) %collective-permute-start.1) | collective-permute-done | bytes 73760 | tf_op jit(solution)/shard_map/ppermute | solution.py:433
  8.3 0.0 copy-start
  8.3 0.0 copy-start.1
  8.3 0.0 copy-start.2
  8.4 1.8 %collective-permute-start.2 = (f32[18,8,128]{2,1,0:T(8,128)S(1)}, f32[18,8,128]{2,1,0:T(8,128)S(1)}, u32[]{:S(2)}, u32[]{:S(2)}) collective-permute-start(f32[18,8,128]{2,1,0:T(8,128)S(1)} %get-tuple-element.22), channel_id=1, source_target_pairs={{0,64},{1,2},{2,1},{3,4},{4,3},{5,6},{6,5},{7,8},{8,7},{9,10},{10,... | collective-permute-start | bytes 221192 | tf_op jit(solution)/shard_map/ppermute | solution.py:448
  10.1 2.1 %collective-permute-start.3 = (f32[18,8,128]{2,1,0:T(8,128)S(1)}, f32[18,8,128]{2,1,0:T(8,128)S(1)}, u32[]{:S(2)}, u32[]{:S(2)}) collective-permute-start(f32[18,8,128]{2,1,0:T(8,128)S(1)} %get-tuple-element.23), channel_id=1, source_target_pairs={{0,1},{1,0},{2,3},{3,2},{4,5},{5,4},{6,7},{7,6},{8,9},{9,8},{10,11... | collective-permute-start | bytes 221192 | tf_op jit(solution)/shard_map/ppermute | solution.py:449
  12.3 0.0 copy-done
  12.3 0.0 copy-done.1
  12.3 0.0 copy-done.2
  12.3 0.8 %gram.1 = (f32[32,128]{1,0:T(8,128)S(1)}, f32[2,16,1024]{2,1,0:T(8,128)S(1)}) custom-call(f32[4,4,16,1024]{3,2,1,0:T(8,128)S(1)} %copy-done, f32[4,4,16,1024]{3,2,1,0:T(8,128)S(1)} %copy-done.1, s32[2,8,512]{2,1,0:T(8,128)S(1)} %copy-done.2), custom_call_target="tpu_custom_call" | custom-call | flops 8000000000 | bytes 43000000 | tf_op jit(solution)/shard_map/gram/pallas_call | solution.py:451
  13.1 0.0 collective-permute-done.4.odd_ref
  13.1 0.0 collective-permute-done.5.even_ref
  13.1 0.6 %inner.1 = (f32[10,16,8,128]{3,2,1,0:T(8,128)S(1)}, f32[10,16,8,128]{3,2,1,0:T(8,128)S(1)}, f32[10,16,8,128]{3,2,1,0:T(8,128)S(1)}, f32[512,128]{1,0:T(8,128)S(1)}) custom-call(f32[4,16,8,128]{3,2,1,0:T(8,128)S(1)} %bitcast.10, f32[18,8,128]{2,1,0:T(8,128)S(1)} %collective-permute-done.odd_ref.rim_odd_ref, ...), custom_call_target="tpu_custom_call" | custom-call | tf_op jit(solution)/shard_map/inner/pallas_call | solution.py:464
  13.7 0.0 collective-permute-done.2.row_odd_ref
  13.7 0.0 collective-permute-done.3.row_even_ref
  13.7 0.6 %outer.1 = (f32[4,16,1024]{2,1,0:T(8,128)S(1)}, f32[256,128]{1,0:T(8,128)S(1)}) custom-call(f32[18,8,128]{2,1,0:T(8,128)S(1)} %collective-permute-done.2.row_odd_ref, f32[18,8,128]{2,1,0:T(8,128)S(1)} %collective-permute-done.3.row_even_ref, f32[10,16,8,128]{3,2,1,0:T(8,128)S(1)} %get-tuple-element.25.inner_start_ref, ...), custom_call_target="tpu_custom_call" | custom-call | tf_op jit(solution)/shard_map/outer/pallas_call | solution.py:474
  14.3 28.0 %all_to_all.11 = f32[256,1,128]{2,1,0:T(1,128)S(1)} all-to-all(f32[256,1,128]{2,1,0:T(1,128)S(1)} %bitcast.11), channel_id=1, replica_groups=mesh['slab'=16,'tile'=16] {'slab','tile'}, dimensions={0} | all-to-all | bytes 262144 | tf_op jit(solution)/shard_map/all_to_all | solution.py:490
  42.3 0.9 %combine.1 = f32[4,16,1024]{2,1,0:T(8,128)} custom-call(f32[256,128]{1,0:T(8,128)S(1)} %bitcast.8, f32[4,16,1024]{2,1,0:T(8,128)S(1)} %get-tuple-element.32.grad_ref, f32[4,4,16,1024]{3,2,1,0:T(8,128)S(1)} %copy-done, f32[4,4,16,1024]{3,2,1,0:T(8,128)S(1)} %copy-done.1), custom_call_target="tpu_custom_call" | custom-call | tf_op jit(solution)/shard_map/combine/pallas_call | solution.py:492
  (1 shorter events, 0.0 us)
Async XLA Ops:
  1.2 5.5 %collective-permute-start = (f32[18,8,128]{2,1,0:T(8,128)S(1)}, f32[18,8,128]{2,1,0:T(8,128)S(1)}, u32[]{:S(2)}, u32[]{:S(2)}) collective-permute-start(f32[18,8,128]{2,1,0:T(8,128)S(1)} %bitcast.15), channel_id=1, source_target_pairs={{0,1},{1,0},{2,3},{3,2},{4,5},{5,4},{6,7},{7,6},{8,9},{9,8},{10,11... | collective-permute-start | bytes 221192 | tf_op jit(solution)/shard_map/ppermute | solution.py:432
  4.5 3.8 %collective-permute-start.1 = (f32[18,8,128]{2,1,0:T(8,128)S(1)}, f32[18,8,128]{2,1,0:T(8,128)S(1)}, u32[]{:S(2)}, u32[]{:S(2)}) collective-permute-start(f32[18,8,128]{2,1,0:T(8,128)S(1)} %bitcast.14), channel_id=1, source_target_pairs={{0,16},{1,17},{2,18},{3,19},{4,20},{5,21},{6,22},{7,23},{8,24},{9,... | collective-permute-start | bytes 221192 | tf_op jit(solution)/shard_map/ppermute | solution.py:433
  4.5 8.6 %collective-permute-start.4 = (f32[2,16,8,128]{3,2,1,0:T(8,128)S(1)}, f32[2,16,8,128]{3,2,1,0:T(8,128)S(1)}, u32[]{:S(2)}, u32[]{:S(2)}) collective-permute-start(f32[2,16,8,128]{3,2,1,0:T(8,128)S(1)} %bitcast.12), channel_id=1, source_target_pairs={{0,1},{1,0},{2,3},{3,2},{4,5},{5,4},{6,7},{7,6},{8,9},{9,8},{10,11... | collective-permute-start | bytes 393224 | tf_op jit(solution)/shard_map/ppermute | solution.py:434
  5.8 7.3 %collective-permute-start.5 = (f32[2,16,8,128]{3,2,1,0:T(8,128)S(1)}, f32[2,16,8,128]{3,2,1,0:T(8,128)S(1)}, u32[]{:S(2)}, u32[]{:S(2)}) collective-permute-start(f32[2,16,8,128]{3,2,1,0:T(8,128)S(1)} %bitcast.13), channel_id=1, source_target_pairs={{0,16},{1,17},{2,18},{3,19},{4,20},{5,21},{6,22},{7,23},{8,24},{9,... | collective-permute-start | bytes 393224 | tf_op jit(solution)/shard_map/ppermute | solution.py:435
  8.3 3.9 %copy-start = (f32[4,4,16,1024]{3,2,1,0:T(8,128)S(1)}, f32[4,4,16,1024]{3,2,1,0:T(8,128)}, u32[]{:S(2)}) copy-start(f32[4,4,16,1024]{3,2,1,0:T(8,128)} %steps_ref.5) | copy-start | bytes 3145732
  8.3 3.9 %copy-start.1 = (f32[4,4,16,1024]{3,2,1,0:T(8,128)S(1)}, f32[4,4,16,1024]{3,2,1,0:T(8,128)}, u32[]{:S(2)}) copy-start(f32[4,4,16,1024]{3,2,1,0:T(8,128)} %changes_ref.5) | copy-start | bytes 3145732
  8.3 3.9 %copy-start.2 = (s32[2,8,512]{2,1,0:T(8,128)S(1)}, s32[2,8,512]{2,1,0:T(8,128)}, u32[]{:S(2)}) copy-start(s32[2,8,512]{2,1,0:T(8,128)} %passive_ref.1) | copy-start | bytes 98308
  8.4 5.3 %collective-permute-start.2 = (f32[18,8,128]{2,1,0:T(8,128)S(1)}, f32[18,8,128]{2,1,0:T(8,128)S(1)}, u32[]{:S(2)}, u32[]{:S(2)}) collective-permute-start(f32[18,8,128]{2,1,0:T(8,128)S(1)} %get-tuple-element.22), channel_id=1, source_target_pairs={{0,64},{1,2},{2,1},{3,4},{4,3},{5,6},{6,5},{7,8},{8,7},{9,10},{10,... | collective-permute-start | bytes 221192 | tf_op jit(solution)/shard_map/ppermute | solution.py:448
  10.1 3.6 %collective-permute-start.3 = (f32[18,8,128]{2,1,0:T(8,128)S(1)}, f32[18,8,128]{2,1,0:T(8,128)S(1)}, u32[]{:S(2)}, u32[]{:S(2)}) collective-permute-start(f32[18,8,128]{2,1,0:T(8,128)S(1)} %get-tuple-element.23), channel_id=1, source_target_pairs={{0,1},{1,0},{2,3},{3,2},{4,5},{5,4},{6,7},{7,6},{8,9},{9,8},{10,11... | collective-permute-start | bytes 221192 | tf_op jit(solution)/shard_map/ppermute | solution.py:449
